TPU v7x, 32 devices: a whole 2x2x4 slice. The times are simulated.
32 devices in a mesh: seq: 8 (over z, x), head: 4 (over y, core).
Axes of the slice: x: 2, y: 2, z: 4, core: 2. Of those that a mesh axis runs over, the one named last changes fastest.
Arguments:
- queries: bfloat16 [4096, 4096], P('seq', 'head'), may hold values from -0.3984375 to 0.3984375
- keys: bfloat16 [4096, 4096], P('seq', 'head'), may hold values from -0.3984375 to 0.3984375
- values: bfloat16 [4096, 1024], P('seq', 'head'), may hold values from -3 to 3
- out_grad: bfloat16 [4096, 1024], P('seq', 'head'), may hold values from -0.29882812 to 0.29882812
- transitions: bfloat16 [32, 256, 256], replicated, may hold values from -1 to 1, as said below
- gammas: float32 [16], P('head'), may hold values from 0.6 to 1
- regimes: int32 [16], replicated, may hold values from 0 to 31
- documents: int32 [16], replicated, may hold values from 0 to 2, never falling along the last dimension, each value on 1 to 8 neighbouring positions
Outputs:
- query_grad: bfloat16 [4096, 4096], P('seq', 'head')
- key_grad: bfloat16 [4096, 4096], P('seq', 'head')
- value_grad: bfloat16 [4096, 1024], P('seq', 'head')
- regime_grad: float32 [32, 256, 256], P('seq', 'head')
Inputs may be any that keep to these rules, and one draw needn't show every extreme that they name: `transitions`: diagonal entries lie in 0.9 to 1.0, the others are small. `documents`: document numbers never fall; each document spans at most 8 blocks and one spans exactly that many.
All inputs are finite; a program needn't handle non-finite values.
Results may differ from a plain program's by a relative error of at most 0.005.
Values sent between devices are 32-bit elements; how exact they have to be, the bound alone decides.
No kernel may reach another device: no remote copies, remote signals or barrier semaphores. Data moves between devices by JAX's collectives and lax.ppermute only.
A program may use at most 64 MiB of HBM per device.

v0:
```python
import jax
import jax.numpy as jnp
from jax import lax
from jax.sharding import PartitionSpec as P

STATE = 256
HEAD_DIM = 64
REGIMES = 32
BLOCK = 256


PRECISE = lax.Precision.HIGHEST


def from_behind(x, axis, by):
    count = lax.axis_size(axis)
    pairs = [(i, i + by) for i in range(count) if 0 <= i + by < count]
    return lax.ppermute(x, axis, pairs)


def rotate(matrix, state):
    return jnp.einsum("nm,hmp->hnp", matrix, state, precision=PRECISE)


def extend_forward(current, matrix, keep_one, update, decays):
    current_mat, current_scale, current_sum = current
    factor = keep_one * decays
    return (
        keep_one * jnp.dot(matrix, current_mat, precision=PRECISE),
        decays * current_scale,
        update + factor[:, None, None] * rotate(matrix, current_sum),
    )


def extend_backward(current, matrix, keep_one, source, decays):
    current_mat, current_scale, current_sum = current
    factor = keep_one * decays
    flipped = matrix.T
    return (
        keep_one * jnp.dot(flipped, current_mat, precision=PRECISE),
        decays * current_scale,
        factor[:, None, None] * rotate(flipped, source + current_sum),
    )


def apply_map(current, state):
    current_mat, current_scale, current_sum = current
    return current_scale[:, None, None] * rotate(current_mat, state) + current_sum


def relay_forward(current):
    devices_seq = lax.axis_size("seq")

    def relay_step(number, carried_pair):
        arriving = from_behind(carried_pair[1], "seq", 1)
        return (arriving, apply_map(current, arriving))

    initial = (jnp.zeros_like(current[2]), current[2])
    return lax.fori_loop(0, devices_seq - 1, relay_step, initial)[0]


def relay_backward(current):
    devices_seq = lax.axis_size("seq")

    def relay_step(number, carried_pair):
        arriving = from_behind(carried_pair[1], "seq", -1)
        return (arriving, apply_map(current, arriving))

    initial = (jnp.zeros_like(current[2]), current[2])
    return lax.fori_loop(0, devices_seq - 1, relay_step, initial)[0]


def local(queries, keys, values, out_grad, transitions, gammas, regimes, documents):
    tokens_dev = queries.shape[0]
    heads_dev = gammas.shape[0]
    blocks_dev = tokens_dev // BLOCK
    query_rows = queries.reshape(blocks_dev, BLOCK, heads_dev, STATE)
    key_rows = keys.reshape(blocks_dev, BLOCK, heads_dev, STATE)
    value_rows = values.reshape(blocks_dev, BLOCK, heads_dev, HEAD_DIM)
    grad_rows = out_grad.reshape(blocks_dev, BLOCK, heads_dev, HEAD_DIM)
    first_block = lax.axis_index("seq") * blocks_dev
    same_doc = (documents[1:] == documents[:-1]).astype(jnp.float32)
    kept_all = jnp.concatenate([jnp.zeros((1,), jnp.float32), same_doc])
    kept = lax.dynamic_slice_in_dim(kept_all, first_block, blocks_dev)
    picked = lax.dynamic_slice_in_dim(regimes, first_block, blocks_dev)
    matrices = jnp.take(transitions, picked, axis=0).astype(jnp.float32)
    updates = jnp.einsum(
        "clhn,clhp->chnp", key_rows, value_rows, preferred_element_type=jnp.float32
    )
    sources = jnp.einsum(
        "clhn,clhp->chnp", query_rows, grad_rows, preferred_element_type=jnp.float32
    )
    eye_mat = jnp.eye(STATE, dtype=jnp.float32)
    ones_scale = jnp.ones((heads_dev,), jnp.float32)
    zero_state = jnp.zeros((heads_dev, STATE, HEAD_DIM), jnp.float32)
    identity = (eye_mat, ones_scale, zero_state)
    forward_map = identity
    for number in range(blocks_dev):
        forward_map = extend_forward(
            forward_map, matrices[number], kept[number], updates[number], gammas
        )
    backward_map = identity
    for number in reversed(range(blocks_dev)):
        backward_map = extend_backward(
            backward_map, matrices[number], kept[number], sources[number], gammas
        )
    state_in = relay_forward(forward_map)
    grad_in = relay_backward(backward_map)
    previous = state_in
    entry_list = []
    before_list = []
    for number in range(blocks_dev):
        factor = kept[number] * gammas
        entry = factor[:, None, None] * rotate(matrices[number], previous)
        before_list.append(previous)
        entry_list.append(entry)
        previous = entry + updates[number]
    carried = grad_in
    leave_list = [None] * blocks_dev
    total_list = [None] * blocks_dev
    for number in reversed(range(blocks_dev)):
        leave_list[number] = carried
        total = sources[number] + carried
        total_list[number] = total
        factor = kept[number] * gammas
        carried = factor[:, None, None] * jnp.einsum(
            "nm,hnp->hmp", matrices[number], total, precision=PRECISE
        )
    terms = jnp.stack(
        [
            kept[number]
            * jnp.einsum(
                "h,hnp,hmp->nm", gammas, total_list[number], before_list[number], precision=PRECISE
            )
            for number in range(blocks_dev)
        ]
    )
    head_summed = lax.psum_scatter(terms, "head", scatter_dimension=1, tiled=True)
    owned = REGIMES // lax.axis_size("seq")
    regime_ids = lax.axis_index("seq") * owned + jnp.arange(owned, dtype=jnp.int32)
    onehot = (regimes[:, None] == regime_ids[None, :]).astype(jnp.float32)
    regime_grad = jnp.einsum(
        "cr,cij->rij",
        onehot,
        lax.all_gather(head_summed, "seq", axis=0, tiled=True),
        precision=PRECISE,
    )
    entries_b = jnp.stack(entry_list).astype(jnp.bfloat16)
    leaving_b = jnp.stack(leave_list).astype(jnp.bfloat16)
    causal = lax.broadcasted_iota(jnp.int32, (BLOCK, BLOCK), 0) >= lax.broadcasted_iota(
        jnp.int32, (BLOCK, BLOCK), 1
    )

    def within(inputs):
        query_block, key_block, value_block, grad_block, entry_block, leave_block = inputs
        scores = jnp.einsum(
            "lhn,shn->hls", query_block, key_block, preferred_element_type=jnp.float32
        )
        probs = jnp.where(causal[None], scores, 0.0).astype(jnp.bfloat16)
        dots = jnp.einsum(
            "lhp,shp->hls", grad_block, value_block, preferred_element_type=jnp.float32
        )
        dscore = jnp.where(causal[None], dots, 0.0).astype(jnp.bfloat16)
        query_grad = jnp.einsum(
            "lhp,hnp->lhn", grad_block, entry_block, preferred_element_type=jnp.float32
        ) + jnp.einsum("hls,shn->lhn", dscore, key_block, preferred_element_type=jnp.float32)
        key_grad = jnp.einsum(
            "shp,hnp->shn", value_block, leave_block, preferred_element_type=jnp.float32
        ) + jnp.einsum("hls,lhn->shn", dscore, query_block, preferred_element_type=jnp.float32)
        value_grad = jnp.einsum(
            "shn,hnp->shp", key_block, leave_block, preferred_element_type=jnp.float32
        ) + jnp.einsum("hls,lhp->shp", probs, grad_block, preferred_element_type=jnp.float32)
        return (
            query_grad.astype(jnp.bfloat16),
            key_grad.astype(jnp.bfloat16),
            value_grad.astype(jnp.bfloat16),
        )

    query_grad, key_grad, value_grad = lax.map(
        within, (query_rows, key_rows, value_rows, grad_rows, entries_b, leaving_b)
    )
    return (
        query_grad.reshape(tokens_dev, heads_dev * STATE),
        key_grad.reshape(tokens_dev, heads_dev * STATE),
        value_grad.reshape(tokens_dev, heads_dev * HEAD_DIM),
        regime_grad,
    )


def solution(mesh):
    in_specs = (
        P("seq", "head"),
        P("seq", "head"),
        P("seq", "head"),
        P("seq", "head"),
        P(),
        P("head"),
        P(),
        P(),
    )
    out_specs = (P("seq", "head"), P("seq", "head"), P("seq", "head"), P("seq", "head", None))
    return jax.shard_map(local, mesh=mesh, in_specs=in_specs, out_specs=out_specs, check_vma=False)
```

profile of v0, /device:TPU:0, one launch (start us, length us, event | category | flops | bytes accessed | tf_op | source)
XLA Modules:
  0.0 261.5 jit_solution(17035493498791510945)
XLA Ops:
  9.6 2.7 %gather_fusion = bf16[2,256,256]{2,1,0:T(8,128)(2,1)S(1)} fusion(bf16[32,256,256]{2,1,0:T(8,128)(2,1)} %param.18, s32[1024]{0:T(1024)S(1)} %pad_clamp_fusion), kind=kCustom, calls=%fused_computation | custom fusion | bytes 524296 | tf_op jit(solution)/shard_map/jit(_take)/gather | solution.py:86
  26.1 71.9 %while.41 = (s32[]{:T(128)}, f32[4,256,64]{1,2,0:T(8,128)}, f32[4,256,64]{1,2,0:T(8,128)S(1)}, f32[4]{0:T(128)S(1)}, f32[256,256]{1,0:T(8,128)S(1)}, /*index=5*/f32[4,256,64]{1,2,0:T(8,128)S(1)}, s32[]{:T(128)}) while((s32[]{:T(128)}, f32[4,256,64]{1,2,0:T(8,128)}, f32[4,256,64]{1,2,0:T(8,128)S(1)}, f32[4]{0:T(128)S(1)}, ...), condition=%wide.region_3.4_spmd, body=%wide.region_2.3_spmd.sunk | while | flops 201457664 | bytes 3145889 | solution.py:70
  27.4 9.8 %collective-permute-done.1 = f32[4,256,64]{1,2,0:T(8,128)S(1)} collective-permute-done((f32[4,256,64]{1,2,0:T(8,128)S(1)}, f32[4,256,64]{1,2,0:T(8,128)S(1)}, u32[]{:S(2)}, u32[]{:S(2)}) %collective-permute-start.1) | collective-permute-done | bytes 262176 | tf_op jit(solution)/shard_map/while/body/eval_jaxpr/ppermute | solution.py:18
  39.2 8.7 %collective-permute-done.1 = f32[4,256,64]{1,2,0:T(8,128)S(1)} collective-permute-done((f32[4,256,64]{1,2,0:T(8,128)S(1)}, f32[4,256,64]{1,2,0:T(8,128)S(1)}, u32[]{:S(2)}, u32[]{:S(2)}) %collective-permute-start.1) | collective-permute-done | bytes 262176 | tf_op jit(solution)/shard_map/while/body/eval_jaxpr/ppermute | solution.py:18
  49.8 7.7 %collective-permute-done.1 = f32[4,256,64]{1,2,0:T(8,128)S(1)} collective-permute-done((f32[4,256,64]{1,2,0:T(8,128)S(1)}, f32[4,256,64]{1,2,0:T(8,128)S(1)}, u32[]{:S(2)}, u32[]{:S(2)}) %collective-permute-start.1) | collective-permute-done | bytes 262176 | tf_op jit(solution)/shard_map/while/body/eval_jaxpr/ppermute | solution.py:18
  59.6 7.7 %collective-permute-done.1 = f32[4,256,64]{1,2,0:T(8,128)S(1)} collective-permute-done((f32[4,256,64]{1,2,0:T(8,128)S(1)}, f32[4,256,64]{1,2,0:T(8,128)S(1)}, u32[]{:S(2)}, u32[]{:S(2)}) %collective-permute-start.1) | collective-permute-done | bytes 262176 | tf_op jit(solution)/shard_map/while/body/eval_jaxpr/ppermute | solution.py:18
  69.3 7.9 %collective-permute-done.1 = f32[4,256,64]{1,2,0:T(8,128)S(1)} collective-permute-done((f32[4,256,64]{1,2,0:T(8,128)S(1)}, f32[4,256,64]{1,2,0:T(8,128)S(1)}, u32[]{:S(2)}, u32[]{:S(2)}) %collective-permute-start.1) | collective-permute-done | bytes 262176 | tf_op jit(solution)/shard_map/while/body/eval_jaxpr/ppermute | solution.py:18
  79.1 8.0 %collective-permute-done.1 = f32[4,256,64]{1,2,0:T(8,128)S(1)} collective-permute-done((f32[4,256,64]{1,2,0:T(8,128)S(1)}, f32[4,256,64]{1,2,0:T(8,128)S(1)}, u32[]{:S(2)}, u32[]{:S(2)}) %collective-permute-start.1) | collective-permute-done | bytes 262176 | tf_op jit(solution)/shard_map/while/body/eval_jaxpr/ppermute | solution.py:18
  89.1 8.1 %collective-permute-done.1 = f32[4,256,64]{1,2,0:T(8,128)S(1)} collective-permute-done((f32[4,256,64]{1,2,0:T(8,128)S(1)}, f32[4,256,64]{1,2,0:T(8,128)S(1)}, u32[]{:S(2)}, u32[]{:S(2)}) %collective-permute-start.1) | collective-permute-done | bytes 262176 | tf_op jit(solution)/shard_map/while/body/eval_jaxpr/ppermute | solution.py:18
  99.2 2.6 %reshape.44 = bf16[2,256,4,256]{3,2,1,0:T(4,128)(2,1)} reshape(bf16[512,1024]{1,0:T(8,128)(2,1)} %param.15) | data formatting | bytes 2097152 | tf_op jit(solution)/shard_map/reshape | solution.py:78
  105.4 71.1 %while.40 = (s32[]{:T(128)}, f32[4,256,64]{1,2,0:T(8,128)}, f32[4,256,64]{1,2,0:T(8,128)S(1)}, f32[4]{0:T(128)S(1)}, f32[256,256]{1,0:T(8,128)S(1)}, /*index=5*/f32[4,256,64]{1,2,0:T(8,128)S(1)}, s32[]{:T(128)}) while((s32[]{:T(128)}, f32[4,256,64]{1,2,0:T(8,128)}, f32[4,256,64]{1,2,0:T(8,128)S(1)}, f32[4]{0:T(128)S(1)}, ...), condition=%wide.region_1.2_spmd, body=%wide.region_0.1_spmd.sunk | while | flops 201457664 | bytes 3145889 | solution.py:59
  105.4 4.8 %collective-permute-start = (f32[4,256,64]{1,2,0:T(8,128)S(1)}, f32[4,256,64]{1,2,0:T(8,128)S(1)}, u32[]{:S(2)}, u32[]{:S(2)}) collective-permute-start(f32[4,256,64]{1,2,0:T(8,128)S(1)} %get-tuple-element.412), channel_id=1, source_target_pairs={{0,4},{4,8},{8,12},{12,16},{16,20},{20,24},{24,28},{1,5},{5,9},{9,... | collective-permute-start | bytes 786440 | tf_op jit(solution)/shard_map/while/body/eval_jaxpr/ppermute | solution.py:18
  110.2 5.9 %collective-permute-done = f32[4,256,64]{1,2,0:T(8,128)S(1)} collective-permute-done((f32[4,256,64]{1,2,0:T(8,128)S(1)}, f32[4,256,64]{1,2,0:T(8,128)S(1)}, u32[]{:S(2)}, u32[]{:S(2)}) %collective-permute-start) | collective-permute-done | bytes 262176 | tf_op jit(solution)/shard_map/while/body/eval_jaxpr/ppermute | solution.py:18
  116.8 4.4 %collective-permute-start = (f32[4,256,64]{1,2,0:T(8,128)S(1)}, f32[4,256,64]{1,2,0:T(8,128)S(1)}, u32[]{:S(2)}, u32[]{:S(2)}) collective-permute-start(f32[4,256,64]{1,2,0:T(8,128)S(1)} %get-tuple-element.412), channel_id=1, source_target_pairs={{0,4},{4,8},{8,12},{12,16},{16,20},{20,24},{24,28},{1,5},{5,9},{9,... | collective-permute-start | bytes 786440 | tf_op jit(solution)/shard_map/while/body/eval_jaxpr/ppermute | solution.py:18
  121.2 5.0 %collective-permute-done = f32[4,256,64]{1,2,0:T(8,128)S(1)} collective-permute-done((f32[4,256,64]{1,2,0:T(8,128)S(1)}, f32[4,256,64]{1,2,0:T(8,128)S(1)}, u32[]{:S(2)}, u32[]{:S(2)}) %collective-permute-start) | collective-permute-done | bytes 262176 | tf_op jit(solution)/shard_map/while/body/eval_jaxpr/ppermute | solution.py:18
  126.9 4.4 %collective-permute-start = (f32[4,256,64]{1,2,0:T(8,128)S(1)}, f32[4,256,64]{1,2,0:T(8,128)S(1)}, u32[]{:S(2)}, u32[]{:S(2)}) collective-permute-start(f32[4,256,64]{1,2,0:T(8,128)S(1)} %get-tuple-element.412), channel_id=1, source_target_pairs={{0,4},{4,8},{8,12},{12,16},{16,20},{20,24},{24,28},{1,5},{5,9},{9,... | collective-permute-start | bytes 786440 | tf_op jit(solution)/shard_map/while/body/eval_jaxpr/ppermute | solution.py:18
  131.3 4.9 %collective-permute-done = f32[4,256,64]{1,2,0:T(8,128)S(1)} collective-permute-done((f32[4,256,64]{1,2,0:T(8,128)S(1)}, f32[4,256,64]{1,2,0:T(8,128)S(1)}, u32[]{:S(2)}, u32[]{:S(2)}) %collective-permute-start) | collective-permute-done | bytes 262176 | tf_op jit(solution)/shard_map/while/body/eval_jaxpr/ppermute | solution.py:18
  136.9 5.3 %collective-permute-start = (f32[4,256,64]{1,2,0:T(8,128)S(1)}, f32[4,256,64]{1,2,0:T(8,128)S(1)}, u32[]{:S(2)}, u32[]{:S(2)}) collective-permute-start(f32[4,256,64]{1,2,0:T(8,128)S(1)} %get-tuple-element.412), channel_id=1, source_target_pairs={{0,4},{4,8},{8,12},{12,16},{16,20},{20,24},{24,28},{1,5},{5,9},{9,... | collective-permute-start | bytes 786440 | tf_op jit(solution)/shard_map/while/body/eval_jaxpr/ppermute | solution.py:18
  142.2 4.1 %collective-permute-done = f32[4,256,64]{1,2,0:T(8,128)S(1)} collective-permute-done((f32[4,256,64]{1,2,0:T(8,128)S(1)}, f32[4,256,64]{1,2,0:T(8,128)S(1)}, u32[]{:S(2)}, u32[]{:S(2)}) %collective-permute-start) | collective-permute-done | bytes 262176 | tf_op jit(solution)/shard_map/while/body/eval_jaxpr/ppermute | solution.py:18
  146.9 5.3 %collective-permute-start = (f32[4,256,64]{1,2,0:T(8,128)S(1)}, f32[4,256,64]{1,2,0:T(8,128)S(1)}, u32[]{:S(2)}, u32[]{:S(2)}) collective-permute-start(f32[4,256,64]{1,2,0:T(8,128)S(1)} %get-tuple-element.412), channel_id=1, source_target_pairs={{0,4},{4,8},{8,12},{12,16},{16,20},{20,24},{24,28},{1,5},{5,9},{9,... | collective-permute-start | bytes 786440 | tf_op jit(solution)/shard_map/while/body/eval_jaxpr/ppermute | solution.py:18
  152.2 3.9 %collective-permute-done = f32[4,256,64]{1,2,0:T(8,128)S(1)} collective-permute-done((f32[4,256,64]{1,2,0:T(8,128)S(1)}, f32[4,256,64]{1,2,0:T(8,128)S(1)}, u32[]{:S(2)}, u32[]{:S(2)}) %collective-permute-start) | collective-permute-done | bytes 262176 | tf_op jit(solution)/shard_map/while/body/eval_jaxpr/ppermute | solution.py:18
  156.8 5.3 %collective-permute-start = (f32[4,256,64]{1,2,0:T(8,128)S(1)}, f32[4,256,64]{1,2,0:T(8,128)S(1)}, u32[]{:S(2)}, u32[]{:S(2)}) collective-permute-start(f32[4,256,64]{1,2,0:T(8,128)S(1)} %get-tuple-element.412), channel_id=1, source_target_pairs={{0,4},{4,8},{8,12},{12,16},{16,20},{20,24},{24,28},{1,5},{5,9},{9,... | collective-permute-start | bytes 786440 | tf_op jit(solution)/shard_map/while/body/eval_jaxpr/ppermute | solution.py:18
  162.1 3.9 %collective-permute-done = f32[4,256,64]{1,2,0:T(8,128)S(1)} collective-permute-done((f32[4,256,64]{1,2,0:T(8,128)S(1)}, f32[4,256,64]{1,2,0:T(8,128)S(1)}, u32[]{:S(2)}, u32[]{:S(2)}) %collective-permute-start) | collective-permute-done | bytes 262176 | tf_op jit(solution)/shard_map/while/body/eval_jaxpr/ppermute | solution.py:18
  166.6 5.3 %collective-permute-start = (f32[4,256,64]{1,2,0:T(8,128)S(1)}, f32[4,256,64]{1,2,0:T(8,128)S(1)}, u32[]{:S(2)}, u32[]{:S(2)}) collective-permute-start(f32[4,256,64]{1,2,0:T(8,128)S(1)} %get-tuple-element.412), channel_id=1, source_target_pairs={{0,4},{4,8},{8,12},{12,16},{16,20},{20,24},{24,28},{1,5},{5,9},{9,... | collective-permute-start | bytes 786440 | tf_op jit(solution)/shard_map/while/body/eval_jaxpr/ppermute | solution.py:18
  171.9 3.9 %collective-permute-done = f32[4,256,64]{1,2,0:T(8,128)S(1)} collective-permute-done((f32[4,256,64]{1,2,0:T(8,128)S(1)}, f32[4,256,64]{1,2,0:T(8,128)S(1)}, u32[]{:S(2)}, u32[]{:S(2)}) %collective-permute-start) | collective-permute-done | bytes 262176 | tf_op jit(solution)/shard_map/while/body/eval_jaxpr/ppermute | solution.py:18
  177.9 2.3 fusion.56
  180.2 2.3 fusion.54
  184.8 24.3 %reduce-scatter.2.cloned.1.call-done = f32[2,64,256]{2,1,0:T(8,128)} async-done(((f32[2,256,256]{2,1,0:T(8,128)}), f32[2,64,256]{2,1,0:T(8,128)}) %reduce-scatter.2.cloned.1.call-update) | async-done | bytes 131088 | tf_op jit(solution)/shard_map/reduce_scatter | solution.py:138
  209.1 21.8 %while.42 = (s32[]{:T(128)}, bf16[2,256,4,256]{3,2,1,0:T(4,128)(2,1)}, bf16[2,256,4,256]{3,2,1,0:T(4,128)(2,1)}, bf16[2,256,4,64]{1,3,2,0:T(8,128)(2,1)}, bf16[2...) while((s32[]{:T(128)}, ...), condition=%wide.region_5.6_spmd.clone.clone, body=%wide.region_4.5_spmd.clone.clone.sunk | while | flops 572719104 | bytes 19730564 | solution.py:179
  230.9 2.5 copy.71
  236.9 14.8 %all-gather.2.cloned.1.call-done = f32[16,64,256]{2,1,0:T(8,128)} async-done(((f32[2,64,256]{2,1,0:T(8,128)}), f32[16,64,256]{2,1,0:T(8,128)}) %all-gather.2.cloned.1.call-update) | async-done | bytes 1048592 | tf_op jit(solution)/shard_map/all_gather | solution.py:145
  251.6 2.2 fusion.68
  (140 shorter events, 68.8 us)
Async XLA Ops:
  7.2 13.3 %copy-start.6 = (bf16[512,256]{1,0:T(8,128)(2,1)S(1)}, bf16[512,256]{1,0:T(8,128)(2,1)}, u32[]{:S(2)}) copy-start(bf16[512,256]{1,0:T(8,128)(2,1)} %param.17) | copy-start | bytes 786436
  7.2 201.9 %reduce-scatter.2.cloned.1.call-start = ((), (), s32[]{:S(2)}) async-start(), calls=%async_computation.1 | async-start | bytes 655360 | tf_op jit(solution)/shard_map/reduce_scatter | solution.py:138
  26.1 11.1 %collective-permute-start.1 = (f32[4,256,64]{1,2,0:T(8,128)S(1)}, f32[4,256,64]{1,2,0:T(8,128)S(1)}, u32[]{:S(2)}, u32[]{:S(2)}) collective-permute-start(f32[4,256,64]{1,2,0:T(8,128)S(1)} %get-tuple-element.433), channel_id=1, source_target_pairs={{4,0},{8,4},{12,8},{16,12},{20,16},{24,20},{28,24},{5,1},{9,5},{13... | collective-permute-start | bytes 786440 | tf_op jit(solution)/shard_map/while/body/eval_jaxpr/ppermute | solution.py:18
  37.2 0.7 copy-start
  37.9 9.9 %collective-permute-start.1 = (f32[4,256,64]{1,2,0:T(8,128)S(1)}, f32[4,256,64]{1,2,0:T(8,128)S(1)}, u32[]{:S(2)}, u32[]{:S(2)}) collective-permute-start(f32[4,256,64]{1,2,0:T(8,128)S(1)} %get-tuple-element.433), channel_id=1, source_target_pairs={{4,0},{8,4},{12,8},{16,12},{20,16},{24,20},{28,24},{5,1},{9,5},{13... | collective-permute-start | bytes 786440 | tf_op jit(solution)/shard_map/while/body/eval_jaxpr/ppermute | solution.py:18
  47.9 0.7 copy-start
  48.6 9.0 %collective-permute-start.1 = (f32[4,256,64]{1,2,0:T(8,128)S(1)}, f32[4,256,64]{1,2,0:T(8,128)S(1)}, u32[]{:S(2)}, u32[]{:S(2)}) collective-permute-start(f32[4,256,64]{1,2,0:T(8,128)S(1)} %get-tuple-element.433), channel_id=1, source_target_pairs={{4,0},{8,4},{12,8},{16,12},{20,16},{24,20},{28,24},{5,1},{9,5},{13... | collective-permute-start | bytes 786440 | tf_op jit(solution)/shard_map/while/body/eval_jaxpr/ppermute | solution.py:18
  57.6 0.7 copy-start
  58.3 9.0 %collective-permute-start.1 = (f32[4,256,64]{1,2,0:T(8,128)S(1)}, f32[4,256,64]{1,2,0:T(8,128)S(1)}, u32[]{:S(2)}, u32[]{:S(2)}) collective-permute-start(f32[4,256,64]{1,2,0:T(8,128)S(1)} %get-tuple-element.433), channel_id=1, source_target_pairs={{4,0},{8,4},{12,8},{16,12},{20,16},{24,20},{28,24},{5,1},{9,5},{13... | collective-permute-start | bytes 786440 | tf_op jit(solution)/shard_map/while/body/eval_jaxpr/ppermute | solution.py:18
  67.3 0.7 copy-start
  68.0 9.2 %collective-permute-start.1 = (f32[4,256,64]{1,2,0:T(8,128)S(1)}, f32[4,256,64]{1,2,0:T(8,128)S(1)}, u32[]{:S(2)}, u32[]{:S(2)}) collective-permute-start(f32[4,256,64]{1,2,0:T(8,128)S(1)} %get-tuple-element.433), channel_id=1, source_target_pairs={{4,0},{8,4},{12,8},{16,12},{20,16},{24,20},{28,24},{5,1},{9,5},{13... | collective-permute-start | bytes 786440 | tf_op jit(solution)/shard_map/while/body/eval_jaxpr/ppermute | solution.py:18
  77.1 0.7 copy-start
  77.8 9.3 %collective-permute-start.1 = (f32[4,256,64]{1,2,0:T(8,128)S(1)}, f32[4,256,64]{1,2,0:T(8,128)S(1)}, u32[]{:S(2)}, u32[]{:S(2)}) collective-permute-start(f32[4,256,64]{1,2,0:T(8,128)S(1)} %get-tuple-element.433), channel_id=1, source_target_pairs={{4,0},{8,4},{12,8},{16,12},{20,16},{24,20},{28,24},{5,1},{9,5},{13... | collective-permute-start | bytes 786440 | tf_op jit(solution)/shard_map/while/body/eval_jaxpr/ppermute | solution.py:18
  87.1 0.7 copy-start
  87.8 9.4 %collective-permute-start.1 = (f32[4,256,64]{1,2,0:T(8,128)S(1)}, f32[4,256,64]{1,2,0:T(8,128)S(1)}, u32[]{:S(2)}, u32[]{:S(2)}) collective-permute-start(f32[4,256,64]{1,2,0:T(8,128)S(1)} %get-tuple-element.433), channel_id=1, source_target_pairs={{4,0},{8,4},{12,8},{16,12},{20,16},{24,20},{28,24},{5,1},{9,5},{13... | collective-permute-start | bytes 786440 | tf_op jit(solution)/shard_map/while/body/eval_jaxpr/ppermute | solution.py:18
  97.3 0.7 copy-start
  103.5 0.8 copy-start.3
  103.5 74.4 %copy-start.7 = (f32[4]{0:T(128)S(1)}, f32[4]{0:T(128)}, u32[]{:S(2)}) copy-start(f32[4]{0:T(128)} %param.19) | copy-start | bytes 52
  104.3 75.9 %copy-start.1 = (f32[4,256,64]{1,2,0:T(8,128)S(1)}, f32[4,256,64]{1,2,0:T(8,128)}, u32[]{:S(2)}) copy-start(f32[4,256,64]{1,2,0:T(8,128)} %get-tuple-element.129) | copy-start | bytes 786436
  105.4 10.7 %collective-permute-start = (f32[4,256,64]{1,2,0:T(8,128)S(1)}, f32[4,256,64]{1,2,0:T(8,128)S(1)}, u32[]{:S(2)}, u32[]{:S(2)}) collective-permute-start(f32[4,256,64]{1,2,0:T(8,128)S(1)} %get-tuple-element.412), channel_id=1, source_target_pairs={{0,4},{4,8},{8,12},{12,16},{16,20},{20,24},{24,28},{1,5},{5,9},{9,... | collective-permute-start | bytes 786440 | tf_op jit(solution)/shard_map/while/body/eval_jaxpr/ppermute | solution.py:18
  116.1 0.7 copy-start.2
  116.8 9.4 %collective-permute-start = (f32[4,256,64]{1,2,0:T(8,128)S(1)}, f32[4,256,64]{1,2,0:T(8,128)S(1)}, u32[]{:S(2)}, u32[]{:S(2)}) collective-permute-start(f32[4,256,64]{1,2,0:T(8,128)S(1)} %get-tuple-element.412), channel_id=1, source_target_pairs={{0,4},{4,8},{8,12},{12,16},{16,20},{20,24},{24,28},{1,5},{5,9},{9,... | collective-permute-start | bytes 786440 | tf_op jit(solution)/shard_map/while/body/eval_jaxpr/ppermute | solution.py:18
  126.2 0.7 copy-start.2
  126.9 9.3 %collective-permute-start = (f32[4,256,64]{1,2,0:T(8,128)S(1)}, f32[4,256,64]{1,2,0:T(8,128)S(1)}, u32[]{:S(2)}, u32[]{:S(2)}) collective-permute-start(f32[4,256,64]{1,2,0:T(8,128)S(1)} %get-tuple-element.412), channel_id=1, source_target_pairs={{0,4},{4,8},{8,12},{12,16},{16,20},{20,24},{24,28},{1,5},{5,9},{9,... | collective-permute-start | bytes 786440 | tf_op jit(solution)/shard_map/while/body/eval_jaxpr/ppermute | solution.py:18
  136.9 9.4 %collective-permute-start = (f32[4,256,64]{1,2,0:T(8,128)S(1)}, f32[4,256,64]{1,2,0:T(8,128)S(1)}, u32[]{:S(2)}, u32[]{:S(2)}) collective-permute-start(f32[4,256,64]{1,2,0:T(8,128)S(1)} %get-tuple-element.412), channel_id=1, source_target_pairs={{0,4},{4,8},{8,12},{12,16},{16,20},{20,24},{24,28},{1,5},{5,9},{9,... | collective-permute-start | bytes 786440 | tf_op jit(solution)/shard_map/while/body/eval_jaxpr/ppermute | solution.py:18
  146.9 9.2 %collective-permute-start = (f32[4,256,64]{1,2,0:T(8,128)S(1)}, f32[4,256,64]{1,2,0:T(8,128)S(1)}, u32[]{:S(2)}, u32[]{:S(2)}) collective-permute-start(f32[4,256,64]{1,2,0:T(8,128)S(1)} %get-tuple-element.412), channel_id=1, source_target_pairs={{0,4},{4,8},{8,12},{12,16},{16,20},{20,24},{24,28},{1,5},{5,9},{9,... | collective-permute-start | bytes 786440 | tf_op jit(solution)/shard_map/while/body/eval_jaxpr/ppermute | solution.py:18
  156.8 9.2 %collective-permute-start = (f32[4,256,64]{1,2,0:T(8,128)S(1)}, f32[4,256,64]{1,2,0:T(8,128)S(1)}, u32[]{:S(2)}, u32[]{:S(2)}) collective-permute-start(f32[4,256,64]{1,2,0:T(8,128)S(1)} %get-tuple-element.412), channel_id=1, source_target_pairs={{0,4},{4,8},{8,12},{12,16},{16,20},{20,24},{24,28},{1,5},{5,9},{9,... | collective-permute-start | bytes 786440 | tf_op jit(solution)/shard_map/while/body/eval_jaxpr/ppermute | solution.py:18
  166.6 9.2 %collective-permute-start = (f32[4,256,64]{1,2,0:T(8,128)S(1)}, f32[4,256,64]{1,2,0:T(8,128)S(1)}, u32[]{:S(2)}, u32[]{:S(2)}) collective-permute-start(f32[4,256,64]{1,2,0:T(8,128)S(1)} %get-tuple-element.412), channel_id=1, source_target_pairs={{0,4},{4,8},{8,12},{12,16},{16,20},{20,24},{24,28},{1,5},{5,9},{9,... | collective-permute-start | bytes 786440 | tf_op jit(solution)/shard_map/while/body/eval_jaxpr/ppermute | solution.py:18
  176.5 7.2 %copy-start.4 = (f32[2,4,256,64]{2,3,1,0:T(8,128)S(1)}, f32[2,4,256,64]{2,3,1,0:T(8,128)}, u32[]{:S(2)}) copy-start(f32[2,4,256,64]{2,3,1,0:T(8,128)} %copy-done.3) | copy-start | bytes 1572868
  183.3 68.3 %all-gather.2.cloned.1.call-start = ((), (), s32[]{:S(2)}) async-start(), calls=%async_computation.2 | async-start | bytes 1179648 | tf_op jit(solution)/shard_map/all_gather | solution.py:145
  230.9 4.8 %copy-start.5 = (bf16[2,256,4,256]{3,2,1,0:T(4,128)(2,1)S(1)}, bf16[2,256,4,256]{3,2,1,0:T(4,128)(2,1)}, u32[]{:S(2)}) copy-start(bf16[2,256,4,256]{3,2,1,0:T(4,128)(2,1)} %get-tuple-element.131) | copy-start | bytes 3145732
  230.9 20.8 %copy-start.8 = (s32[16]{0:T(128)S(1)}, s32[16]{0:T(128)}, u32[]{:S(2)}) copy-start(s32[16]{0:T(128)} %param.20) | copy-start | bytes 196
  (5 other events, 3.5 us)
Sparse Core Ops, SparseCore 0:
  183.5 25.5 reduce-scatter.1
  211.4 40.2 all-gather.1
where the time goes:
time: 263 us; the launch traced here: 261 us
  waiting for transfers between devices  128 us (49%)
  starting transfers between devices  44 us (17%)
  matrix products  36.9 us (14%)
  local copies, waits for them, and re-layouts  32 us (12%)
  between operations  14.3 us (5%)
  other arithmetic  5.43 us (2%)
    ppermute x14, waiting for transfers between devices, from_behind(): return lax.ppermute(x, axis, pairs)  89.4 us
    ppermute x14, starting transfers between devices, from_behind(): return lax.ppermute(x, axis, pairs)  43.7 us
    reduce_scatter x1, waiting for transfers between devices, local(): lax.psum_scatter(terms, 'head', scatter_dimension=1, tiled=True)  24.3 us
    all_gather x1, waiting for transfers between devices, local(): lax.all_gather(head_summed, 'seq', axis=0, tiled=True)  14.8 us
    dot_general x20, matrix products, rotate(): return jnp.einsum('nm,hmp->hnp', matrix, state, precision=PRECISE)  8.68 us
    unnamed x22, local copies, waits for them, and re-layouts  8.21 us
  transfers between devices with their start and end apart: 16, of which 16 were waited for; matrix products, arithmetic and copies ran while one was open for 11% of the time, Pallas kernels for 0%

commit v1 on v0

v1 whole, which is shorter than its diff:
```python
import functools

import jax
import jax.numpy as jnp
from jax import lax
from jax.experimental import pallas as pl
from jax.experimental.pallas import tpu as pltpu
from jax.sharding import PartitionSpec as P

STATE = 256
HEAD_DIM = 64
REGIMES = 32
BLOCK = 256

F32 = jnp.float32
BF16 = jnp.bfloat16
NN = (((1,), (0,)), ((), ()))
NT = (((1,), (1,)), ((), ()))
TN = (((0,), (0,)), ((), ()))
VMEM = pl.BlockSpec(memory_space=pltpu.VMEM)
SMEM = pl.BlockSpec(memory_space=pltpu.SMEM)
PARAMS = pltpu.CompilerParams(vmem_limit_bytes=48 << 20)


def dot(a, b, dims):
    return lax.dot_general(a, b, dims, preferred_element_type=F32)


def halves(x):
    high = x.astype(BF16)
    return high, (x - high.astype(F32)).astype(BF16)


def dot_exact(x, matrix, dims):
    high, low = halves(x)
    return dot(high, matrix, dims) + dot(low, matrix, dims)


def dot_pair(a, b, dims):
    return dot(a[0], b[0], dims) + (dot(a[0], b[1], dims) + dot(a[1], b[0], dims))


def kept_at(documents, block):
    before = documents[jnp.maximum(block - 1, 0)]
    same = jnp.where(documents[block] == before, 1.0, 0.0)
    return jnp.where(block > 0, same, 0.0).astype(F32)


def decay_column(gammas, first, count, power):
    parts = []
    for i in range(count):
        g = gammas[first + i]
        value = g
        for _ in range(power - 1):
            value = value * g
        parts.append(jnp.full((HEAD_DIM, 1), value, F32))
    return jnp.concatenate(parts, axis=0)


def local_kernel(blocks, heads, regimes, documents, pos, gammas, q, k, v, dy, *rest):
    mats, (update, source, sent, held) = rest[:blocks], rest[blocks:]
    seq = pos[0]
    rows = heads * HEAD_DIM
    half = rows // 2
    decay = decay_column(gammas, 0, heads, 1)
    for c in range(blocks):
        token = slice(c * BLOCK, (c + 1) * BLOCK)
        for h in range(heads):
            wide = slice(h * STATE, (h + 1) * STATE)
            narrow = slice(h * HEAD_DIM, (h + 1) * HEAD_DIM)
            update[c, narrow, :] = dot(v[token, narrow], k[token, wide], TN)
            source[c, narrow, :] = dot(dy[token, narrow], q[token, wide], TN)
    state = update[0]
    for c in range(1, blocks):
        factor = kept_at(documents, seq * blocks + c) * decay
        state = update[c] + factor * dot_exact(state, mats[c][0], NT)
    carried = None
    for c in reversed(range(blocks)):
        total = source[c] if carried is None else source[c] + carried
        factor = kept_at(documents, seq * blocks + c) * decay
        carried = factor * dot_exact(total, mats[c][0], NN)
    upper = lax.rem(seq, 2) == 1
    for i, value in enumerate((state, carried)):
        first, second = value[:half], value[half:]
        held[i] = jnp.where(upper, second, first)
        sent[i] = jnp.where(upper, first, second)


def maps_kernel(blocks, reach, last_block, regimes, documents, pos, transitions, device_maps, *far):
    seq = pos[0]
    level = lax.div(seq, 2)

    def device_map(device):
        result = None
        for c in range(blocks):
            block = jnp.clip(device * blocks + c, 0, last_block)
            mat = transitions[regimes[block]]
            kept = kept_at(documents, block)
            if result is None:
                result = mat.astype(F32)
            elif c == 1:
                result = dot(mat, result.astype(BF16), NN)
            else:
                high, low = halves(result)
                result = dot(mat, high, NN) + dot(mat, low, NN)
            result = result * kept
        return result

    def pair_map(at):
        low = halves(device_map(at * 2))
        high = halves(device_map(at * 2 + 1))
        return dot_pair(high, low, NN)

    for i in range(2):
        device_maps[i, 0], device_maps[i, 1] = halves(device_map(level * 2 + i))
    if reach > 1:
        far = far[0]
        forward = backward = None
        for distance in range(2, reach + 1):
            behind = pair_map(level - distance + 1)
            ahead = pair_map(level + distance - 1)
            if forward is None:
                forward, backward = behind, ahead
            else:
                forward = dot_pair(halves(forward), halves(behind), NN)
                backward = dot_pair(halves(ahead), halves(backward), NN)
            far[distance - 2, 0, 0], far[distance - 2, 0, 1] = halves(forward)
            far[distance - 2, 1, 0], far[distance - 2, 1, 1] = halves(backward)


def pair_kernel(blocks, heads, routes, pos, gammas, held, arrived, device_maps, *outs):
    seq = pos[0]
    level, upper = lax.div(seq, 2), lax.rem(seq, 2)
    is_upper = upper == 1
    decay = decay_column(gammas, upper * (heads // 2), heads // 2, blocks)
    ends = [jnp.where(is_upper, arrived[0], held[0]), jnp.where(is_upper, held[0], arrived[0])]
    starts = [jnp.where(is_upper, arrived[1], held[1]), jnp.where(is_upper, held[1], arrived[1])]
    low_map = (device_maps[0, 0], device_maps[0, 1])
    high_map = (device_maps[1, 0], device_maps[1, 1])
    forward = ends[1] + decay * dot_pair(halves(ends[0]), high_map, NT)
    backward = starts[0] + decay * dot_pair(halves(starts[1]), low_map, NN)
    for out, (distance, parity) in zip(outs, routes):
        ahead = lax.rem(lax.div(level, distance), 2) == parity
        out[...] = jnp.where(ahead, forward, backward)


def entry_kernel(blocks, heads, reach, routes, pos, gammas, held, arrived, device_maps, *rest):
    count = len(routes)
    received, (own, sent) = rest[:count], rest[-2:]
    far = rest[count] if reach > 1 else None
    seq = pos[0]
    level, upper = lax.div(seq, 2), lax.rem(seq, 2)
    is_upper = upper == 1
    decay = decay_column(gammas, upper * (heads // 2), heads // 2, blocks)
    found = dict(zip(routes, received))
    forward = backward = None
    for distance in range(1, reach + 1):
        even = found[distance, 0][...]
        odd = found[distance, 1][...] if (distance, 1) in found else jnp.zeros_like(even)
        flip = lax.rem(lax.div(level, distance), 2) == 1
        behind = jnp.where(flip, even, odd)
        ahead = jnp.where(flip, odd, even)
        if distance == 1:
            forward, backward = behind, ahead
        else:
            power = decay_column(
                gammas, upper * (heads // 2), heads // 2, 2 * blocks * (distance - 1)
            )
            i = distance - 2
            forward += power * dot_pair(halves(behind), (far[i, 0, 0], far[i, 0, 1]), NT)
            backward += power * dot_pair(halves(ahead), (far[i, 1, 0], far[i, 1, 1]), NN)
    low_map = (device_maps[0, 0], device_maps[0, 1])
    high_map = (device_maps[1, 0], device_maps[1, 1])
    low_end = jnp.where(is_upper, arrived[0], held[0])
    high_start = jnp.where(is_upper, held[1], arrived[1])
    inner_forward = low_end + decay * dot_pair(halves(forward), low_map, NT)
    inner_backward = high_start + decay * dot_pair(halves(backward), high_map, NN)
    own[0] = jnp.where(is_upper, inner_forward, forward)
    own[1] = jnp.where(is_upper, backward, inner_backward)
    sent[0] = jnp.where(is_upper, forward, inner_forward)
    sent[1] = jnp.where(is_upper, inner_backward, backward)


def terms_kernel(
    blocks, heads, ways, regimes, documents, pos, gammas, own, arrived, update, source, *rest
):
    mats, (entries, leaves, held, sent, term) = rest[:blocks], rest[blocks:]
    seq, head = pos[0], pos[1]
    upper = lax.rem(seq, 2) == 1
    decay = decay_column(gammas, 0, heads, 1)

    def whole(i):
        first = jnp.where(upper, arrived[i], own[i])
        second = jnp.where(upper, own[i], arrived[i])
        return jnp.concatenate([first, second], axis=0)

    before, carried = whole(0), whole(1)
    kept = [kept_at(documents, seq * blocks + c) for c in range(blocks)]
    befores, totals = [], []
    for c in range(blocks):
        befores.append(halves(before))
        high, low = befores[-1]
        entry = (kept[c] * decay) * (dot(high, mats[c][0], NT) + dot(low, mats[c][0], NT))
        entries[c] = entry.astype(BF16)
        before = entry + update[c]
    for c in reversed(range(blocks)):
        leaves[c] = carried.astype(BF16)
        total = source[c] + carried
        totals.insert(0, total)
        carried = (kept[c] * decay) * dot_exact(total, mats[c][0], NN)
    part = STATE // ways
    core = lax.rem(head, 2)
    for c in range(blocks):
        term[...] = dot_pair(halves((kept[c] * decay) * totals[c]), befores[c], TN)
        for i in range(ways // 2):
            held[c, i] = term[pl.ds(pl.multiple_of((2 * i + core) * part, part), part), :]
            sent[c, i] = term[pl.ds(pl.multiple_of((2 * i + 1 - core) * part, part), part), :]


def regime_kernel(blocks, owned, count, regimes, base, sources, *rest):
    pieces, out = rest[:count], rest[count]
    for r in range(owned):
        total = None
        for i in range(count):
            for c in range(blocks):
                block = jnp.maximum(sources[i], 0) * blocks + c
                match = (sources[i] >= 0) & (regimes[block] == base[0] + r)
                value = jnp.where(match, pieces[i][c], 0.0)
                total = value if total is None else total + value
        out[r] = total


def within_kernel(q, k, v, dy, entry, leave, dq, dk, dv):
    heads = v.shape[1] // HEAD_DIM
    causal = lax.broadcasted_iota(jnp.int32, (BLOCK, BLOCK), 0) >= lax.broadcasted_iota(
        jnp.int32, (BLOCK, BLOCK), 1
    )
    for h in range(heads):
        wide = slice(h * STATE, (h + 1) * STATE)
        narrow = slice(h * HEAD_DIM, (h + 1) * HEAD_DIM)
        qh, kh, vh, gh = q[:, wide], k[:, wide], v[:, narrow], dy[:, narrow]
        eh, lh = entry[0, narrow, :], leave[0, narrow, :]
        probs = jnp.where(causal, dot(qh, kh, NT), 0.0).astype(BF16)
        dscore = jnp.where(causal, dot(gh, vh, NT), 0.0).astype(BF16)
        dq[:, wide] = (dot(gh, eh, NN) + dot(dscore, kh, NN)).astype(BF16)
        dk[:, wide] = (dot(vh, lh, NN) + dot(dscore, qh, TN)).astype(BF16)
        dv[:, narrow] = (dot(kh, lh, NT) + dot(probs, gh, TN)).astype(BF16)


def swap(x, axis, by):
    count = lax.axis_size(axis)
    return lax.ppermute(x, axis, [(i, i ^ by) for i in range(count)])


def level_route(x, distance, parity):
    levels = lax.axis_size("seq") // 2
    pairs = []
    for low in range(levels - distance):
        if (low // distance) % 2 == parity:
            for side in range(2):
                a, b = 2 * low + side, 2 * (low + distance) + side
                pairs += [(a, b), (b, a)]
    return lax.ppermute(x, "seq", pairs)


def routes_up_to(reach, levels):
    return [
        (distance, parity)
        for distance in range(1, reach + 1)
        for parity in range(2)
        if any((low // distance) % 2 == parity for low in range(levels - distance))
    ]


def local(queries, keys, values, out_grad, transitions, gammas, regimes, documents):
    tokens_dev = queries.shape[0]
    heads = gammas.shape[0]
    blocks = tokens_dev // BLOCK
    all_blocks = documents.shape[0]
    devices, ways = lax.axis_size("seq"), lax.axis_size("head")
    levels = devices // 2
    rows = heads * HEAD_DIM
    half = rows // 2
    reach = min(levels - 1, -(-(all_blocks // 2 - 1) // (2 * blocks)))
    routes = routes_up_to(reach, levels)
    seq, head = lax.axis_index("seq"), lax.axis_index("head")
    pos = jnp.stack([seq, head]).astype(jnp.int32)

    def shape(*dims, dtype=F32):
        return jax.ShapeDtypeStruct(dims, dtype)

    def whole(x):
        return pl.BlockSpec(x.shape, lambda i, *_: (0,) * len(x.shape))

    def own_mats():
        return [
            pl.BlockSpec(
                (1, STATE, STATE),
                lambda i, regimes, documents, pos, c=c: (regimes[pos[0] * blocks + c], 0, 0),
            )
            for c in range(blocks)
        ]

    state_shape = shape(blocks, rows, STATE)
    half_shape = shape(2, half, STATE)
    outs = (state_shape, state_shape, half_shape, half_shape)
    update, source, sent, held = pl.pallas_call(
        functools.partial(local_kernel, blocks, heads),
        grid_spec=pltpu.PrefetchScalarGridSpec(
            num_scalar_prefetch=3,
            grid=(1,),
            in_specs=[SMEM] + [whole(x) for x in (queries, keys, values, out_grad)] + own_mats(),
            out_specs=[whole(x) for x in outs],
        ),
        out_shape=outs,
        compiler_params=PARAMS,
    )(regimes, documents, pos, gammas, queries, keys, values, out_grad, *[transitions] * blocks)

    arrived = swap(sent, "seq", 1)
    map_shapes = (shape(2, 2, STATE, STATE, dtype=BF16),)
    if reach > 1:
        map_shapes += (shape(reach - 1, 2, 2, STATE, STATE, dtype=BF16),)
    maps = pl.pallas_call(
        functools.partial(maps_kernel, blocks, reach, all_blocks - 1),
        in_specs=[SMEM, SMEM, SMEM, VMEM],
        out_specs=(VMEM,) * len(map_shapes),
        out_shape=map_shapes,
        compiler_params=PARAMS,
    )(regimes, documents, pos, transitions)

    trades = pl.pallas_call(
        functools.partial(pair_kernel, blocks, heads, routes),
        in_specs=[SMEM, SMEM, VMEM, VMEM, VMEM],
        out_specs=(VMEM,) * len(routes),
        out_shape=(shape(half, STATE),) * len(routes),
        compiler_params=PARAMS,
    )(pos, gammas, held, arrived, maps[0])
    received = [level_route(x, *route) for x, route in zip(trades, routes)]

    own, sent_entry = pl.pallas_call(
        functools.partial(entry_kernel, blocks, heads, reach, routes),
        in_specs=[SMEM, SMEM] + [VMEM] * (3 + len(received) + len(maps) - 1),
        out_specs=(VMEM, VMEM),
        out_shape=(half_shape, half_shape),
        compiler_params=PARAMS,
    )(pos, gammas, held, arrived, maps[0], *received, *maps[1:])
    arrived_entry = swap(sent_entry, "seq", 1)

    part = STATE // ways
    part_shape = shape(blocks, ways // 2, part, STATE)
    bf16_states = shape(blocks, rows, STATE, dtype=BF16)
    outs = (bf16_states, bf16_states, part_shape, part_shape)
    entries, leaves, held_term, sent_term = pl.pallas_call(
        functools.partial(terms_kernel, blocks, heads, ways),
        grid_spec=pltpu.PrefetchScalarGridSpec(
            num_scalar_prefetch=3,
            grid=(1,),
            in_specs=[SMEM]
            + [whole(x) for x in (own, arrived_entry, update, source)]
            + own_mats(),
            out_specs=[whole(x) for x in outs],
            scratch_shapes=[pltpu.VMEM((STATE, STATE), F32)],
        ),
        out_shape=outs,
        compiler_params=PARAMS,
    )(regimes, documents, pos, gammas, own, arrived_entry, update, source, *[transitions] * blocks)

    summed = held_term + swap(sent_term, "head", 1)
    by = 2
    while by < ways:
        split = summed.reshape(blocks, -1, 2, part, STATE)
        bit = lax.rem(lax.div(head, by), 2)
        going = lax.dynamic_index_in_dim(split, 1 - bit, 2, keepdims=False)
        staying = lax.dynamic_index_in_dim(split, bit, 2, keepdims=False)
        summed = staying + swap(going, "head", by)
        by *= 2
    summed = summed.reshape(blocks, part, STATE)

    level, side = lax.div(seq, 2), lax.rem(seq, 2)
    pieces, sources = [summed], [seq]
    for distance, parity in routes_up_to(levels - 1, levels):
        pieces.append(level_route(summed, distance, parity))
        lower = lax.rem(lax.div(level, distance), 2) == parity
        other = jnp.where(lower, level + distance, level - distance)
        valid = (other >= 0) & (other < levels)
        sources.append(jnp.where(valid, other * 2 + side, -1))
    sources = jnp.stack(sources).astype(jnp.int32)
    owned = REGIMES // devices

    def regime_sum(device):
        return pl.pallas_call(
            functools.partial(regime_kernel, blocks, owned, len(pieces)),
            in_specs=[SMEM] * 3 + [VMEM] * len(pieces),
            out_specs=VMEM,
            out_shape=shape(owned, part, STATE),
            compiler_params=PARAMS,
        )(regimes, jnp.reshape(device * owned, (1,)).astype(jnp.int32), sources, *pieces)

    regime_grad = regime_sum(seq) + swap(regime_sum(seq ^ 1), "seq", 1)

    wide = pl.BlockSpec((BLOCK, 2 * STATE), lambda c, h: (c, h))
    narrow = pl.BlockSpec((BLOCK, 2 * HEAD_DIM), lambda c, h: (c, h))
    states = pl.BlockSpec((1, 2 * HEAD_DIM, STATE), lambda c, h: (c, h, 0))
    query_grad, key_grad, value_grad = pl.pallas_call(
        within_kernel,
        grid=(blocks, heads // 2),
        in_specs=[wide, wide, narrow, narrow, states, states],
        out_specs=[wide, wide, narrow],
        out_shape=(
            shape(*queries.shape, dtype=BF16),
            shape(*keys.shape, dtype=BF16),
            shape(*values.shape, dtype=BF16),
        ),
        compiler_params=PARAMS,
        cost_estimate=pl.CostEstimate(
            flops=blocks * heads * 10 * BLOCK * BLOCK * STATE,
            bytes_accessed=6 << 20,
            transcendentals=0,
        ),
    )(queries, keys, values, out_grad, entries, leaves)
    return query_grad, key_grad, value_grad, regime_grad


def solution(mesh):
    in_specs = (
        P("seq", "head"),
        P("seq", "head"),
        P("seq", "head"),
        P("seq", "head"),
        P(),
        P("head"),
        P(),
        P(),
    )
    out_specs = (P("seq", "head"), P("seq", "head"), P("seq", "head"), P("seq", "head", None))
    return jax.shard_map(local, mesh=mesh, in_specs=in_specs, out_specs=out_specs, check_vma=False)
```

time: 263 us -> 85 us (0.32)
  waiting for transfers between devices: 128 us -> 31 us
  matrix products: 36.9 us -> 0 us
  local copies, waits for them, and re-layouts: 32 us -> 9.02 us
  starting transfers between devices: 44 us -> 25 us
  Pallas kernels: 0 us -> 15.9 us
  between operations: 14.3 us -> 0.81 us
  other arithmetic: 5.43 us -> 2.77 us
    ppermute x14 -> x12, waiting for transfers between devices: 89.4 us -> 31 us  [the longest x5 15.6 us: swap(): return lax.ppermute(x, axis, [(i, i ^ by) for i in range(count)])]
    dot_general x44 -> x0, matrix products: 36.9 us -> none  [the longest x20 8.68 us: rotate(): return jnp.einsum('nm,hmp->hnp', matrix, state, precision=PRECISE)]
    reduce_scatter x1 -> x0, waiting for transfers between devices: 24.3 us -> none  [local(): lax.psum_scatter(terms, 'head', scatter_dimension=1, tiled=True)]
    ppermute x14 -> x12, starting transfers between devices: 43.7 us -> 25 us  [the longest x7 17.3 us: level_route(): return lax.ppermute(x, 'seq', pairs)]
    pallas_call x0 -> x8, Pallas kernels: none -> 15.9 us  [the longest x1 5.38 us: local(): pl.pallas_call(within_kernel, grid=(blocks, heads // 2), in_specs=[wide,...]
    all_gather x1 -> x0, waiting for transfers between devices: 14.8 us -> none  [local(): lax.all_gather(head_summed, 'seq', axis=0, tiled=True)]
    reshape x5 -> x0, local copies, waits for them, and re-layouts: 6.93 us -> none  [the longest x1 2.64 us: local(): key_rows = keys.reshape(blocks_dev, BLOCK, heads_dev, STATE)]
    dynamic_slice x9 -> x0, local copies, waits for them, and re-layouts: 4.22 us -> none  [the longest x8 4.14 us: local(): lax.map(within, (query_rows, key_rows, value_rows, grad_rows, entries_b,...]
  transfers between devices with their start and end apart: 16 -> 12, of which waited for: 16 -> 7; matrix products, arithmetic and copies ran while one was open for 11% -> 0% of each run, Pallas kernels for 0% -> 9%
where the time goes in v1:
time: 85 us; the launch traced here: 84.5 us
  waiting for transfers between devices  31 us (36%)
  starting transfers between devices  25 us (29%)
  Pallas kernels  15.9 us (19%)
  local copies, waits for them, and re-layouts  9.02 us (11%)
  other arithmetic  2.77 us (3%)
    ppermute x7, starting transfers between devices, level_route(): return lax.ppermute(x, 'seq', pairs)  17.3 us
    ppermute x5, waiting for transfers between devices, swap(): return lax.ppermute(x, axis, [(i, i ^ by) for i in range(count)])  15.6 us
    ppermute x7, waiting for transfers between devices, level_route(): return lax.ppermute(x, 'seq', pairs)  15.4 us
    unnamed x34, local copies, waits for them, and re-layouts  8.9 us
    ppermute x5, starting transfers between devices, swap(): return lax.ppermute(x, axis, [(i, i ^ by) for i in range(count)])  7.7 us
    pallas_call x1, Pallas kernels, local(): pl.pallas_call(within_kernel, grid=(blocks, heads // 2), in_specs=[wide,...  5.38 us
    pallas_call x1, Pallas kernels, local(): pl.pallas_call(functools.partial(local_kernel, blocks, heads), grid_spec=...  2.9 us
    pallas_call x1, Pallas kernels, local(): pl.pallas_call(functools.partial(terms_kernel, blocks, heads, ways), grid...  2.66 us
  transfers between devices with their start and end apart: 12, of which 7 were waited for; matrix products, arithmetic and copies ran while one was open for 0% of the time, Pallas kernels for 9%

profile of v1, /device:TPU:0, one launch (start us, length us, event | category | flops | bytes accessed | tf_op | source)
XLA Modules:
  0.0 84.5 jit_solution(17144129129749976065)
XLA Ops:
  0.7 1.2 %copy-done.1 = bf16[512,1024]{1,0:T(8,128)(2,1)S(1)} copy-done((bf16[512,1024]{1,0:T(8,128)(2,1)S(1)}, bf16[512,1024]{1,0:T(8,128)(2,1)}, u32[]{:S(2)}) %copy-start.1) | copy-done | bytes 1048600
  1.9 1.2 %copy-done.3 = bf16[512,1024]{1,0:T(8,128)(2,1)S(1)} copy-done((bf16[512,1024]{1,0:T(8,128)(2,1)S(1)}, bf16[512,1024]{1,0:T(8,128)(2,1)}, u32[]{:S(2)}) %copy-start.3) | copy-done | bytes 1048600
  3.2 0.9 %copy-done.5 = bf16[512,256]{1,0:T(8,128)(2,1)S(1)} copy-done((bf16[512,256]{1,0:T(8,128)(2,1)S(1)}, bf16[512,256]{1,0:T(8,128)(2,1)}, u32[]{:S(2)}) %copy-start.5) | copy-done | bytes 262168
  4.1 0.9 %copy-done.7 = bf16[512,256]{1,0:T(8,128)(2,1)S(1)} copy-done((bf16[512,256]{1,0:T(8,128)(2,1)S(1)}, bf16[512,256]{1,0:T(8,128)(2,1)}, u32[]{:S(2)}) %copy-start.7) | copy-done | bytes 262168
  7.0 2.9 %shard_map.111 = (f32[2,256,256]{2,1,0:T(8,128)S(1)}, f32[2,256,256]{2,1,0:T(8,128)S(1)}, f32[2,128,256]{2,1,0:T(8,128)S(1)}, f32[2,128,256]{2,1,0:T(8,128)S(1)}) custom-call(s32[16]{0:T(128)S(1)} %copy-done.9, s32[16]{0:T(128)S(1)} %copy-done.12, s32[2]{0:T(128)S(1)} %pad_add_fusion.pos, f32[4]{0:T(128)S(1)} %copy-done.11, bf16[512,1024]{1,0:T(8,128)(2,1)S(1)} %copy-done.1, ...), custom_call_target="tpu_custom_call" | custom-call | tf_op jit(solution)/shard_map/pallas_call | solution.py:307
  9.9 3.0 %collective-permute-start = (f32[2,128,256]{2,1,0:T(8,128)S(1)}, f32[2,128,256]{2,1,0:T(8,128)S(1)}, u32[]{:S(2)}, u32[]{:S(2)}) collective-permute-start(f32[2,128,256]{2,1,0:T(8,128)S(1)} %get-tuple-element.23), channel_id=1, source_target_pairs={{0,4},{4,0},{8,12},{12,8},{16,20},{20,16},{24,28},{28,24},{1,5},{5... | collective-permute-start | bytes 786440 | tf_op jit(solution)/shard_map/ppermute | solution.py:252
  12.9 1.3 %shard_map.112 = (bf16[2,2,256,256]{3,2,1,0:T(8,128)(2,1)S(1)}, bf16[1,2,2,256,256]{4,3,2,1,0:T(8,128)(2,1)S(1)}) custom-call(s32[16]{0:T(128)S(1)} %copy-done.9, s32[16]{0:T(128)S(1)} %copy-done.12, s32[2]{0:T(128)S(1)} %pad_add_fusion.pos, bf16[32,256,256]{2,1,0:T(8,128)(2,1)S(1)} %copy-done), custom_call_target="tpu_custom_call" | custom-call | tf_op jit(solution)/shard_map/pallas_call | solution.py:323
  14.2 5.0 %collective-permute-done.arrived = f32[2,128,256]{2,1,0:T(8,128)S(1)} collective-permute-done((f32[2,128,256]{2,1,0:T(8,128)S(1)}, f32[2,128,256]{2,1,0:T(8,128)S(1)}, u32[]{:S(2)}, u32[]{:S(2)}) %collective-permute-start) | collective-permute-done | bytes 262176 | tf_op jit(solution)/shard_map/ppermute | solution.py:252
  19.2 0.9 %shard_map.113 = (f32[128,256]{1,0:T(8,128)S(1)}, f32[128,256]{1,0:T(8,128)S(1)}, f32[128,256]{1,0:T(8,128)S(1)}) custom-call(s32[2]{0:T(128)S(1)} %pad_add_fusion.pos, f32[4]{0:T(128)S(1)} %copy-done.11, f32[2,128,256]{2,1,0:T(8,128)S(1)} %get-tuple-element.22.held, f32[2,128,256]{2,1,0:T(8,128)S(1)} %collective-permute-done.arrived, ...), custom_call_target="tpu_custom_call" | custom-call | tf_op jit(solution)/shard_map/pallas_call | solution.py:331
  20.2 1.9 %collective-permute-start.1 = (f32[128,256]{1,0:T(8,128)S(1)}, f32[128,256]{1,0:T(8,128)S(1)}, u32[]{:S(2)}, u32[]{:S(2)}) collective-permute-start(f32[128,256]{1,0:T(8,128)S(1)} %get-tuple-element.25), channel_id=1, source_target_pairs={{0,8},{8,0},{4,12},{12,4},{16,24},{24,16},{20,28},{28,20},{1,9},{9... | collective-permute-start | bytes 393224 | tf_op jit(solution)/shard_map/ppermute | solution.py:263
  22.1 0.7 collective-permute-start.2
  22.7 3.9 %collective-permute-start.3 = (f32[128,256]{1,0:T(8,128)S(1)}, f32[128,256]{1,0:T(8,128)S(1)}, u32[]{:S(2)}, u32[]{:S(2)}) collective-permute-start(f32[128,256]{1,0:T(8,128)S(1)} %get-tuple-element.27), channel_id=1, source_target_pairs={{0,16},{16,0},{4,20},{20,4},{8,24},{24,8},{12,28},{28,12},{1,17},{... | collective-permute-start | bytes 393224 | tf_op jit(solution)/shard_map/ppermute | solution.py:263
  26.6 7.9 %collective-permute-done.3.rest_2_ = f32[128,256]{1,0:T(8,128)S(1)} collective-permute-done((f32[128,256]{1,0:T(8,128)S(1)}, f32[128,256]{1,0:T(8,128)S(1)}, u32[]{:S(2)}, u32[]{:S(2)}) %collective-permute-start.3) | collective-permute-done | bytes 131104 | tf_op jit(solution)/shard_map/ppermute | solution.py:263
  34.5 1.2 %shard_map.114 = (f32[2,128,256]{2,1,0:T(8,128)S(1)}, f32[2,128,256]{2,1,0:T(8,128)S(1)}) custom-call(s32[2]{0:T(128)S(1)} %pad_add_fusion.pos, f32[4]{0:T(128)S(1)} %copy-done.11, f32[2,128,256]{2,1,0:T(8,128)S(1)} %get-tuple-element.22.held, f32[2,128,256]{2,1,0:T(8,128)S(1)} %collective-permute-done.arrived, ...), custom_call_target="tpu_custom_call" | custom-call | tf_op jit(solution)/shard_map/pallas_call | solution.py:340
  35.7 1.6 %collective-permute-start.4 = (f32[2,128,256]{2,1,0:T(8,128)S(1)}, f32[2,128,256]{2,1,0:T(8,128)S(1)}, u32[]{:S(2)}, u32[]{:S(2)}) collective-permute-start(f32[2,128,256]{2,1,0:T(8,128)S(1)} %get-tuple-element.30), channel_id=1, source_target_pairs={{0,4},{4,0},{8,12},{12,8},{16,20},{20,16},{24,28},{28,24},{1,5},{5... | collective-permute-start | bytes 786440 | tf_op jit(solution)/shard_map/ppermute | solution.py:252
  37.2 4.9 %collective-permute-done.4.arrived = f32[2,128,256]{2,1,0:T(8,128)S(1)} collective-permute-done((f32[2,128,256]{2,1,0:T(8,128)S(1)}, f32[2,128,256]{2,1,0:T(8,128)S(1)}, u32[]{:S(2)}, u32[]{:S(2)}) %collective-permute-start.4) | collective-permute-done | bytes 262176 | tf_op jit(solution)/shard_map/ppermute | solution.py:252
  42.1 2.7 %shard_map.115 = (bf16[2,256,256]{2,1,0:T(8,128)(2,1)S(1)}, bf16[2,256,256]{2,1,0:T(8,128)(2,1)S(1)}, f32[2,2,64,256]{3,2,1,0:T(8,128)S(1)}, f32[2,2,64,256]{3,2,1,0:T(8,128)S(1)}) custom-call(s32[16]{0:T(128)S(1)} %copy-done.9, s32[16]{0:T(128)S(1)} %copy-done.12, s32[2]{0:T(128)S(1)} %pad_add_fusion.pos, f32[4]{0:T(128)S(1)} %copy-done.11, ...), custom_call_target="tpu_custom_call" | custom-call | tf_op jit(solution)/shard_map/pallas_call | solution.py:353
  45.5 1.7 %collective-permute-done.5 = f32[2,2,64,256]{3,2,0,1:T(8,128)} collective-permute-done((f32[2,2,64,256]{3,2,0,1:T(8,128)S(1)}, f32[2,2,64,256]{3,2,0,1:T(8,128)}, u32[]{:S(2)}, u32[]{:S(2)}) %collective-permute-start.5) | collective-permute-done | bytes 262176 | tf_op jit(solution)/shard_map/ppermute | solution.py:252
  47.2 1.0 %copy_add_fusion = f32[2,2,64,256]{3,2,0,1:T(8,128)S(1)} fusion(f32[2,2,64,256]{3,2,0,1:T(8,128)} %collective-permute-done.5, f32[2,2,64,256]{3,2,1,0:T(8,128)S(1)} %get-tuple-element.38), kind=kLoop, calls=%fused_computation | loop fusion | flops 65536 | bytes 786432 | tf_op jit(solution)/shard_map/add | solution.py:368
  48.2 1.6 %collective-permute-start.6 = (f32[2,1,64,256]{3,2,0,1:T(8,128)S(1)}, f32[2,1,64,256]{3,2,0,1:T(8,128)S(1)}, u32[]{:S(2)}, u32[]{:S(2)}) collective-permute-start(f32[2,1,64,256]{3,2,0,1:T(8,128)S(1)} %constant_dynamic-slice_fusion), channel_id=1, source_target_pairs={{0,2},{1,3},{2,0},{3,1},{4,6},{5,7},{6,4},{7,5},{8,10},{9,11},{10,... | collective-permute-start | bytes 393224 | tf_op jit(solution)/shard_map/ppermute | solution.py:252
  49.8 4.0 %collective-permute-done.6 = f32[2,1,64,256]{3,2,0,1:T(8,128)S(1)} collective-permute-done((f32[2,1,64,256]{3,2,0,1:T(8,128)S(1)}, f32[2,1,64,256]{3,2,0,1:T(8,128)S(1)}, u32[]{:S(2)}, u32[]{:S(2)}) %collective-permute-start.6) | collective-permute-done | bytes 131104 | tf_op jit(solution)/shard_map/ppermute | solution.py:252
  53.8 5.3 %collective-permute-start.10 = (f32[2,64,256]{2,1,0:T(8,128)S(1)}, f32[2,64,256]{2,1,0:T(8,128)S(1)}, u32[]{:S(2)}, u32[]{:S(2)}) collective-permute-start(f32[2,64,256]{2,1,0:T(8,128)S(1)} %add_bitcast_fusion.rest_0_), channel_id=1, source_target_pairs={{0,24},{24,0},{4,28},{28,4},{1,25},{25,1},{5,29},{29,5},{2,26},{26... | collective-permute-start | bytes 393224 | tf_op jit(solution)/shard_map/ppermute | solution.py:263
  59.2 0.7 collective-permute-start.8
  59.9 4.8 %collective-permute-start.9 = (f32[2,64,256]{2,1,0:T(8,128)S(1)}, f32[2,64,256]{2,1,0:T(8,128)S(1)}, u32[]{:S(2)}, u32[]{:S(2)}) collective-permute-start(f32[2,64,256]{2,1,0:T(8,128)S(1)} %add_bitcast_fusion.rest_0_), channel_id=1, source_target_pairs={{0,16},{16,0},{4,20},{20,4},{8,24},{24,8},{12,28},{28,12},{1,17},{... | collective-permute-start | bytes 393224 | tf_op jit(solution)/shard_map/ppermute | solution.py:263
  65.1 7.3 %collective-permute-done.9.rest_3_ = f32[2,64,256]{2,1,0:T(8,128)S(1)} collective-permute-done((f32[2,64,256]{2,1,0:T(8,128)S(1)}, f32[2,64,256]{2,1,0:T(8,128)S(1)}, u32[]{:S(2)}, u32[]{:S(2)}) %collective-permute-start.9) | collective-permute-done | bytes 131104 | tf_op jit(solution)/shard_map/ppermute | solution.py:263
  72.3 0.8 shard_map.118
  73.1 1.6 %collective-permute-start.11 = (f32[4,64,256]{2,1,0:T(8,128)S(1)}, f32[4,64,256]{2,1,0:T(8,128)}, u32[]{:S(2)}, u32[]{:S(2)}) collective-permute-start(f32[4,64,256]{2,1,0:T(8,128)S(1)} %shard_map.118), channel_id=1, source_target_pairs={{0,4},{4,0},{8,12},{12,8},{16,20},{20,16},{24,28},{28,24},{1,5},{5... | collective-permute-start | bytes 786440 | tf_op jit(solution)/shard_map/ppermute | solution.py:252
  74.7 0.9 %copy-done.14 = bf16[2,256,256]{2,1,0:T(8,128)(2,1)S(1)} copy-done((bf16[2,256,256]{2,1,0:T(8,128)(2,1)S(1)}, bf16[2,256,256]{2,1,0:T(8,128)(2,1)}, u32[]{:S(2)}) %copy-start.14) | copy-done | bytes 262168
  75.7 0.9 %copy-done.16 = bf16[2,256,256]{2,1,0:T(8,128)(2,1)S(1)} copy-done((bf16[2,256,256]{2,1,0:T(8,128)(2,1)S(1)}, bf16[2,256,256]{2,1,0:T(8,128)(2,1)}, u32[]{:S(2)}) %copy-start.16) | copy-done | bytes 262168
  76.6 5.4 %shard_map.116 = (bf16[512,1024]{1,0:T(8,128)(2,1)}, bf16[512,1024]{1,0:T(8,128)(2,1)}, bf16[512,256]{1,0:T(8,128)(2,1)}) custom-call(bf16[512,1024]{1,0:T(8,128)(2,1)S(1)} %copy-done.2, bf16[512,1024]{1,0:T(8,128)(2,1)S(1)} %copy-done.4, bf16[512,256]{1,0:T(8,128)(2,1)S(1)} %copy-done.6, bf16[512,256]{1,0:T(8,128)(2,1)S(1)} %copy-done.8, ...), custom_call_target="tpu_custom_call" | custom-call | flops 1342177280 | bytes 6291456 | tf_op jit(solution)/shard_map/pallas_call | solution.py:404
  82.0 0.8 shard_map.117
  82.8 1.7 %add.53 = f32[4,64,256]{2,1,0:T(8,128)} add(f32[4,64,256]{2,1,0:T(8,128)S(1)} %shard_map.117, f32[4,64,256]{2,1,0:T(8,128)} %collective-permute-done.11) | non-fusion elementwise | flops 65536 | bytes 786432 | tf_op jit(solution)/shard_map/add | solution.py:399
  (41 shorter events, 3.3 us)
Async XLA Ops:
  0.7 1.2 %copy-start.1 = (bf16[512,1024]{1,0:T(8,128)(2,1)S(1)}, bf16[512,1024]{1,0:T(8,128)(2,1)}, u32[]{:S(2)}) copy-start(bf16[512,1024]{1,0:T(8,128)(2,1)} %q.3) | copy-start | bytes 3145732
  1.9 1.2 %copy-start.3 = (bf16[512,1024]{1,0:T(8,128)(2,1)S(1)}, bf16[512,1024]{1,0:T(8,128)(2,1)}, u32[]{:S(2)}) copy-start(bf16[512,1024]{1,0:T(8,128)(2,1)} %k.3) | copy-start | bytes 3145732
  3.2 0.9 %copy-start.5 = (bf16[512,256]{1,0:T(8,128)(2,1)S(1)}, bf16[512,256]{1,0:T(8,128)(2,1)}, u32[]{:S(2)}) copy-start(bf16[512,256]{1,0:T(8,128)(2,1)} %v.3) | copy-start | bytes 786436
  4.1 0.9 %copy-start.7 = (bf16[512,256]{1,0:T(8,128)(2,1)S(1)}, bf16[512,256]{1,0:T(8,128)(2,1)}, u32[]{:S(2)}) copy-start(bf16[512,256]{1,0:T(8,128)(2,1)} %dy.3) | copy-start | bytes 786436
  5.1 0.7 copy-start.9
  5.7 0.7 copy-start.11
  6.4 0.7 copy-start.12
  7.0 5.9 %copy-start = (bf16[32,256,256]{2,1,0:T(8,128)(2,1)S(1)}, bf16[32,256,256]{2,1,0:T(8,128)(2,1)}, u32[]{:S(2)}) copy-start(bf16[32,256,256]{2,1,0:T(8,128)(2,1)} %rest_1_.3) | copy-start | bytes 12582916
  9.9 9.3 %collective-permute-start = (f32[2,128,256]{2,1,0:T(8,128)S(1)}, f32[2,128,256]{2,1,0:T(8,128)S(1)}, u32[]{:S(2)}, u32[]{:S(2)}) collective-permute-start(f32[2,128,256]{2,1,0:T(8,128)S(1)} %get-tuple-element.23), channel_id=1, source_target_pairs={{0,4},{4,0},{8,12},{12,8},{16,20},{20,16},{24,28},{28,24},{1,5},{5... | collective-permute-start | bytes 786440 | tf_op jit(solution)/shard_map/ppermute | solution.py:252
  20.2 6.5 %collective-permute-start.1 = (f32[128,256]{1,0:T(8,128)S(1)}, f32[128,256]{1,0:T(8,128)S(1)}, u32[]{:S(2)}, u32[]{:S(2)}) collective-permute-start(f32[128,256]{1,0:T(8,128)S(1)} %get-tuple-element.25), channel_id=1, source_target_pairs={{0,8},{8,0},{4,12},{12,4},{16,24},{24,16},{20,28},{28,20},{1,9},{9... | collective-permute-start | bytes 393224 | tf_op jit(solution)/shard_map/ppermute | solution.py:263
  22.1 4.6 %collective-permute-start.2 = (f32[128,256]{1,0:T(8,128)S(1)}, f32[128,256]{1,0:T(8,128)S(1)}, u32[]{:S(2)}, u32[]{:S(2)}) collective-permute-start(f32[128,256]{1,0:T(8,128)S(1)} %get-tuple-element.26), channel_id=1, source_target_pairs={{8,16},{16,8},{12,20},{20,12},{9,17},{17,9},{13,21},{21,13},{10,18... | collective-permute-start | bytes 393224 | tf_op jit(solution)/shard_map/ppermute | solution.py:263
  22.7 11.8 %collective-permute-start.3 = (f32[128,256]{1,0:T(8,128)S(1)}, f32[128,256]{1,0:T(8,128)S(1)}, u32[]{:S(2)}, u32[]{:S(2)}) collective-permute-start(f32[128,256]{1,0:T(8,128)S(1)} %get-tuple-element.27), channel_id=1, source_target_pairs={{0,16},{16,0},{4,20},{20,4},{8,24},{24,8},{12,28},{28,12},{1,17},{... | collective-permute-start | bytes 393224 | tf_op jit(solution)/shard_map/ppermute | solution.py:263
  35.7 6.4 %collective-permute-start.4 = (f32[2,128,256]{2,1,0:T(8,128)S(1)}, f32[2,128,256]{2,1,0:T(8,128)S(1)}, u32[]{:S(2)}, u32[]{:S(2)}) collective-permute-start(f32[2,128,256]{2,1,0:T(8,128)S(1)} %get-tuple-element.30), channel_id=1, source_target_pairs={{0,4},{4,0},{8,12},{12,8},{16,20},{20,16},{24,28},{28,24},{1,5},{5... | collective-permute-start | bytes 786440 | tf_op jit(solution)/shard_map/ppermute | solution.py:252
  42.1 30.2 %copy-start.10 = (s32[16]{0:T(128)S(1)}, s32[16]{0:T(128)}, u32[]{:S(2)}) copy-start(s32[16]{0:T(128)} %regimes.9) | copy-start | bytes 196
  42.1 32.6 %copy-start.2 = (bf16[512,1024]{1,0:T(8,128)(2,1)S(1)}, bf16[512,1024]{1,0:T(8,128)(2,1)}, u32[]{:S(2)}) copy-start(bf16[512,1024]{1,0:T(8,128)(2,1)} %q.3) | copy-start | bytes 3145732
  42.1 32.6 %copy-start.4 = (bf16[512,1024]{1,0:T(8,128)(2,1)S(1)}, bf16[512,1024]{1,0:T(8,128)(2,1)}, u32[]{:S(2)}) copy-start(bf16[512,1024]{1,0:T(8,128)(2,1)} %k.3) | copy-start | bytes 3145732
  42.1 32.6 %copy-start.6 = (bf16[512,256]{1,0:T(8,128)(2,1)S(1)}, bf16[512,256]{1,0:T(8,128)(2,1)}, u32[]{:S(2)}) copy-start(bf16[512,256]{1,0:T(8,128)(2,1)} %v.3) | copy-start | bytes 786436
  42.1 32.6 %copy-start.8 = (bf16[512,256]{1,0:T(8,128)(2,1)S(1)}, bf16[512,256]{1,0:T(8,128)(2,1)}, u32[]{:S(2)}) copy-start(bf16[512,256]{1,0:T(8,128)(2,1)} %dy.3) | copy-start | bytes 786436
  44.8 0.7 copy-start.15
  44.8 27.5 %copy-start.13 = (bf16[2,256,256]{2,1,0:T(8,128)(2,1)}, bf16[2,256,256]{2,1,0:T(8,128)(2,1)S(1)}, u32[]{:S(2)}) copy-start(bf16[2,256,256]{2,1,0:T(8,128)(2,1)S(1)} %get-tuple-element.33.entry) | copy-start | bytes 786436
  45.5 1.7 %collective-permute-start.5 = (f32[2,2,64,256]{3,2,0,1:T(8,128)S(1)}, f32[2,2,64,256]{3,2,0,1:T(8,128)}, u32[]{:S(2)}, u32[]{:S(2)}) collective-permute-start(f32[2,2,64,256]{3,2,0,1:T(8,128)S(1)} %copy.12), channel_id=1, source_target_pairs={{0,1},{1,0},{2,3},{3,2},{4,5},{5,4},{6,7},{7,6},{8,9},{9,8},{10,11... | collective-permute-start | bytes 786440 | tf_op jit(solution)/shard_map/ppermute | solution.py:252
  48.2 5.6 %collective-permute-start.6 = (f32[2,1,64,256]{3,2,0,1:T(8,128)S(1)}, f32[2,1,64,256]{3,2,0,1:T(8,128)S(1)}, u32[]{:S(2)}, u32[]{:S(2)}) collective-permute-start(f32[2,1,64,256]{3,2,0,1:T(8,128)S(1)} %constant_dynamic-slice_fusion), channel_id=1, source_target_pairs={{0,2},{1,3},{2,0},{3,1},{4,6},{5,7},{6,4},{7,5},{8,10},{9,11},{10,... | collective-permute-start | bytes 393224 | tf_op jit(solution)/shard_map/ppermute | solution.py:252
  53.8 10.9 %collective-permute-start.10 = (f32[2,64,256]{2,1,0:T(8,128)S(1)}, f32[2,64,256]{2,1,0:T(8,128)S(1)}, u32[]{:S(2)}, u32[]{:S(2)}) collective-permute-start(f32[2,64,256]{2,1,0:T(8,128)S(1)} %add_bitcast_fusion.rest_0_), channel_id=1, source_target_pairs={{0,24},{24,0},{4,28},{28,4},{1,25},{25,1},{5,29},{29,5},{2,26},{26... | collective-permute-start | bytes 393224 | tf_op jit(solution)/shard_map/ppermute | solution.py:263
  59.2 5.9 %collective-permute-start.7 = (f32[2,64,256]{2,1,0:T(8,128)S(1)}, f32[2,64,256]{2,1,0:T(8,128)S(1)}, u32[]{:S(2)}, u32[]{:S(2)}) collective-permute-start(f32[2,64,256]{2,1,0:T(8,128)S(1)} %add_bitcast_fusion.rest_0_), channel_id=1, source_target_pairs={{0,8},{8,0},{4,12},{12,4},{16,24},{24,16},{20,28},{28,20},{1,9},{9... | collective-permute-start | bytes 393224 | tf_op jit(solution)/shard_map/ppermute | solution.py:263
  59.2 5.8 %collective-permute-start.8 = (f32[2,64,256]{2,1,0:T(8,128)S(1)}, f32[2,64,256]{2,1,0:T(8,128)S(1)}, u32[]{:S(2)}, u32[]{:S(2)}) collective-permute-start(f32[2,64,256]{2,1,0:T(8,128)S(1)} %add_bitcast_fusion.rest_0_), channel_id=1, source_target_pairs={{8,16},{16,8},{12,20},{20,12},{9,17},{17,9},{13,21},{21,13},{10,18... | collective-permute-start | bytes 393224 | tf_op jit(solution)/shard_map/ppermute | solution.py:263
  59.9 12.4 %collective-permute-start.9 = (f32[2,64,256]{2,1,0:T(8,128)S(1)}, f32[2,64,256]{2,1,0:T(8,128)S(1)}, u32[]{:S(2)}, u32[]{:S(2)}) collective-permute-start(f32[2,64,256]{2,1,0:T(8,128)S(1)} %add_bitcast_fusion.rest_0_), channel_id=1, source_target_pairs={{0,16},{16,0},{4,20},{20,4},{8,24},{24,8},{12,28},{28,12},{1,17},{... | collective-permute-start | bytes 393224 | tf_op jit(solution)/shard_map/ppermute | solution.py:263
  73.1 9.7 %collective-permute-start.11 = (f32[4,64,256]{2,1,0:T(8,128)S(1)}, f32[4,64,256]{2,1,0:T(8,128)}, u32[]{:S(2)}, u32[]{:S(2)}) collective-permute-start(f32[4,64,256]{2,1,0:T(8,128)S(1)} %shard_map.118), channel_id=1, source_target_pairs={{0,4},{4,0},{8,12},{12,8},{16,20},{20,16},{24,28},{28,24},{1,5},{5... | collective-permute-start | bytes 786440 | tf_op jit(solution)/shard_map/ppermute | solution.py:252
  74.7 1.0 %copy-start.14 = (bf16[2,256,256]{2,1,0:T(8,128)(2,1)S(1)}, bf16[2,256,256]{2,1,0:T(8,128)(2,1)}, u32[]{:S(2)}) copy-start(bf16[2,256,256]{2,1,0:T(8,128)(2,1)} %copy-done.13) | copy-start | bytes 786436
  75.7 0.9 %copy-start.16 = (bf16[2,256,256]{2,1,0:T(8,128)(2,1)S(1)}, bf16[2,256,256]{2,1,0:T(8,128)(2,1)}, u32[]{:S(2)}) copy-start(bf16[2,256,256]{2,1,0:T(8,128)(2,1)} %copy-done.15) | copy-start | bytes 786436

commit v2 on v1

--- a/solution.py
+++ b/solution.py
@@ -19,6 +19,7 @@
 TN = (((0,), (0,)), ((), ()))
 VMEM = pl.BlockSpec(memory_space=pltpu.VMEM)
 SMEM = pl.BlockSpec(memory_space=pltpu.SMEM)
+HBM = pl.BlockSpec(memory_space=pltpu.HBM)
 PARAMS = pltpu.CompilerParams(vmem_limit_bytes=48 << 20)
 
 
@@ -57,28 +58,64 @@
     return jnp.concatenate(parts, axis=0)
 
 
-def local_kernel(blocks, heads, regimes, documents, pos, gammas, q, k, v, dy, *rest):
-    mats, (update, source, sent, held) = rest[:blocks], rest[blocks:]
-    seq = pos[0]
-    rows = heads * HEAD_DIM
-    half = rows // 2
+def local_kernel(
+    blocks, heads, regimes_hbm, documents_hbm, gammas_hbm, transitions, q_hbm, k_hbm, v_hbm, dy_hbm,
+    update, source, sent, held,
+    regimes, documents, gammas, mats, q, k, v, dy, small_sems, mat_sems, row_sems, wide_sems,
+):
+    seq = lax.axis_index("seq")
+    half = heads * HEAD_DIM // 2
+    split = heads * STATE // 2
+    small = [
+        pltpu.make_async_copy(a, b, small_sems.at[i])
+        for i, (a, b) in enumerate(
+            ((regimes_hbm, regimes), (documents_hbm, documents), (gammas_hbm, gammas))
+        )
+    ]
+    for copy in small:
+        copy.start()
+    rows, wide = {}, {}
+    for i, (a, b, wide_a, wide_b) in enumerate(((v_hbm, v, k_hbm, k), (dy_hbm, dy, q_hbm, q))):
+        for c in range(blocks):
+            token = pl.ds(c * BLOCK, BLOCK)
+            rows[i, c] = pltpu.make_async_copy(a.at[token], b.at[token], row_sems.at[i, c])
+            rows[i, c].start()
+            for j in range(2):
+                at = (token, pl.ds(j * split, split))
+                wide[i, c, j] = pltpu.make_async_copy(
+                    wide_a.at[at], wide_b.at[at], wide_sems.at[i, c, j]
+                )
+                wide[i, c, j].start()
+    small[0].wait()
+    mat_copies = []
+    for c in range(blocks):
+        copy = pltpu.make_async_copy(
+            transitions.at[regimes[seq * blocks + c]], mats.at[c], mat_sems.at[c]
+        )
+        copy.start()
+        mat_copies.append(copy)
+    for i, (out, narrow_in, wide_in) in enumerate(((update, v, k), (source, dy, q))):
+        for c in range(blocks):
+            token = slice(c * BLOCK, (c + 1) * BLOCK)
+            rows[i, c].wait()
+            for h in range(heads):
+                if h % (heads // 2) == 0:
+                    wide[i, c, h // (heads // 2)].wait()
+                columns = slice(h * STATE, (h + 1) * STATE)
+                narrow = slice(h * HEAD_DIM, (h + 1) * HEAD_DIM)
+                out[c, narrow, :] = dot(narrow_in[token, narrow], wide_in[token, columns], TN)
+    for copy in small[1:] + mat_copies:
+        copy.wait()
     decay = decay_column(gammas, 0, heads, 1)
-    for c in range(blocks):
-        token = slice(c * BLOCK, (c + 1) * BLOCK)
-        for h in range(heads):
-            wide = slice(h * STATE, (h + 1) * STATE)
-            narrow = slice(h * HEAD_DIM, (h + 1) * HEAD_DIM)
-            update[c, narrow, :] = dot(v[token, narrow], k[token, wide], TN)
-            source[c, narrow, :] = dot(dy[token, narrow], q[token, wide], TN)
     state = update[0]
     for c in range(1, blocks):
         factor = kept_at(documents, seq * blocks + c) * decay
-        state = update[c] + factor * dot_exact(state, mats[c][0], NT)
+        state = update[c] + factor * dot_exact(state, mats[c], NT)
     carried = None
     for c in reversed(range(blocks)):
         total = source[c] if carried is None else source[c] + carried
         factor = kept_at(documents, seq * blocks + c) * decay
-        carried = factor * dot_exact(total, mats[c][0], NN)
+        carried = factor * dot_exact(total, mats[c], NN)
     upper = lax.rem(seq, 2) == 1
     for i, value in enumerate((state, carried)):
         first, second = value[:half], value[half:]
@@ -181,33 +218,38 @@
     sent[1] = jnp.where(is_upper, inner_backward, backward)
 
 
-def terms_kernel(
-    blocks, heads, ways, regimes, documents, pos, gammas, own, arrived, update, source, *rest
-):
-    mats, (entries, leaves, held, sent, term) = rest[:blocks], rest[blocks:]
-    seq, head = pos[0], pos[1]
-    upper = lax.rem(seq, 2) == 1
-    decay = decay_column(gammas, 0, heads, 1)
-
+def states_of(blocks, upper, kept, decay, own, arrived, update, source, mats):
     def whole(i):
         first = jnp.where(upper, arrived[i], own[i])
         second = jnp.where(upper, own[i], arrived[i])
         return jnp.concatenate([first, second], axis=0)
 
     before, carried = whole(0), whole(1)
-    kept = [kept_at(documents, seq * blocks + c) for c in range(blocks)]
-    befores, totals = [], []
+    befores, entries, leaves, totals = [], [], [None] * blocks, [None] * blocks
     for c in range(blocks):
         befores.append(halves(before))
         high, low = befores[-1]
         entry = (kept[c] * decay) * (dot(high, mats[c][0], NT) + dot(low, mats[c][0], NT))
-        entries[c] = entry.astype(BF16)
+        entries.append(entry)
         before = entry + update[c]
     for c in reversed(range(blocks)):
-        leaves[c] = carried.astype(BF16)
-        total = source[c] + carried
-        totals.insert(0, total)
-        carried = (kept[c] * decay) * dot_exact(total, mats[c][0], NN)
+        leaves[c] = carried
+        totals[c] = source[c] + carried
+        if c > 0:
+            carried = (kept[c] * decay) * dot_exact(totals[c], mats[c][0], NN)
+    return befores, entries, leaves, totals
+
+
+def terms_kernel(
+    blocks, heads, ways, regimes, documents, pos, gammas, own, arrived, update, source, *rest
+):
+    mats, (held, sent, term) = rest[:blocks], rest[blocks:]
+    seq, head = pos[0], pos[1]
+    decay = decay_column(gammas, 0, heads, 1)
+    kept = [kept_at(documents, seq * blocks + c) for c in range(blocks)]
+    befores, _, _, totals = states_of(
+        blocks, lax.rem(seq, 2) == 1, kept, decay, own, arrived, update, source, mats
+    )
     part = STATE // ways
     core = lax.rem(head, 2)
     for c in range(blocks):
@@ -217,17 +259,35 @@
             sent[c, i] = term[pl.ds(pl.multiple_of((2 * i + 1 - core) * part, part), part), :]
 
 
+def rounded_kernel(
+    blocks, heads, regimes, documents, pos, gammas, own, arrived, update, source, *rest
+):
+    mats, (entries, leaves) = rest[:blocks], rest[blocks:]
+    seq = pos[0]
+    decay = decay_column(gammas, 0, heads, 1)
+    kept = [kept_at(documents, seq * blocks + c) for c in range(blocks)]
+    _, entry, leave, _ = states_of(
+        blocks, lax.rem(seq, 2) == 1, kept, decay, own, arrived, update, source, mats
+    )
+    for c in range(blocks):
+        entries[c] = entry[c].astype(BF16)
+        leaves[c] = leave[c].astype(BF16)
+
+
 def regime_kernel(blocks, owned, count, regimes, base, sources, *rest):
     pieces, out = rest[:count], rest[count]
     for r in range(owned):
         total = None
         for i in range(count):
             for c in range(blocks):
-                block = jnp.maximum(sources[i], 0) * blocks + c
-                match = (sources[i] >= 0) & (regimes[block] == base[0] + r)
+                match = regimes[sources[i] * blocks + c] == base[0] + r
                 value = jnp.where(match, pieces[i][c], 0.0)
                 total = value if total is None else total + value
         out[r] = total
+
+
+def add_kernel(a, b, out):
+    out[...] = a[...] + b[...]
 
 
 def within_kernel(q, k, v, dy, entry, leave, dq, dk, dv):
@@ -282,7 +342,7 @@
     rows = heads * HEAD_DIM
     half = rows // 2
     reach = min(levels - 1, -(-(all_blocks // 2 - 1) // (2 * blocks)))
-    routes = routes_up_to(reach, levels)
+    routes = routes_up_to(reach, levels)[::-1]
     seq, head = lax.axis_index("seq"), lax.axis_index("head")
     pos = jnp.stack([seq, head]).astype(jnp.int32)
 
@@ -306,15 +366,25 @@
     outs = (state_shape, state_shape, half_shape, half_shape)
     update, source, sent, held = pl.pallas_call(
         functools.partial(local_kernel, blocks, heads),
-        grid_spec=pltpu.PrefetchScalarGridSpec(
-            num_scalar_prefetch=3,
-            grid=(1,),
-            in_specs=[SMEM] + [whole(x) for x in (queries, keys, values, out_grad)] + own_mats(),
-            out_specs=[whole(x) for x in outs],
-        ),
+        in_specs=[HBM] * 8,
+        out_specs=(VMEM,) * 4,
         out_shape=outs,
-        compiler_params=PARAMS,
-    )(regimes, documents, pos, gammas, queries, keys, values, out_grad, *[transitions] * blocks)
+        scratch_shapes=[
+            pltpu.SMEM(regimes.shape, jnp.int32),
+            pltpu.SMEM(documents.shape, jnp.int32),
+            pltpu.SMEM(gammas.shape, F32),
+            pltpu.VMEM((blocks, STATE, STATE), BF16),
+            pltpu.VMEM(queries.shape, BF16),
+            pltpu.VMEM(keys.shape, BF16),
+            pltpu.VMEM(values.shape, BF16),
+            pltpu.VMEM(out_grad.shape, BF16),
+            pltpu.SemaphoreType.DMA((3,)),
+            pltpu.SemaphoreType.DMA((blocks,)),
+            pltpu.SemaphoreType.DMA((2, blocks)),
+            pltpu.SemaphoreType.DMA((2, blocks, 2)),
+        ],
+        compiler_params=pltpu.CompilerParams(vmem_limit_bytes=60 << 20),
+    )(regimes, documents, gammas, transitions, queries, keys, values, out_grad)
 
     arrived = swap(sent, "seq", 1)
     map_shapes = (shape(2, 2, STATE, STATE, dtype=BF16),)
@@ -349,21 +419,28 @@
     part = STATE // ways
     part_shape = shape(blocks, ways // 2, part, STATE)
     bf16_states = shape(blocks, rows, STATE, dtype=BF16)
-    outs = (bf16_states, bf16_states, part_shape, part_shape)
-    entries, leaves, held_term, sent_term = pl.pallas_call(
+    states = (own, arrived_entry, update, source)
+
+    def states_call(kernel, states, outs, scratch):
+        return pl.pallas_call(
+            kernel,
+            grid_spec=pltpu.PrefetchScalarGridSpec(
+                num_scalar_prefetch=3,
+                grid=(1,),
+                in_specs=[SMEM] + [whole(x) for x in states] + own_mats(),
+                out_specs=[whole(x) for x in outs],
+                scratch_shapes=scratch,
+            ),
+            out_shape=outs,
+            compiler_params=PARAMS,
+        )(regimes, documents, pos, gammas, *states, *[transitions] * blocks)
+
+    held_term, sent_term = states_call(
         functools.partial(terms_kernel, blocks, heads, ways),
-        grid_spec=pltpu.PrefetchScalarGridSpec(
-            num_scalar_prefetch=3,
-            grid=(1,),
-            in_specs=[SMEM]
-            + [whole(x) for x in (own, arrived_entry, update, source)]
-            + own_mats(),
-            out_specs=[whole(x) for x in outs],
-            scratch_shapes=[pltpu.VMEM((STATE, STATE), F32)],
-        ),
-        out_shape=outs,
-        compiler_params=PARAMS,
-    )(regimes, documents, pos, gammas, own, arrived_entry, update, source, *[transitions] * blocks)
+        states,
+        (part_shape, part_shape),
+        [pltpu.VMEM((STATE, STATE), F32)],
+    )
 
     summed = held_term + swap(sent_term, "head", 1)
     by = 2
@@ -376,28 +453,14 @@
         by *= 2
     summed = summed.reshape(blocks, part, STATE)
 
-    level, side = lax.div(seq, 2), lax.rem(seq, 2)
-    pieces, sources = [summed], [seq]
-    for distance, parity in routes_up_to(levels - 1, levels):
-        pieces.append(level_route(summed, distance, parity))
-        lower = lax.rem(lax.div(level, distance), 2) == parity
-        other = jnp.where(lower, level + distance, level - distance)
-        valid = (other >= 0) & (other < levels)
-        sources.append(jnp.where(valid, other * 2 + side, -1))
-    sources = jnp.stack(sources).astype(jnp.int32)
+    pieces = [summed] + [swap(summed, "seq", 2 * by) for by in range(1, levels)]
+    sources = jnp.stack([seq ^ (2 * by) for by in range(levels)]).astype(jnp.int32)
     owned = REGIMES // devices
 
-    def regime_sum(device):
-        return pl.pallas_call(
-            functools.partial(regime_kernel, blocks, owned, len(pieces)),
-            in_specs=[SMEM] * 3 + [VMEM] * len(pieces),
-            out_specs=VMEM,
-            out_shape=shape(owned, part, STATE),
-            compiler_params=PARAMS,
-        )(regimes, jnp.reshape(device * owned, (1,)).astype(jnp.int32), sources, *pieces)
-
-    regime_grad = regime_sum(seq) + swap(regime_sum(seq ^ 1), "seq", 1)
-
+    states, summed = lax.optimization_barrier((states, summed))
+    entries, leaves = states_call(
+        functools.partial(rounded_kernel, blocks, heads), states, (bf16_states, bf16_states), []
+    )
     wide = pl.BlockSpec((BLOCK, 2 * STATE), lambda c, h: (c, h))
     narrow = pl.BlockSpec((BLOCK, 2 * HEAD_DIM), lambda c, h: (c, h))
     states = pl.BlockSpec((1, 2 * HEAD_DIM, STATE), lambda c, h: (c, h, 0))
@@ -418,6 +481,27 @@
             transcendentals=0,
         ),
     )(queries, keys, values, out_grad, entries, leaves)
+    pieces, query_grad, key_grad, value_grad = lax.optimization_barrier(
+        (pieces, query_grad, key_grad, value_grad)
+    )
+
+    def regime_sum(device):
+        return pl.pallas_call(
+            functools.partial(regime_kernel, blocks, owned, len(pieces)),
+            in_specs=[SMEM] * 3 + [VMEM] * len(pieces),
+            out_specs=VMEM,
+            out_shape=shape(owned, part, STATE),
+            compiler_params=PARAMS,
+        )(regimes, jnp.reshape(device * owned, (1,)).astype(jnp.int32), sources, *pieces)
+
+    arrived_sum = swap(regime_sum(seq ^ 1), "seq", 1)
+    regime_grad = pl.pallas_call(
+        add_kernel,
+        in_specs=[VMEM, VMEM],
+        out_specs=VMEM,
+        out_shape=shape(owned, part, STATE),
+        compiler_params=PARAMS,
+    )(regime_sum(seq), arrived_sum)
     return query_grad, key_grad, value_grad, regime_grad
 
 

time: 85 us -> 67.5 us (0.79)
  waiting for transfers between devices: 31 us -> 22.9 us
  local copies, waits for them, and re-layouts: 9.02 us -> 2.26 us
  starting transfers between devices: 25 us -> 20.5 us
  Pallas kernels: 15.9 us -> 20.3 us
  other arithmetic: 2.77 us -> 0.2 us
    ppermute x7 -> x3, waiting for transfers between devices: 15.4 us -> 3.72 us  [level_route(): return lax.ppermute(x, 'seq', pairs)]
    ppermute x7 -> x3, starting transfers between devices: 17.3 us -> 6.45 us  [level_route(): return lax.ppermute(x, 'seq', pairs)]
    unnamed x34 -> x22, local copies, waits for them, and re-layouts: 8.9 us -> 2.23 us
    ppermute x5 -> x8, starting transfers between devices: 7.7 us -> 14 us  [swap(): return lax.ppermute(x, axis, [(i, i ^ by) for i in range(count)])]
    pallas_call x2 -> x4, Pallas kernels: 5.56 us -> 10.1 us  [the longest x1 4.79 us: local(): pl.pallas_call(functools.partial(local_kernel, blocks, heads), in_specs=[...]
    ppermute x5 -> x8, waiting for transfers between devices: 15.6 us -> 19.1 us  [swap(): return lax.ppermute(x, axis, [(i, i ^ by) for i in range(count)])]
    add x1 -> x0, other arithmetic: 1.69 us -> none  [local(): regime_grad = regime_sum(seq) + swap(regime_sum(seq ^ 1), 'seq', 1)]
    add x1, other arithmetic: 0.98 us -> 0.03 us  [local(): summed = held_term + swap(sent_term, 'head', 1)]
  transfers between devices with their start and end apart: 12 -> 11, of which waited for: 7 -> 8; matrix products, arithmetic and copies ran while one was open for 0% -> 0% of each run, Pallas kernels for 9% -> 14%
where the time goes in v2:
time: 67.5 us; the launch traced here: 66.9 us
  waiting for transfers between devices  22.9 us (34%)
  starting transfers between devices  20.5 us (30%)
  Pallas kernels  20.3 us (30%)
  local copies, waits for them, and re-layouts  2.26 us (3%)
  between operations  0.81 us (1%)
    ppermute x8, waiting for transfers between devices, swap(): return lax.ppermute(x, axis, [(i, i ^ by) for i in range(count)])  19.1 us
    ppermute x8, starting transfers between devices, swap(): return lax.ppermute(x, axis, [(i, i ^ by) for i in range(count)])  14 us
    ppermute x3, starting transfers between devices, level_route(): return lax.ppermute(x, 'seq', pairs)  6.45 us
    pallas_call x1, Pallas kernels, local(): pl.pallas_call(within_kernel, grid=(blocks, heads // 2), in_specs=[wide,...  5.41 us
    pallas_call x1, Pallas kernels, local(): pl.pallas_call(functools.partial(local_kernel, blocks, heads), in_specs=[...  4.79 us
    pallas_call x2, Pallas kernels, states_call(): pl.pallas_call(kernel, grid_spec=pltpu.PrefetchScalarGridSpec(num_scalar_...  4.55 us
    ppermute x3, waiting for transfers between devices, level_route(): return lax.ppermute(x, 'seq', pairs)  3.72 us
    unnamed x22, local copies, waits for them, and re-layouts  2.23 us
  transfers between devices with their start and end apart: 11, of which 8 were waited for; matrix products, arithmetic and copies ran while one was open for 0% of the time, Pallas kernels for 14%

profile of v2, /device:TPU:0, one launch (start us, length us, event | category | flops | bytes accessed | tf_op | source)
XLA Modules:
  0.0 66.9 jit_solution(16450316305305769866)
XLA Ops:
  0.7 4.8 %shard_map.111 = (f32[2,256,256]{2,1,0:T(8,128)}, f32[2,256,256]{2,1,0:T(8,128)}, f32[2,128,256]{2,1,0:T(8,128)}, f32[2,128,256]{2,1,0:T(8,128)}) custom-call(s32[16]{0:T(128)} %regimes.9, s32[16]{0:T(128)} %documents.5, f32[4]{0:T(128)} %gammas.7, bf16[32,256,256]{2,1,0:T(8,128)(2,1)} %rest_1_.3, bf16[512,1024]{1,0:T(8,128)(2,1)} %q.1, ...), custom_call_target="tpu_custom_call" | custom-call | tf_op jit(solution)/shard_map/pallas_call | solution.py:367
  5.5 3.0 %collective-permute-start = (f32[2,128,256]{2,1,0:T(8,128)}, f32[2,128,256]{2,1,0:T(8,128)S(1)}, u32[]{:S(2)}, u32[]{:S(2)}) collective-permute-start(f32[2,128,256]{2,1,0:T(8,128)} %get-tuple-element.34), channel_id=1, source_target_pairs={{0,4},{4,0},{8,12},{12,8},{16,20},{20,16},{24,28},{28,24},{1,5},{5... | collective-permute-start | bytes 786440 | tf_op jit(solution)/shard_map/ppermute | solution.py:312
  8.5 0.1 pad_add_fusion.pos
  8.5 2.2 %copy-done = bf16[32,256,256]{2,1,0:T(8,128)(2,1)S(1)} copy-done((bf16[32,256,256]{2,1,0:T(8,128)(2,1)S(1)}, bf16[32,256,256]{2,1,0:T(8,128)(2,1)}, u32[]{:S(2)}) %copy-start) | copy-done | bytes 4194328
  10.7 1.3 %shard_map.112 = (bf16[2,2,256,256]{3,2,1,0:T(8,128)(2,1)S(1)}, bf16[1,2,2,256,256]{4,3,2,1,0:T(8,128)(2,1)S(1)}) custom-call(s32[16]{0:T(128)S(1)} %copy-done.8, s32[16]{0:T(128)S(1)} %copy-done.10, s32[2]{0:T(128)S(1)} %pad_add_fusion.pos, bf16[32,256,256]{2,1,0:T(8,128)(2,1)S(1)} %copy-done), custom_call_target="tpu_custom_call" | custom-call | tf_op jit(solution)/shard_map/pallas_call | solution.py:393
  12.0 2.9 %collective-permute-done.arrived = f32[2,128,256]{2,1,0:T(8,128)S(1)} collective-permute-done((f32[2,128,256]{2,1,0:T(8,128)}, f32[2,128,256]{2,1,0:T(8,128)S(1)}, u32[]{:S(2)}, u32[]{:S(2)}) %collective-permute-start) | collective-permute-done | bytes 262176 | tf_op jit(solution)/shard_map/ppermute | solution.py:312
  15.0 0.9 %shard_map.113 = (f32[128,256]{1,0:T(8,128)S(1)}, f32[128,256]{1,0:T(8,128)S(1)}, f32[128,256]{1,0:T(8,128)S(1)}) custom-call(s32[2]{0:T(128)S(1)} %pad_add_fusion.pos, f32[4]{0:T(128)S(1)} %copy-done.9, f32[2,128,256]{2,1,0:T(8,128)S(1)} %copy-done.3, f32[2,128,256]{2,1,0:T(8,128)S(1)} %collective-permute-done.arrived, ...), custom_call_target="tpu_custom_call" | custom-call | tf_op jit(solution)/shard_map/pallas_call | solution.py:401
  15.9 2.9 %collective-permute-start.1 = (f32[128,256]{1,0:T(8,128)S(1)}, f32[128,256]{1,0:T(8,128)S(1)}, u32[]{:S(2)}, u32[]{:S(2)}) collective-permute-start(f32[128,256]{1,0:T(8,128)S(1)} %get-tuple-element.36), channel_id=1, source_target_pairs={{0,16},{16,0},{4,20},{20,4},{8,24},{24,8},{12,28},{28,12},{1,17},{... | collective-permute-start | bytes 393224 | tf_op jit(solution)/shard_map/ppermute | solution.py:323
  18.8 0.7 collective-permute-start.2
  19.5 2.9 %collective-permute-start.3 = (f32[128,256]{1,0:T(8,128)S(1)}, f32[128,256]{1,0:T(8,128)S(1)}, u32[]{:S(2)}, u32[]{:S(2)}) collective-permute-start(f32[128,256]{1,0:T(8,128)S(1)} %get-tuple-element.38), channel_id=1, source_target_pairs={{0,8},{8,0},{4,12},{12,4},{16,24},{24,16},{20,28},{28,20},{1,9},{9... | collective-permute-start | bytes 393224 | tf_op jit(solution)/shard_map/ppermute | solution.py:323
  22.4 3.1 %collective-permute-done.1.rest_0_ = f32[128,256]{1,0:T(8,128)S(1)} collective-permute-done((f32[128,256]{1,0:T(8,128)S(1)}, f32[128,256]{1,0:T(8,128)S(1)}, u32[]{:S(2)}, u32[]{:S(2)}) %collective-permute-start.1) | collective-permute-done | bytes 131104 | tf_op jit(solution)/shard_map/ppermute | solution.py:323
  25.4 0.6 collective-permute-done.3.rest_2_
  26.1 1.2 %shard_map.114 = (f32[2,128,256]{2,1,0:T(8,128)S(1)}, f32[2,128,256]{2,1,0:T(8,128)S(1)}) custom-call(s32[2]{0:T(128)S(1)} %pad_add_fusion.pos, f32[4]{0:T(128)S(1)} %copy-done.9, f32[2,128,256]{2,1,0:T(8,128)S(1)} %copy-done.3, f32[2,128,256]{2,1,0:T(8,128)S(1)} %collective-permute-done.arrived, bf16[2,2,256,256]{3,2,1,0:T(8,128)(2,1)S(1)} %get-tuple-element.35.device_maps, ...), custom_call_target="tpu_custom_call" | custom-call | tf_op jit(solution)/shard_map/pallas_call | solution.py:410
  27.3 1.5 %collective-permute-start.4 = (f32[2,128,256]{2,1,0:T(8,128)S(1)}, f32[2,128,256]{2,1,0:T(8,128)S(1)}, u32[]{:S(2)}, u32[]{:S(2)}) collective-permute-start(f32[2,128,256]{2,1,0:T(8,128)S(1)} %get-tuple-element.41), channel_id=1, source_target_pairs={{0,4},{4,0},{8,12},{12,8},{16,20},{20,16},{24,28},{28,24},{1,5},{5... | collective-permute-start | bytes 786440 | tf_op jit(solution)/shard_map/ppermute | solution.py:312
  28.8 4.9 %collective-permute-done.4.arrived = f32[2,128,256]{2,1,0:T(8,128)S(1)} collective-permute-done((f32[2,128,256]{2,1,0:T(8,128)S(1)}, f32[2,128,256]{2,1,0:T(8,128)S(1)}, u32[]{:S(2)}, u32[]{:S(2)}) %collective-permute-start.4) | collective-permute-done | bytes 262176 | tf_op jit(solution)/shard_map/ppermute | solution.py:312
  33.7 2.3 %shard_map.115 = (f32[2,2,64,256]{3,2,1,0:T(8,128)S(1)}, f32[2,2,64,256]{3,2,1,0:T(8,128)S(1)}) custom-call(s32[16]{0:T(128)S(1)} %copy-done.8, s32[16]{0:T(128)S(1)} %copy-done.10, s32[2]{0:T(128)S(1)} %pad_add_fusion.pos, f32[4]{0:T(128)S(1)} %copy-done.9, f32[2,128,256]{2,1,0:T(8,128)S(1)} %get-tuple-element.46.own, ...), custom_call_target="tpu_custom_call" | custom-call | tf_op jit(solution)/shard_map/pallas_call | solution.py:425
  36.1 0.1 collective-permute-start.5
  36.2 1.5 %collective-permute-done.5 = f32[2,2,64,256]{3,2,0,1:T(8,128)S(1)} collective-permute-done((f32[2,2,64,256]{3,2,0,1:T(8,128)S(1)}, f32[2,2,64,256]{3,2,0,1:T(8,128)S(1)}, u32[]{:S(2)}, u32[]{:S(2)}) %collective-permute-start.5) | collective-permute-done | bytes 262176 | tf_op jit(solution)/shard_map/ppermute | solution.py:312
  37.7 1.5 %collective-permute-start.6 = (f32[2,1,64,256]{3,2,0,1:T(8,128)S(1)}, f32[2,1,64,256]{3,2,0,1:T(8,128)S(1)}, u32[]{:S(2)}, u32[]{:S(2)}) collective-permute-start(f32[2,1,64,256]{3,2,0,1:T(8,128)S(1)} %constant_dynamic-slice_fusion), channel_id=1, source_target_pairs={{0,2},{1,3},{2,0},{3,1},{4,6},{5,7},{6,4},{7,5},{8,10},{9,11},{10,... | collective-permute-start | bytes 393224 | tf_op jit(solution)/shard_map/ppermute | solution.py:312
  39.3 4.1 %collective-permute-done.6 = f32[2,1,64,256]{3,2,0,1:T(8,128)S(1)} collective-permute-done((f32[2,1,64,256]{3,2,0,1:T(8,128)S(1)}, f32[2,1,64,256]{3,2,0,1:T(8,128)S(1)}, u32[]{:S(2)}, u32[]{:S(2)}) %collective-permute-start.6) | collective-permute-done | bytes 131104 | tf_op jit(solution)/shard_map/ppermute | solution.py:312
  43.4 3.0 %collective-permute-start.7 = (f32[2,64,256]{2,1,0:T(8,128)S(1)}, f32[2,64,256]{2,1,0:T(8,128)S(1)}, u32[]{:S(2)}, u32[]{:S(2)}) collective-permute-start(f32[2,64,256]{2,1,0:T(8,128)S(1)} %add_bitcast_fusion.rest_0_), channel_id=1, source_target_pairs={{0,8},{4,12},{8,0},{12,4},{16,24},{20,28},{24,16},{28,20},{1,9},{5... | collective-permute-start | bytes 393224 | tf_op jit(solution)/shard_map/ppermute | solution.py:312
  46.3 2.0 %collective-permute-start.8 = (f32[2,64,256]{2,1,0:T(8,128)S(1)}, f32[2,64,256]{2,1,0:T(8,128)S(1)}, u32[]{:S(2)}, u32[]{:S(2)}) collective-permute-start(f32[2,64,256]{2,1,0:T(8,128)S(1)} %add_bitcast_fusion.rest_0_), channel_id=1, source_target_pairs={{0,16},{4,20},{8,24},{12,28},{16,0},{20,4},{24,8},{28,12},{1,17},{... | collective-permute-start | bytes 393224 | tf_op jit(solution)/shard_map/ppermute | solution.py:312
  48.3 1.4 %collective-permute-start.9 = (f32[2,64,256]{2,1,0:T(8,128)S(1)}, f32[2,64,256]{2,1,0:T(8,128)S(1)}, u32[]{:S(2)}, u32[]{:S(2)}) collective-permute-start(f32[2,64,256]{2,1,0:T(8,128)S(1)} %add_bitcast_fusion.rest_0_), channel_id=1, source_target_pairs={{0,24},{4,28},{8,16},{12,20},{16,8},{20,12},{24,0},{28,4},{1,25},{... | collective-permute-start | bytes 393224 | tf_op jit(solution)/shard_map/ppermute | solution.py:312
  49.7 0.1 pad_add_fusion.1.sources
  49.8 2.2 %shard_map.116 = (bf16[2,256,256]{2,1,0:T(8,128)(2,1)S(1)}, bf16[2,256,256]{2,1,0:T(8,128)(2,1)S(1)}) custom-call(s32[16]{0:T(128)S(1)} %copy-done.8, s32[16]{0:T(128)S(1)} %copy-done.10, s32[2]{0:T(128)S(1)} %pad_add_fusion.pos, f32[4]{0:T(128)S(1)} %copy-done.9, f32[2,128,256]{2,1,0:T(8,128)S(1)} %get-tuple-element.46.own, ...), custom_call_target="tpu_custom_call" | custom-call | tf_op jit(solution)/shard_map/pallas_call | solution.py:425
  52.1 5.4 %shard_map.117 = (bf16[512,1024]{1,0:T(8,128)(2,1)}, bf16[512,1024]{1,0:T(8,128)(2,1)}, bf16[512,256]{1,0:T(8,128)(2,1)}) custom-call(bf16[512,1024]{1,0:T(8,128)(2,1)S(1)} %copy-done.4, bf16[512,1024]{1,0:T(8,128)(2,1)S(1)} %copy-done.5, bf16[512,256]{1,0:T(8,128)(2,1)S(1)} %copy-done.6, bf16[512,256]{1,0:T(8,128)(2,1)S(1)} %copy-done.7, ...), custom_call_target="tpu_custom_call" | custom-call | flops 1342177280 | bytes 6291456 | tf_op jit(solution)/shard_map/pallas_call | solution.py:467
  57.5 1.5 %collective-permute-done.8.rest_2_ = f32[2,64,256]{2,1,0:T(8,128)S(1)} collective-permute-done((f32[2,64,256]{2,1,0:T(8,128)S(1)}, f32[2,64,256]{2,1,0:T(8,128)S(1)}, u32[]{:S(2)}, u32[]{:S(2)}) %collective-permute-start.8) | collective-permute-done | bytes 131104 | tf_op jit(solution)/shard_map/ppermute | solution.py:312
  59.0 0.7 %shard_map.119 = f32[4,64,256]{2,1,0:T(8,128)S(1)} custom-call(s32[16]{0:T(128)S(1)} %copy-done.8, s32[1]{0:T(128)} %bitcast.7.base, s32[4]{0:T(128)S(1)} %pad_add_fusion.1.sources, f32[2,64,256]{2,1,0:T(8,128)S(1)} %add_bitcast_fusion.rest_0_, f32[2,64,256]{2,1,0:T(8,128)S(1)} %collective-permute-done.7.rest_1_, ...), custom_call_target="tpu_custom_call" | custom-call | tf_op jit(solution)/shard_map/pallas_call | solution.py:489
  59.7 1.5 %collective-permute-start.10 = (f32[4,64,256]{2,1,0:T(8,128)S(1)}, f32[4,64,256]{2,1,0:T(8,128)S(1)}, u32[]{:S(2)}, u32[]{:S(2)}) collective-permute-start(f32[4,64,256]{2,1,0:T(8,128)S(1)} %shard_map.119), channel_id=1, source_target_pairs={{0,4},{4,0},{8,12},{12,8},{16,20},{20,16},{24,28},{28,24},{1,5},{5... | collective-permute-start | bytes 786440 | tf_op jit(solution)/shard_map/ppermute | solution.py:312
  61.2 0.7 %shard_map.118.a = f32[4,64,256]{2,1,0:T(8,128)S(1)} custom-call(s32[16]{0:T(128)S(1)} %copy-done.8, s32[1]{0:T(128)} %bitcast.3.base, s32[4]{0:T(128)S(1)} %pad_add_fusion.1.sources, f32[2,64,256]{2,1,0:T(8,128)S(1)} %add_bitcast_fusion.rest_0_, f32[2,64,256]{2,1,0:T(8,128)S(1)} %collective-permute-done.7.rest_1_, ...), custom_call_target="tpu_custom_call" | custom-call | tf_op jit(solution)/shard_map/pallas_call | solution.py:489
  61.9 4.2 %collective-permute-done.10.b = f32[4,64,256]{2,1,0:T(8,128)S(1)} collective-permute-done((f32[4,64,256]{2,1,0:T(8,128)S(1)}, f32[4,64,256]{2,1,0:T(8,128)S(1)}, u32[]{:S(2)}, u32[]{:S(2)}) %collective-permute-start.10) | collective-permute-done | bytes 262176 | tf_op jit(solution)/shard_map/ppermute | solution.py:312
  66.1 0.7 %shard_map.120 = f32[4,64,256]{2,1,0:T(8,128)} custom-call(f32[4,64,256]{2,1,0:T(8,128)S(1)} %shard_map.118.a, f32[4,64,256]{2,1,0:T(8,128)S(1)} %collective-permute-done.10.b), custom_call_target="tpu_custom_call" | custom-call | tf_op jit(solution)/shard_map/pallas_call | solution.py:498
  (28 shorter events, 0.1 us)
Async XLA Ops:
  0.6 7.9 %copy-start.8 = (s32[16]{0:T(128)S(1)}, s32[16]{0:T(128)}, u32[]{:S(2)}) copy-start(s32[16]{0:T(128)} %regimes.9) | copy-start | bytes 196
  0.6 7.9 %copy-start.10 = (s32[16]{0:T(128)S(1)}, s32[16]{0:T(128)}, u32[]{:S(2)}) copy-start(s32[16]{0:T(128)} %documents.5) | copy-start | bytes 196
  0.7 14.3 %copy-start.9 = (f32[4]{0:T(128)S(1)}, f32[4]{0:T(128)}, u32[]{:S(2)}) copy-start(f32[4]{0:T(128)} %gammas.7) | copy-start | bytes 52
  5.5 9.5 %collective-permute-start = (f32[2,128,256]{2,1,0:T(8,128)}, f32[2,128,256]{2,1,0:T(8,128)S(1)}, u32[]{:S(2)}, u32[]{:S(2)}) collective-permute-start(f32[2,128,256]{2,1,0:T(8,128)} %get-tuple-element.34), channel_id=1, source_target_pairs={{0,4},{4,0},{8,12},{12,8},{16,20},{20,16},{24,28},{28,24},{1,5},{5... | collective-permute-start | bytes 786440 | tf_op jit(solution)/shard_map/ppermute | solution.py:312
  8.5 2.2 %copy-start = (bf16[32,256,256]{2,1,0:T(8,128)(2,1)S(1)}, bf16[32,256,256]{2,1,0:T(8,128)(2,1)}, u32[]{:S(2)}) copy-start(bf16[32,256,256]{2,1,0:T(8,128)(2,1)} %rest_1_.3) | copy-start | bytes 12582916
  10.7 4.2 %copy-start.3 = (f32[2,128,256]{2,1,0:T(8,128)S(1)}, f32[2,128,256]{2,1,0:T(8,128)}, u32[]{:S(2)}) copy-start(f32[2,128,256]{2,1,0:T(8,128)} %get-tuple-element.33.held) | copy-start | bytes 786436
  10.7 23.0 %copy-start.1 = (f32[2,256,256]{2,1,0:T(8,128)S(1)}, f32[2,256,256]{2,1,0:T(8,128)}, u32[]{:S(2)}) copy-start(f32[2,256,256]{2,1,0:T(8,128)} %get-tuple-element.48.update) | copy-start | bytes 1572868
  10.7 23.0 %copy-start.2 = (f32[2,256,256]{2,1,0:T(8,128)S(1)}, f32[2,256,256]{2,1,0:T(8,128)}, u32[]{:S(2)}) copy-start(f32[2,256,256]{2,1,0:T(8,128)} %get-tuple-element.49.source) | copy-start | bytes 1572868
  15.9 9.6 %collective-permute-start.1 = (f32[128,256]{1,0:T(8,128)S(1)}, f32[128,256]{1,0:T(8,128)S(1)}, u32[]{:S(2)}, u32[]{:S(2)}) collective-permute-start(f32[128,256]{1,0:T(8,128)S(1)} %get-tuple-element.36), channel_id=1, source_target_pairs={{0,16},{16,0},{4,20},{20,4},{8,24},{24,8},{12,28},{28,12},{1,17},{... | collective-permute-start | bytes 393224 | tf_op jit(solution)/shard_map/ppermute | solution.py:323
  18.8 6.7 %collective-permute-start.2 = (f32[128,256]{1,0:T(8,128)S(1)}, f32[128,256]{1,0:T(8,128)S(1)}, u32[]{:S(2)}, u32[]{:S(2)}) collective-permute-start(f32[128,256]{1,0:T(8,128)S(1)} %get-tuple-element.37), channel_id=1, source_target_pairs={{8,16},{16,8},{12,20},{20,12},{9,17},{17,9},{13,21},{21,13},{10,18... | collective-permute-start | bytes 393224 | tf_op jit(solution)/shard_map/ppermute | solution.py:323
  19.5 6.6 %collective-permute-start.3 = (f32[128,256]{1,0:T(8,128)S(1)}, f32[128,256]{1,0:T(8,128)S(1)}, u32[]{:S(2)}, u32[]{:S(2)}) collective-permute-start(f32[128,256]{1,0:T(8,128)S(1)} %get-tuple-element.38), channel_id=1, source_target_pairs={{0,8},{8,0},{4,12},{12,4},{16,24},{24,16},{20,28},{28,20},{1,9},{9... | collective-permute-start | bytes 393224 | tf_op jit(solution)/shard_map/ppermute | solution.py:323
  27.3 6.4 %collective-permute-start.4 = (f32[2,128,256]{2,1,0:T(8,128)S(1)}, f32[2,128,256]{2,1,0:T(8,128)S(1)}, u32[]{:S(2)}, u32[]{:S(2)}) collective-permute-start(f32[2,128,256]{2,1,0:T(8,128)S(1)} %get-tuple-element.41), channel_id=1, source_target_pairs={{0,4},{4,0},{8,12},{12,8},{16,20},{20,16},{24,28},{28,24},{1,5},{5... | collective-permute-start | bytes 786440 | tf_op jit(solution)/shard_map/ppermute | solution.py:312
  36.1 1.6 %collective-permute-start.5 = (f32[2,2,64,256]{3,2,0,1:T(8,128)S(1)}, f32[2,2,64,256]{3,2,0,1:T(8,128)S(1)}, u32[]{:S(2)}, u32[]{:S(2)}) collective-permute-start(f32[2,2,64,256]{3,2,0,1:T(8,128)S(1)} %copy.12), channel_id=1, source_target_pairs={{0,1},{1,0},{2,3},{3,2},{4,5},{5,4},{6,7},{7,6},{8,9},{9,8},{10,11... | collective-permute-start | bytes 786440 | tf_op jit(solution)/shard_map/ppermute | solution.py:312
  37.7 5.6 %collective-permute-start.6 = (f32[2,1,64,256]{3,2,0,1:T(8,128)S(1)}, f32[2,1,64,256]{3,2,0,1:T(8,128)S(1)}, u32[]{:S(2)}, u32[]{:S(2)}) collective-permute-start(f32[2,1,64,256]{3,2,0,1:T(8,128)S(1)} %constant_dynamic-slice_fusion), channel_id=1, source_target_pairs={{0,2},{1,3},{2,0},{3,1},{4,6},{5,7},{6,4},{7,5},{8,10},{9,11},{10,... | collective-permute-start | bytes 393224 | tf_op jit(solution)/shard_map/ppermute | solution.py:312
  43.4 14.1 %collective-permute-start.7 = (f32[2,64,256]{2,1,0:T(8,128)S(1)}, f32[2,64,256]{2,1,0:T(8,128)S(1)}, u32[]{:S(2)}, u32[]{:S(2)}) collective-permute-start(f32[2,64,256]{2,1,0:T(8,128)S(1)} %add_bitcast_fusion.rest_0_), channel_id=1, source_target_pairs={{0,8},{4,12},{8,0},{12,4},{16,24},{20,28},{24,16},{28,20},{1,9},{5... | collective-permute-start | bytes 393224 | tf_op jit(solution)/shard_map/ppermute | solution.py:312
  46.3 12.6 %collective-permute-start.8 = (f32[2,64,256]{2,1,0:T(8,128)S(1)}, f32[2,64,256]{2,1,0:T(8,128)S(1)}, u32[]{:S(2)}, u32[]{:S(2)}) collective-permute-start(f32[2,64,256]{2,1,0:T(8,128)S(1)} %add_bitcast_fusion.rest_0_), channel_id=1, source_target_pairs={{0,16},{4,20},{8,24},{12,28},{16,0},{20,4},{24,8},{28,12},{1,17},{... | collective-permute-start | bytes 393224 | tf_op jit(solution)/shard_map/ppermute | solution.py:312
  48.3 10.6 %collective-permute-start.9 = (f32[2,64,256]{2,1,0:T(8,128)S(1)}, f32[2,64,256]{2,1,0:T(8,128)S(1)}, u32[]{:S(2)}, u32[]{:S(2)}) collective-permute-start(f32[2,64,256]{2,1,0:T(8,128)S(1)} %add_bitcast_fusion.rest_0_), channel_id=1, source_target_pairs={{0,24},{4,28},{8,16},{12,20},{16,8},{20,12},{24,0},{28,4},{1,25},{... | collective-permute-start | bytes 393224 | tf_op jit(solution)/shard_map/ppermute | solution.py:312
  49.8 2.2 %copy-start.4 = (bf16[512,1024]{1,0:T(8,128)(2,1)S(1)}, bf16[512,1024]{1,0:T(8,128)(2,1)}, u32[]{:S(2)}) copy-start(bf16[512,1024]{1,0:T(8,128)(2,1)} %q.1) | copy-start | bytes 3145732
  49.8 2.2 %copy-start.5 = (bf16[512,1024]{1,0:T(8,128)(2,1)S(1)}, bf16[512,1024]{1,0:T(8,128)(2,1)}, u32[]{:S(2)}) copy-start(bf16[512,1024]{1,0:T(8,128)(2,1)} %k.1) | copy-start | bytes 3145732
  49.8 2.3 %copy-start.6 = (bf16[512,256]{1,0:T(8,128)(2,1)S(1)}, bf16[512,256]{1,0:T(8,128)(2,1)}, u32[]{:S(2)}) copy-start(bf16[512,256]{1,0:T(8,128)(2,1)} %v.1) | copy-start | bytes 786436
  49.8 2.3 %copy-start.7 = (bf16[512,256]{1,0:T(8,128)(2,1)S(1)}, bf16[512,256]{1,0:T(8,128)(2,1)}, u32[]{:S(2)}) copy-start(bf16[512,256]{1,0:T(8,128)(2,1)} %dy.1) | copy-start | bytes 786436
  59.7 6.4 %collective-permute-start.10 = (f32[4,64,256]{2,1,0:T(8,128)S(1)}, f32[4,64,256]{2,1,0:T(8,128)S(1)}, u32[]{:S(2)}, u32[]{:S(2)}) collective-permute-start(f32[4,64,256]{2,1,0:T(8,128)S(1)} %shard_map.119), channel_id=1, source_target_pairs={{0,4},{4,0},{8,12},{12,8},{16,20},{20,16},{24,28},{28,24},{1,5},{5... | collective-permute-start | bytes 786440 | tf_op jit(solution)/shard_map/ppermute | solution.py:312

commit v3 on v2

--- a/solution.py
+++ b/solution.py
@@ -20,7 +20,7 @@
 VMEM = pl.BlockSpec(memory_space=pltpu.VMEM)
 SMEM = pl.BlockSpec(memory_space=pltpu.SMEM)
 HBM = pl.BlockSpec(memory_space=pltpu.HBM)
-PARAMS = pltpu.CompilerParams(vmem_limit_bytes=48 << 20)
+PARAMS = pltpu.CompilerParams(vmem_limit_bytes=32 << 20)
 
 
 def dot(a, b, dims):
@@ -60,8 +60,8 @@
 
 def local_kernel(
     blocks, heads, regimes_hbm, documents_hbm, gammas_hbm, transitions, q_hbm, k_hbm, v_hbm, dy_hbm,
-    update, source, sent, held,
-    regimes, documents, gammas, mats, q, k, v, dy, small_sems, mat_sems, row_sems, wide_sems,
+    update, source, sent, held, mats,
+    q, k, v, dy, regimes, documents, gammas, small_sems, mat_sems, row_sems, wide_sems,
 ):
     seq = lax.axis_index("seq")
     half = heads * HEAD_DIM // 2
@@ -229,21 +229,20 @@
     for c in range(blocks):
         befores.append(halves(before))
         high, low = befores[-1]
-        entry = (kept[c] * decay) * (dot(high, mats[c][0], NT) + dot(low, mats[c][0], NT))
+        entry = (kept[c] * decay) * (dot(high, mats[c], NT) + dot(low, mats[c], NT))
         entries.append(entry)
         before = entry + update[c]
     for c in reversed(range(blocks)):
         leaves[c] = carried
         totals[c] = source[c] + carried
         if c > 0:
-            carried = (kept[c] * decay) * dot_exact(totals[c], mats[c][0], NN)
+            carried = (kept[c] * decay) * dot_exact(totals[c], mats[c], NN)
     return befores, entries, leaves, totals
 
 
 def terms_kernel(
-    blocks, heads, ways, regimes, documents, pos, gammas, own, arrived, update, source, *rest
+    blocks, heads, ways, documents, pos, gammas, own, arrived, update, source, mats, held, sent, term
 ):
-    mats, (held, sent, term) = rest[:blocks], rest[blocks:]
     seq, head = pos[0], pos[1]
     decay = decay_column(gammas, 0, heads, 1)
     kept = [kept_at(documents, seq * blocks + c) for c in range(blocks)]
@@ -255,14 +254,13 @@
     for c in range(blocks):
         term[...] = dot_pair(halves((kept[c] * decay) * totals[c]), befores[c], TN)
         for i in range(ways // 2):
-            held[c, i] = term[pl.ds(pl.multiple_of((2 * i + core) * part, part), part), :]
-            sent[c, i] = term[pl.ds(pl.multiple_of((2 * i + 1 - core) * part, part), part), :]
+            held[i, c] = term[pl.ds(pl.multiple_of((2 * i + core) * part, part), part), :]
+            sent[i, c] = term[pl.ds(pl.multiple_of((2 * i + 1 - core) * part, part), part), :]
 
 
 def rounded_kernel(
-    blocks, heads, regimes, documents, pos, gammas, own, arrived, update, source, *rest
+    blocks, heads, documents, pos, gammas, own, arrived, update, source, mats, entries, leaves
 ):
-    mats, (entries, leaves) = rest[:blocks], rest[blocks:]
     seq = pos[0]
     decay = decay_column(gammas, 0, heads, 1)
     kept = [kept_at(documents, seq * blocks + c) for c in range(blocks)]
@@ -290,21 +288,22 @@
     out[...] = a[...] + b[...]
 
 
-def within_kernel(q, k, v, dy, entry, leave, dq, dk, dv):
-    heads = v.shape[1] // HEAD_DIM
-    causal = lax.broadcasted_iota(jnp.int32, (BLOCK, BLOCK), 0) >= lax.broadcasted_iota(
-        jnp.int32, (BLOCK, BLOCK), 1
-    )
-    for h in range(heads):
+def within_kernel(q, k, v, dy, entries, leaves, *rest):
+    dq, dk, dv = rest[-3:]
+    row = lax.broadcasted_iota(jnp.int32, (BLOCK, BLOCK), 0)
+    column = lax.broadcasted_iota(jnp.int32, (BLOCK, BLOCK), 1)
+    lower, upper = row >= column, row <= column
+    for h in range(v.shape[1] // HEAD_DIM):
         wide = slice(h * STATE, (h + 1) * STATE)
         narrow = slice(h * HEAD_DIM, (h + 1) * HEAD_DIM)
         qh, kh, vh, gh = q[:, wide], k[:, wide], v[:, narrow], dy[:, narrow]
-        eh, lh = entry[0, narrow, :], leave[0, narrow, :]
-        probs = jnp.where(causal, dot(qh, kh, NT), 0.0).astype(BF16)
-        dscore = jnp.where(causal, dot(gh, vh, NT), 0.0).astype(BF16)
-        dq[:, wide] = (dot(gh, eh, NN) + dot(dscore, kh, NN)).astype(BF16)
-        dk[:, wide] = (dot(vh, lh, NN) + dot(dscore, qh, TN)).astype(BF16)
-        dv[:, narrow] = (dot(kh, lh, NT) + dot(probs, gh, TN)).astype(BF16)
+        entry, leave = entries[0, narrow, :], leaves[0, narrow, :]
+        probs_t = jnp.where(upper, dot(kh, qh, NT), 0.0).astype(BF16)
+        dscore = jnp.where(lower, dot(gh, vh, NT), 0.0).astype(BF16)
+        dscore_t = jnp.where(upper, dot(vh, gh, NT), 0.0).astype(BF16)
+        dq[:, wide] = (dot(gh, entry, NN) + dot(dscore, kh, NN)).astype(BF16)
+        dk[:, wide] = (dot(vh, leave, NN) + dot(dscore_t, qh, NN)).astype(BF16)
+        dv[:, narrow] = (dot(kh, leave, NT) + dot(probs_t, gh, NN)).astype(BF16)
 
 
 def swap(x, axis, by):
@@ -349,42 +348,36 @@
     def shape(*dims, dtype=F32):
         return jax.ShapeDtypeStruct(dims, dtype)
 
-    def whole(x):
-        return pl.BlockSpec(x.shape, lambda i, *_: (0,) * len(x.shape))
-
-    def own_mats():
-        return [
-            pl.BlockSpec(
-                (1, STATE, STATE),
-                lambda i, regimes, documents, pos, c=c: (regimes[pos[0] * blocks + c], 0, 0),
-            )
-            for c in range(blocks)
-        ]
-
     state_shape = shape(blocks, rows, STATE)
     half_shape = shape(2, half, STATE)
     outs = (state_shape, state_shape, half_shape, half_shape)
-    update, source, sent, held = pl.pallas_call(
+    def in_hbm(x):
+        return pltpu.with_memory_space_constraint(x, pltpu.HBM)
+
+    def in_vmem(x):
+        return pltpu.VMEM(x.shape, x.dtype)
+
+    mat_shape = shape(blocks, STATE, STATE, dtype=BF16)
+    inputs = (queries, keys, values, out_grad)
+    update, source, sent, held, mats = pl.pallas_call(
         functools.partial(local_kernel, blocks, heads),
         in_specs=[HBM] * 8,
-        out_specs=(VMEM,) * 4,
-        out_shape=outs,
-        scratch_shapes=[
+        out_specs=(VMEM,) * 5,
+        out_shape=tuple(in_vmem(x) for x in outs + (mat_shape,)),
+        scratch_shapes=[in_vmem(x) for x in inputs]
+        + [
             pltpu.SMEM(regimes.shape, jnp.int32),
             pltpu.SMEM(documents.shape, jnp.int32),
             pltpu.SMEM(gammas.shape, F32),
-            pltpu.VMEM((blocks, STATE, STATE), BF16),
-            pltpu.VMEM(queries.shape, BF16),
-            pltpu.VMEM(keys.shape, BF16),
-            pltpu.VMEM(values.shape, BF16),
-            pltpu.VMEM(out_grad.shape, BF16),
             pltpu.SemaphoreType.DMA((3,)),
             pltpu.SemaphoreType.DMA((blocks,)),
             pltpu.SemaphoreType.DMA((2, blocks)),
             pltpu.SemaphoreType.DMA((2, blocks, 2)),
         ],
-        compiler_params=pltpu.CompilerParams(vmem_limit_bytes=60 << 20),
-    )(regimes, documents, gammas, transitions, queries, keys, values, out_grad)
+        compiler_params=PARAMS,
+    )(
+        *[in_hbm(x) for x in (regimes, documents, gammas, transitions) + inputs]
+    )
 
     arrived = swap(sent, "seq", 1)
     map_shapes = (shape(2, 2, STATE, STATE, dtype=BF16),)
@@ -417,23 +410,19 @@
     arrived_entry = swap(sent_entry, "seq", 1)
 
     part = STATE // ways
-    part_shape = shape(blocks, ways // 2, part, STATE)
+    part_shape = shape(ways // 2, blocks, part, STATE)
     bf16_states = shape(blocks, rows, STATE, dtype=BF16)
-    states = (own, arrived_entry, update, source)
+    states = (own, arrived_entry, update, source, mats)
 
     def states_call(kernel, states, outs, scratch):
         return pl.pallas_call(
             kernel,
-            grid_spec=pltpu.PrefetchScalarGridSpec(
-                num_scalar_prefetch=3,
-                grid=(1,),
-                in_specs=[SMEM] + [whole(x) for x in states] + own_mats(),
-                out_specs=[whole(x) for x in outs],
-                scratch_shapes=scratch,
-            ),
+            in_specs=[SMEM] * 3 + [VMEM] * len(states),
+            out_specs=(VMEM,) * len(outs),
             out_shape=outs,
+            scratch_shapes=scratch,
             compiler_params=PARAMS,
-        )(regimes, documents, pos, gammas, *states, *[transitions] * blocks)
+        )(documents, pos, gammas, *states)
 
     held_term, sent_term = states_call(
         functools.partial(terms_kernel, blocks, heads, ways),
@@ -443,47 +432,52 @@
     )
 
     summed = held_term + swap(sent_term, "head", 1)
-    by = 2
-    while by < ways:
-        split = summed.reshape(blocks, -1, 2, part, STATE)
-        bit = lax.rem(lax.div(head, by), 2)
-        going = lax.dynamic_index_in_dim(split, 1 - bit, 2, keepdims=False)
-        staying = lax.dynamic_index_in_dim(split, bit, 2, keepdims=False)
-        summed = staying + swap(going, "head", by)
-        by *= 2
-    summed = summed.reshape(blocks, part, STATE)
-
-    pieces = [summed] + [swap(summed, "seq", 2 * by) for by in range(1, levels)]
-    sources = jnp.stack([seq ^ (2 * by) for by in range(levels)]).astype(jnp.int32)
-    owned = REGIMES // devices
-
     states, summed = lax.optimization_barrier((states, summed))
     entries, leaves = states_call(
         functools.partial(rounded_kernel, blocks, heads), states, (bf16_states, bf16_states), []
     )
-    wide = pl.BlockSpec((BLOCK, 2 * STATE), lambda c, h: (c, h))
-    narrow = pl.BlockSpec((BLOCK, 2 * HEAD_DIM), lambda c, h: (c, h))
-    states = pl.BlockSpec((1, 2 * HEAD_DIM, STATE), lambda c, h: (c, h, 0))
-    query_grad, key_grad, value_grad = pl.pallas_call(
-        within_kernel,
-        grid=(blocks, heads // 2),
-        in_specs=[wide, wide, narrow, narrow, states, states],
-        out_specs=[wide, wide, narrow],
-        out_shape=(
-            shape(*queries.shape, dtype=BF16),
-            shape(*keys.shape, dtype=BF16),
-            shape(*values.shape, dtype=BF16),
-        ),
-        compiler_params=PARAMS,
-        cost_estimate=pl.CostEstimate(
-            flops=blocks * heads * 10 * BLOCK * BLOCK * STATE,
-            bytes_accessed=6 << 20,
-            transcendentals=0,
-        ),
-    )(queries, keys, values, out_grad, entries, leaves)
-    pieces, query_grad, key_grad, value_grad = lax.optimization_barrier(
-        (pieces, query_grad, key_grad, value_grad)
-    )
+    by = 2
+    while by < ways:
+        split = summed.reshape(-1, 2, blocks, part, STATE)
+        bit = lax.rem(lax.div(head, by), 2)
+        going = lax.dynamic_index_in_dim(split, 1 - bit, 1, keepdims=False)
+        staying = lax.dynamic_index_in_dim(split, bit, 1, keepdims=False)
+        arrived_part = swap(going, "head", by)
+        arrived_part, entries, leaves = lax.optimization_barrier((arrived_part, entries, leaves))
+        summed = staying + arrived_part
+        by *= 2
+    summed = summed.reshape(blocks, part, STATE)
+    summed, entries, leaves = lax.optimization_barrier((summed, entries, leaves))
+
+    def output_call(c, entries, leaves, before):
+        wide = pl.BlockSpec((BLOCK, 2 * STATE), lambda h: (c, h))
+        narrow = pl.BlockSpec((BLOCK, 2 * HEAD_DIM), lambda h: (c, h))
+        state = pl.BlockSpec((1, 2 * HEAD_DIM, STATE), lambda h: (c, h, 0))
+        return pl.pallas_call(
+            within_kernel,
+            grid=(heads // 2,),
+            in_specs=[wide, wide, narrow, narrow, state, state] + [HBM] * len(before),
+            out_specs=[wide, wide, narrow],
+            out_shape=[shape(*x.shape, dtype=BF16) for x in inputs[:3]],
+            input_output_aliases={6 + i: i for i in range(len(before))},
+            compiler_params=PARAMS,
+            cost_estimate=pl.CostEstimate(
+                flops=20 * heads * BLOCK * BLOCK * STATE,
+                bytes_accessed=3 << 20,
+                transcendentals=0,
+            ),
+        )(*[in_hbm(x) for x in inputs], entries, leaves, *before)
+
+    pieces, sources, by = [summed], [seq], devices // 2
+    direct = [swap(summed, "seq", 1 << i) for i in range(1, by.bit_length())][::-1]
+    grads = output_call(0, entries, leaves, ())
+    direct, grads = lax.optimization_barrier((direct, grads))
+    while by > 1:
+        pieces += [direct[0]] + [swap(x, "seq", by) for x in pieces[1:]]
+        sources += [x ^ by for x in sources]
+        direct, by = direct[1:], by // 2
+    sources = jnp.stack(sources).astype(jnp.int32)
+    owned = REGIMES // devices
 
     def regime_sum(device):
         return pl.pallas_call(
@@ -494,15 +488,21 @@
             compiler_params=PARAMS,
         )(regimes, jnp.reshape(device * owned, (1,)).astype(jnp.int32), sources, *pieces)
 
-    arrived_sum = swap(regime_sum(seq ^ 1), "seq", 1)
+    sent_sum = regime_sum(seq ^ 1)
+    sent_sum, grads = lax.optimization_barrier((sent_sum, grads))
+    arrived_sum = swap(sent_sum, "seq", 1)
+    for c in range(1, blocks):
+        grads = output_call(c, entries, leaves, grads)
+    own_sum = regime_sum(seq)
+    arrived_sum, own_sum, grads = lax.optimization_barrier((arrived_sum, own_sum, grads))
     regime_grad = pl.pallas_call(
         add_kernel,
         in_specs=[VMEM, VMEM],
         out_specs=VMEM,
         out_shape=shape(owned, part, STATE),
         compiler_params=PARAMS,
-    )(regime_sum(seq), arrived_sum)
-    return query_grad, key_grad, value_grad, regime_grad
+    )(own_sum, arrived_sum)
+    return (*grads, regime_grad)
 
 
 def solution(mesh):

time: 67.5 us -> 64.8 us (0.960)
  waiting for transfers between devices: 22.9 us -> 20.9 us
  Pallas kernels: 20.3 us -> 19.3 us
  starting transfers between devices: 20.5 us -> 21.3 us
    ppermute x8, waiting for transfers between devices: 19.1 us -> 17.2 us  [swap(): return lax.ppermute(x, axis, [(i, i ^ by) for i in range(count)])]
    ppermute x8, starting transfers between devices: 14 us -> 14.8 us  [swap(): return lax.ppermute(x, axis, [(i, i ^ by) for i in range(count)])]
    pallas_call x1, Pallas kernels: 4.79 us -> 4.01 us  [local(): pl.pallas_call(functools.partial(local_kernel, blocks, heads), in_specs=[...]
    pallas_call x3 -> x4, Pallas kernels: 9.96 us -> 9.75 us  [the longest x2 7.37 us: output_call(): pl.pallas_call(within_kernel, grid=(heads // 2,), in_specs=[wide, wide, n...]
    unnamed x22 -> x8, local copies, waits for them, and re-layouts: 2.23 us -> 2.2 us
  transfers between devices with their start and end apart: 11 -> 11, of which waited for: 8 -> 9; matrix products, arithmetic and copies ran while one was open for 0% -> 0% of each run, Pallas kernels for 14% -> 16%
where the time goes in v3:
time: 64.8 us; the launch traced here: 64.6 us
  starting transfers between devices  21.3 us (33%)
  waiting for transfers between devices  20.9 us (32%)
  Pallas kernels  19.3 us (30%)
  local copies, waits for them, and re-layouts  2.22 us (3%)
  between operations  0.76 us (1%)
    ppermute x8, waiting for transfers between devices, swap(): return lax.ppermute(x, axis, [(i, i ^ by) for i in range(count)])  17.2 us
    ppermute x8, starting transfers between devices, swap(): return lax.ppermute(x, axis, [(i, i ^ by) for i in range(count)])  14.8 us
    pallas_call x2, Pallas kernels, output_call(): pl.pallas_call(within_kernel, grid=(heads // 2,), in_specs=[wide, wide, n...  7.37 us
    ppermute x3, starting transfers between devices, level_route(): return lax.ppermute(x, 'seq', pairs)  6.46 us
    pallas_call x1, Pallas kernels, local(): pl.pallas_call(functools.partial(local_kernel, blocks, heads), in_specs=[...  4.01 us
    ppermute x3, waiting for transfers between devices, level_route(): return lax.ppermute(x, 'seq', pairs)  3.73 us
    pallas_call x2, Pallas kernels, states_call(): pl.pallas_call(kernel, in_specs=[SMEM] * 3 + [VMEM] * len(states), out_sp...  2.37 us
    unnamed x8, local copies, waits for them, and re-layouts  2.2 us
  transfers between devices with their start and end apart: 11, of which 9 were waited for; matrix products, arithmetic and copies ran while one was open for 0% of the time, Pallas kernels for 16%

profile of v3, /device:TPU:0, one launch (start us, length us, event | category | flops | bytes accessed | tf_op | source)
XLA Modules:
  0.0 64.6 jit_solution(810830345529167126)
XLA Ops:
  0.7 4.0 %shard_map.111 = (f32[2,256,256]{2,1,0:T(8,128)S(1)}, f32[2,256,256]{2,1,0:T(8,128)S(1)}, f32[2,128,256]{2,1,0:T(8,128)S(1)}, f32[2,128,256]{2,1,0:T(8,128)S(1)}, bf16[2,256,256]{2,1,0:T(8,128)(2,1)S(1)}) custom-call(s32[16]{0:T(128)} %regimes.5, s32[16]{0:T(128)} %documents.5, f32[4]{0:T(128)} %gammas.7, bf16[32,256,256]{2,1,0:T(8,128)(2,1)} %transitions.3, ...), custom_call_target="tpu_custom_call" | custom-call | tf_op jit(solution)/shard_map/pallas_call | solution.py:362
  4.7 3.0 %collective-permute-start = (f32[2,128,256]{2,1,0:T(8,128)S(1)}, f32[2,128,256]{2,1,0:T(8,128)S(1)}, u32[]{:S(2)}, u32[]{:S(2)}) collective-permute-start(f32[2,128,256]{2,1,0:T(8,128)S(1)} %get-tuple-element.53), channel_id=1, source_target_pairs={{0,4},{4,0},{8,12},{12,8},{16,20},{20,16},{24,28},{28,24},{1,5},{5... | collective-permute-start | bytes 786440 | tf_op jit(solution)/shard_map/ppermute | solution.py:311
  7.8 2.2 %copy-done = bf16[32,256,256]{2,1,0:T(8,128)(2,1)S(1)} copy-done((bf16[32,256,256]{2,1,0:T(8,128)(2,1)S(1)}, bf16[32,256,256]{2,1,0:T(8,128)(2,1)}, u32[]{:S(2)}) %copy-start) | copy-done | bytes 4194328
  9.9 1.3 %shard_map.112 = (bf16[2,2,256,256]{3,2,1,0:T(8,128)(2,1)S(1)}, bf16[1,2,2,256,256]{4,3,2,1,0:T(8,128)(2,1)S(1)}) custom-call(s32[16]{0:T(128)S(1)} %copy-done.2, s32[16]{0:T(128)S(1)} %copy-done.3, s32[2]{0:T(128)S(1)} %pad_add_fusion.1.pos, bf16[32,256,256]{2,1,0:T(8,128)(2,1)S(1)} %copy-done), custom_call_target="tpu_custom_call" | custom-call | tf_op jit(solution)/shard_map/pallas_call | solution.py:386
  11.2 2.7 %collective-permute-done.arrived = f32[2,128,256]{2,1,0:T(8,128)S(1)} collective-permute-done((f32[2,128,256]{2,1,0:T(8,128)S(1)}, f32[2,128,256]{2,1,0:T(8,128)S(1)}, u32[]{:S(2)}, u32[]{:S(2)}) %collective-permute-start) | collective-permute-done | bytes 262176 | tf_op jit(solution)/shard_map/ppermute | solution.py:311
  14.0 0.9 %shard_map.113 = (f32[128,256]{1,0:T(8,128)S(1)}, f32[128,256]{1,0:T(8,128)S(1)}, f32[128,256]{1,0:T(8,128)S(1)}) custom-call(s32[2]{0:T(128)S(1)} %pad_add_fusion.1.pos, f32[4]{0:T(128)S(1)} %copy-done.1, f32[2,128,256]{2,1,0:T(8,128)S(1)} %get-tuple-element.52.held, f32[2,128,256]{2,1,0:T(8,128)S(1)} %collective-permute-done.arrived, ...), custom_call_target="tpu_custom_call" | custom-call | tf_op jit(solution)/shard_map/pallas_call | solution.py:394
  14.9 2.9 %collective-permute-start.1 = (f32[128,256]{1,0:T(8,128)S(1)}, f32[128,256]{1,0:T(8,128)S(1)}, u32[]{:S(2)}, u32[]{:S(2)}) collective-permute-start(f32[128,256]{1,0:T(8,128)S(1)} %get-tuple-element.55), channel_id=1, source_target_pairs={{0,16},{16,0},{4,20},{20,4},{8,24},{24,8},{12,28},{28,12},{1,17},{... | collective-permute-start | bytes 393224 | tf_op jit(solution)/shard_map/ppermute | solution.py:322
  17.8 0.7 %collective-permute-start.2 = (f32[128,256]{1,0:T(8,128)S(1)}, f32[128,256]{1,0:T(8,128)S(1)}, u32[]{:S(2)}, u32[]{:S(2)}) collective-permute-start(f32[128,256]{1,0:T(8,128)S(1)} %get-tuple-element.56), channel_id=1, source_target_pairs={{8,16},{16,8},{12,20},{20,12},{9,17},{17,9},{13,21},{21,13},{10,18... | collective-permute-start | bytes 393224 | tf_op jit(solution)/shard_map/ppermute | solution.py:322
  18.5 2.9 %collective-permute-start.3 = (f32[128,256]{1,0:T(8,128)S(1)}, f32[128,256]{1,0:T(8,128)S(1)}, u32[]{:S(2)}, u32[]{:S(2)}) collective-permute-start(f32[128,256]{1,0:T(8,128)S(1)} %get-tuple-element.57), channel_id=1, source_target_pairs={{0,8},{8,0},{4,12},{12,4},{16,24},{24,16},{20,28},{28,20},{1,9},{9... | collective-permute-start | bytes 393224 | tf_op jit(solution)/shard_map/ppermute | solution.py:322
  21.4 3.1 %collective-permute-done.1.rest_0_ = f32[128,256]{1,0:T(8,128)S(1)} collective-permute-done((f32[128,256]{1,0:T(8,128)S(1)}, f32[128,256]{1,0:T(8,128)S(1)}, u32[]{:S(2)}, u32[]{:S(2)}) %collective-permute-start.1) | collective-permute-done | bytes 131104 | tf_op jit(solution)/shard_map/ppermute | solution.py:322
  24.5 0.6 collective-permute-done.3.rest_2_
  25.1 1.2 %shard_map.114 = (f32[2,128,256]{2,1,0:T(8,128)S(1)}, f32[2,128,256]{2,1,0:T(8,128)S(1)}) custom-call(s32[2]{0:T(128)S(1)} %pad_add_fusion.1.pos, f32[4]{0:T(128)S(1)} %copy-done.1, f32[2,128,256]{2,1,0:T(8,128)S(1)} %get-tuple-element.52.held, f32[2,128,256]{2,1,0:T(8,128)S(1)} %collective-permute-done.arrived, ...), custom_call_target="tpu_custom_call" | custom-call | tf_op jit(solution)/shard_map/pallas_call | solution.py:403
  26.3 1.5 %collective-permute-start.4 = (f32[2,128,256]{2,1,0:T(8,128)S(1)}, f32[2,128,256]{2,1,0:T(8,128)S(1)}, u32[]{:S(2)}, u32[]{:S(2)}) collective-permute-start(f32[2,128,256]{2,1,0:T(8,128)S(1)} %get-tuple-element.60), channel_id=1, source_target_pairs={{0,4},{4,0},{8,12},{12,8},{16,20},{20,16},{24,28},{28,24},{1,5},{5... | collective-permute-start | bytes 786440 | tf_op jit(solution)/shard_map/ppermute | solution.py:311
  27.8 4.9 %collective-permute-done.4.arrived = f32[2,128,256]{2,1,0:T(8,128)S(1)} collective-permute-done((f32[2,128,256]{2,1,0:T(8,128)S(1)}, f32[2,128,256]{2,1,0:T(8,128)S(1)}, u32[]{:S(2)}, u32[]{:S(2)}) %collective-permute-start.4) | collective-permute-done | bytes 262176 | tf_op jit(solution)/shard_map/ppermute | solution.py:311
  32.7 1.4 %shard_map.115 = (f32[2,2,64,256]{3,2,1,0:T(8,128)S(1)}, f32[2,2,64,256]{3,2,1,0:T(8,128)S(1)}) custom-call(s32[16]{0:T(128)S(1)} %copy-done.3, s32[2]{0:T(128)S(1)} %pad_add_fusion.1.pos, f32[4]{0:T(128)S(1)} %copy-done.1, f32[2,128,256]{2,1,0:T(8,128)S(1)} %get-tuple-element.67.own, f32[2,128,256]{2,1,0:T(8,128)S(1)} %collective-permute-done.4.arrived, ...), custom_call_target="tpu_custom_call" | custom-call | tf_op jit(solution)/shard_map/pallas_call | solution.py:418
  34.2 1.5 %collective-permute-done.5 = f32[2,2,64,256]{3,2,1,0:T(8,128)S(1)} collective-permute-done((f32[2,2,64,256]{3,2,1,0:T(8,128)S(1)}, f32[2,2,64,256]{3,2,1,0:T(8,128)S(1)}, u32[]{:S(2)}, u32[]{:S(2)}) %collective-permute-start.5) | collective-permute-done | bytes 262176 | tf_op jit(solution)/shard_map/ppermute | solution.py:311
  35.7 1.5 %collective-permute-start.6 = (f32[1,2,64,256]{3,2,1,0:T(8,128)S(1)}, f32[1,2,64,256]{3,2,1,0:T(8,128)S(1)}, u32[]{:S(2)}, u32[]{:S(2)}) collective-permute-start(f32[1,2,64,256]{3,2,1,0:T(8,128)S(1)} %constant_dynamic-slice_fusion), channel_id=1, source_target_pairs={{0,2},{1,3},{2,0},{3,1},{4,6},{5,7},{6,4},{7,5},{8,10},{9,11},{10,... | collective-permute-start | bytes 393224 | tf_op jit(solution)/shard_map/ppermute | solution.py:311
  37.3 1.0 %shard_map.116 = (bf16[2,256,256]{2,1,0:T(8,128)(2,1)S(1)}, bf16[2,256,256]{2,1,0:T(8,128)(2,1)S(1)}) custom-call(s32[16]{0:T(128)S(1)} %copy-done.3, s32[2]{0:T(128)S(1)} %pad_add_fusion.1.pos, f32[4]{0:T(128)S(1)} %copy-done.1, f32[2,128,256]{2,1,0:T(8,128)S(1)} %get-tuple-element.67.own, f32[2,128,256]{2,1,0:T(8,128)S(1)} %collective-permute-done.4.arrived, ...), custom_call_target="tpu_custom_call" | custom-call | tf_op jit(solution)/shard_map/pallas_call | solution.py:418
  38.3 3.0 %collective-permute-done.6 = f32[1,2,64,256]{3,2,1,0:T(8,128)S(1)} collective-permute-done((f32[1,2,64,256]{3,2,1,0:T(8,128)S(1)}, f32[1,2,64,256]{3,2,1,0:T(8,128)S(1)}, u32[]{:S(2)}, u32[]{:S(2)}) %collective-permute-start.6) | collective-permute-done | bytes 131104 | tf_op jit(solution)/shard_map/ppermute | solution.py:311
  41.4 3.0 %collective-permute-start.8 = (f32[2,64,256]{2,1,0:T(8,128)S(1)}, f32[2,64,256]{2,1,0:T(8,128)S(1)}, u32[]{:S(2)}, u32[]{:S(2)}) collective-permute-start(f32[2,64,256]{2,1,0:T(8,128)S(1)} %add_bitcast_fusion.rest_0_), channel_id=1, source_target_pairs={{0,8},{4,12},{8,0},{12,4},{16,24},{20,28},{24,16},{28,20},{1,9},{5... | collective-permute-start | bytes 393224 | tf_op jit(solution)/shard_map/ppermute | solution.py:311
  44.3 2.0 %collective-permute-start.7 = (f32[2,64,256]{2,1,0:T(8,128)S(1)}, f32[2,64,256]{2,1,0:T(8,128)S(1)}, u32[]{:S(2)}, u32[]{:S(2)}) collective-permute-start(f32[2,64,256]{2,1,0:T(8,128)S(1)} %add_bitcast_fusion.rest_0_), channel_id=1, source_target_pairs={{0,16},{4,20},{8,24},{12,28},{16,0},{20,4},{24,8},{28,12},{1,17},{... | collective-permute-start | bytes 393224 | tf_op jit(solution)/shard_map/ppermute | solution.py:311
  46.3 3.7 %shard_map.117 = (bf16[512,1024]{1,0:T(8,128)(2,1)}, bf16[512,1024]{1,0:T(8,128)(2,1)}, bf16[512,256]{1,0:T(8,128)(2,1)}) custom-call(bf16[512,1024]{1,0:T(8,128)(2,1)} %q.3, bf16[512,1024]{1,0:T(8,128)(2,1)} %k.3, bf16[512,256]{1,0:T(8,128)(2,1)} %v.3, bf16[512,256]{1,0:T(8,128)(2,1)} %dy.3, bf16[2,256,256]{2,1,0:T(8,128)(2,1)S(1)} %get-tuple-element.78.entries, ...), custom_call_target="tpu_custom_call" | custom-call | flops 1342177280 | bytes 3145728 | tf_op jit(solution)/shard_map/pallas_call | solution.py:456
  50.0 1.6 %collective-permute-done.7.rest_1_ = f32[2,64,256]{2,1,0:T(8,128)S(1)} collective-permute-done((f32[2,64,256]{2,1,0:T(8,128)S(1)}, f32[2,64,256]{2,1,0:T(8,128)S(1)}, u32[]{:S(2)}, u32[]{:S(2)}) %collective-permute-start.7) | collective-permute-done | bytes 131104 | tf_op jit(solution)/shard_map/ppermute | solution.py:311
  51.6 2.2 %collective-permute-start.9 = (f32[2,64,256]{2,1,0:T(8,128)S(1)}, f32[2,64,256]{2,1,0:T(8,128)S(1)}, u32[]{:S(2)}, u32[]{:S(2)}) collective-permute-start(f32[2,64,256]{2,1,0:T(8,128)S(1)} %collective-permute-done.7.rest_1_), channel_id=1, source_target_pairs={{0,8},{4,12},{8,0},{12,4},{16,24},{20,28},{24,16},{28,20},{1,9},{5... | collective-permute-start | bytes 393224 | tf_op jit(solution)/shard_map/ppermute | solution.py:311
  53.8 0.1 pad_add_fusion.sources
  53.9 2.9 %collective-permute-done.9.rest_3_ = f32[2,64,256]{2,1,0:T(8,128)S(1)} collective-permute-done((f32[2,64,256]{2,1,0:T(8,128)S(1)}, f32[2,64,256]{2,1,0:T(8,128)S(1)}, u32[]{:S(2)}, u32[]{:S(2)}) %collective-permute-start.9) | collective-permute-done | bytes 131104 | tf_op jit(solution)/shard_map/ppermute | solution.py:311
  56.7 0.7 %shard_map.118 = f32[4,64,256]{2,1,0:T(8,128)S(1)} custom-call(s32[16]{0:T(128)S(1)} %copy-done.2, s32[1]{0:T(128)} %bitcast.base, s32[4]{0:T(128)S(1)} %pad_add_fusion.sources, f32[2,64,256]{2,1,0:T(8,128)S(1)} %add_bitcast_fusion.rest_0_, f32[2,64,256]{2,1,0:T(8,128)S(1)} %collective-permute-done.7.rest_1_, ...), custom_call_target="tpu_custom_call" | custom-call | tf_op jit(solution)/shard_map/pallas_call | solution.py:483
  57.4 1.6 %collective-permute-start.10 = (f32[4,64,256]{2,1,0:T(8,128)S(1)}, f32[4,64,256]{2,1,0:T(8,128)S(1)}, u32[]{:S(2)}, u32[]{:S(2)}) collective-permute-start(f32[4,64,256]{2,1,0:T(8,128)S(1)} %shard_map.118), channel_id=1, source_target_pairs={{0,4},{4,0},{8,12},{12,8},{16,20},{20,16},{24,28},{28,24},{1,5},{5... | collective-permute-start | bytes 786440 | tf_op jit(solution)/shard_map/ppermute | solution.py:311
  59.0 0.7 %shard_map.119.a = f32[4,64,256]{2,1,0:T(8,128)S(1)} custom-call(s32[16]{0:T(128)S(1)} %copy-done.2, s32[1]{0:T(128)} %bitcast.7.base, s32[4]{0:T(128)S(1)} %pad_add_fusion.sources, f32[2,64,256]{2,1,0:T(8,128)S(1)} %add_bitcast_fusion.rest_0_, f32[2,64,256]{2,1,0:T(8,128)S(1)} %collective-permute-done.7.rest_1_, ...), custom_call_target="tpu_custom_call" | custom-call | tf_op jit(solution)/shard_map/pallas_call | solution.py:483
  59.7 3.7 %shard_map.120 = (bf16[512,1024]{1,0:T(8,128)(2,1)}, bf16[512,1024]{1,0:T(8,128)(2,1)}, bf16[512,256]{1,0:T(8,128)(2,1)}) custom-call(bf16[512,1024]{1,0:T(8,128)(2,1)} %q.3, bf16[512,1024]{1,0:T(8,128)(2,1)} %k.3, bf16[512,256]{1,0:T(8,128)(2,1)} %v.3, bf16[512,256]{1,0:T(8,128)(2,1)} %dy.3, ...), custom_call_target="tpu_custom_call", output_to_operand_aliasing={{0}: (6, {}), {1}: (7, {}), {2}: (8, {})} | custom-call | flops 1342177280 | bytes 3145728 | tf_op jit(solution)/shard_map/pallas_call | solution.py:456
  63.4 0.5 collective-permute-done.10.b
  63.9 0.7 %shard_map.121 = f32[4,64,256]{2,1,0:T(8,128)} custom-call(f32[4,64,256]{2,1,0:T(8,128)S(1)} %shard_map.119.a, f32[4,64,256]{2,1,0:T(8,128)S(1)} %collective-permute-done.10.b), custom_call_target="tpu_custom_call" | custom-call | tf_op jit(solution)/shard_map/pallas_call | solution.py:498
  (14 shorter events, 0.2 us)
Async XLA Ops:
  0.6 13.4 %copy-start.1 = (f32[4]{0:T(128)S(1)}, f32[4]{0:T(128)}, u32[]{:S(2)}) copy-start(f32[4]{0:T(128)} %gammas.7) | copy-start | bytes 52
  0.6 7.1 %copy-start.3 = (s32[16]{0:T(128)S(1)}, s32[16]{0:T(128)}, u32[]{:S(2)}) copy-start(s32[16]{0:T(128)} %documents.5) | copy-start | bytes 196
  0.7 7.1 %copy-start.2 = (s32[16]{0:T(128)S(1)}, s32[16]{0:T(128)}, u32[]{:S(2)}) copy-start(s32[16]{0:T(128)} %regimes.5) | copy-start | bytes 196
  4.7 9.3 %collective-permute-start = (f32[2,128,256]{2,1,0:T(8,128)S(1)}, f32[2,128,256]{2,1,0:T(8,128)S(1)}, u32[]{:S(2)}, u32[]{:S(2)}) collective-permute-start(f32[2,128,256]{2,1,0:T(8,128)S(1)} %get-tuple-element.53), channel_id=1, source_target_pairs={{0,4},{4,0},{8,12},{12,8},{16,20},{20,16},{24,28},{28,24},{1,5},{5... | collective-permute-start | bytes 786440 | tf_op jit(solution)/shard_map/ppermute | solution.py:311
  7.8 2.2 %copy-start = (bf16[32,256,256]{2,1,0:T(8,128)(2,1)S(1)}, bf16[32,256,256]{2,1,0:T(8,128)(2,1)}, u32[]{:S(2)}) copy-start(bf16[32,256,256]{2,1,0:T(8,128)(2,1)} %transitions.3) | copy-start | bytes 12582916
  14.9 9.6 %collective-permute-start.1 = (f32[128,256]{1,0:T(8,128)S(1)}, f32[128,256]{1,0:T(8,128)S(1)}, u32[]{:S(2)}, u32[]{:S(2)}) collective-permute-start(f32[128,256]{1,0:T(8,128)S(1)} %get-tuple-element.55), channel_id=1, source_target_pairs={{0,16},{16,0},{4,20},{20,4},{8,24},{24,8},{12,28},{28,12},{1,17},{... | collective-permute-start | bytes 393224 | tf_op jit(solution)/shard_map/ppermute | solution.py:322
  17.8 6.7 %collective-permute-start.2 = (f32[128,256]{1,0:T(8,128)S(1)}, f32[128,256]{1,0:T(8,128)S(1)}, u32[]{:S(2)}, u32[]{:S(2)}) collective-permute-start(f32[128,256]{1,0:T(8,128)S(1)} %get-tuple-element.56), channel_id=1, source_target_pairs={{8,16},{16,8},{12,20},{20,12},{9,17},{17,9},{13,21},{21,13},{10,18... | collective-permute-start | bytes 393224 | tf_op jit(solution)/shard_map/ppermute | solution.py:322
  18.5 6.6 %collective-permute-start.3 = (f32[128,256]{1,0:T(8,128)S(1)}, f32[128,256]{1,0:T(8,128)S(1)}, u32[]{:S(2)}, u32[]{:S(2)}) collective-permute-start(f32[128,256]{1,0:T(8,128)S(1)} %get-tuple-element.57), channel_id=1, source_target_pairs={{0,8},{8,0},{4,12},{12,4},{16,24},{24,16},{20,28},{28,20},{1,9},{9... | collective-permute-start | bytes 393224 | tf_op jit(solution)/shard_map/ppermute | solution.py:322
  26.3 6.4 %collective-permute-start.4 = (f32[2,128,256]{2,1,0:T(8,128)S(1)}, f32[2,128,256]{2,1,0:T(8,128)S(1)}, u32[]{:S(2)}, u32[]{:S(2)}) collective-permute-start(f32[2,128,256]{2,1,0:T(8,128)S(1)} %get-tuple-element.60), channel_id=1, source_target_pairs={{0,4},{4,0},{8,12},{12,8},{16,20},{20,16},{24,28},{28,24},{1,5},{5... | collective-permute-start | bytes 786440 | tf_op jit(solution)/shard_map/ppermute | solution.py:311
  34.1 1.6 %collective-permute-start.5 = (f32[2,2,64,256]{3,2,1,0:T(8,128)S(1)}, f32[2,2,64,256]{3,2,1,0:T(8,128)S(1)}, u32[]{:S(2)}, u32[]{:S(2)}) collective-permute-start(f32[2,2,64,256]{3,2,1,0:T(8,128)S(1)} %get-tuple-element.65), channel_id=1, source_target_pairs={{0,1},{1,0},{2,3},{3,2},{4,5},{5,4},{6,7},{7,6},{8,9},{9,8},{10,11... | collective-permute-start | bytes 786440 | tf_op jit(solution)/shard_map/ppermute | solution.py:311
  35.7 5.6 %collective-permute-start.6 = (f32[1,2,64,256]{3,2,1,0:T(8,128)S(1)}, f32[1,2,64,256]{3,2,1,0:T(8,128)S(1)}, u32[]{:S(2)}, u32[]{:S(2)}) collective-permute-start(f32[1,2,64,256]{3,2,1,0:T(8,128)S(1)} %constant_dynamic-slice_fusion), channel_id=1, source_target_pairs={{0,2},{1,3},{2,0},{3,1},{4,6},{5,7},{6,4},{7,5},{8,10},{9,11},{10,... | collective-permute-start | bytes 393224 | tf_op jit(solution)/shard_map/ppermute | solution.py:311
  41.4 8.6 %collective-permute-start.8 = (f32[2,64,256]{2,1,0:T(8,128)S(1)}, f32[2,64,256]{2,1,0:T(8,128)S(1)}, u32[]{:S(2)}, u32[]{:S(2)}) collective-permute-start(f32[2,64,256]{2,1,0:T(8,128)S(1)} %add_bitcast_fusion.rest_0_), channel_id=1, source_target_pairs={{0,8},{4,12},{8,0},{12,4},{16,24},{20,28},{24,16},{28,20},{1,9},{5... | collective-permute-start | bytes 393224 | tf_op jit(solution)/shard_map/ppermute | solution.py:311
  44.3 7.3 %collective-permute-start.7 = (f32[2,64,256]{2,1,0:T(8,128)S(1)}, f32[2,64,256]{2,1,0:T(8,128)S(1)}, u32[]{:S(2)}, u32[]{:S(2)}) collective-permute-start(f32[2,64,256]{2,1,0:T(8,128)S(1)} %add_bitcast_fusion.rest_0_), channel_id=1, source_target_pairs={{0,16},{4,20},{8,24},{12,28},{16,0},{20,4},{24,8},{28,12},{1,17},{... | collective-permute-start | bytes 393224 | tf_op jit(solution)/shard_map/ppermute | solution.py:311
  51.6 5.1 %collective-permute-start.9 = (f32[2,64,256]{2,1,0:T(8,128)S(1)}, f32[2,64,256]{2,1,0:T(8,128)S(1)}, u32[]{:S(2)}, u32[]{:S(2)}) collective-permute-start(f32[2,64,256]{2,1,0:T(8,128)S(1)} %collective-permute-done.7.rest_1_), channel_id=1, source_target_pairs={{0,8},{4,12},{8,0},{12,4},{16,24},{20,28},{24,16},{28,20},{1,9},{5... | collective-permute-start | bytes 393224 | tf_op jit(solution)/shard_map/ppermute | solution.py:311
  57.4 6.4 %collective-permute-start.10 = (f32[4,64,256]{2,1,0:T(8,128)S(1)}, f32[4,64,256]{2,1,0:T(8,128)S(1)}, u32[]{:S(2)}, u32[]{:S(2)}) collective-permute-start(f32[4,64,256]{2,1,0:T(8,128)S(1)} %shard_map.118), channel_id=1, source_target_pairs={{0,4},{4,0},{8,12},{12,8},{16,20},{20,16},{24,28},{28,24},{1,5},{5... | collective-permute-start | bytes 786440 | tf_op jit(solution)/shard_map/ppermute | solution.py:311

commit v4 on v3

--- a/solution.py
+++ b/solution.py
@@ -65,7 +65,6 @@
 ):
     seq = lax.axis_index("seq")
     half = heads * HEAD_DIM // 2
-    split = heads * STATE // 2
     small = [
         pltpu.make_async_copy(a, b, small_sems.at[i])
         for i, (a, b) in enumerate(
@@ -74,18 +73,15 @@
     ]
     for copy in small:
         copy.start()
-    rows, wide = {}, {}
-    for i, (a, b, wide_a, wide_b) in enumerate(((v_hbm, v, k_hbm, k), (dy_hbm, dy, q_hbm, q))):
-        for c in range(blocks):
-            token = pl.ds(c * BLOCK, BLOCK)
-            rows[i, c] = pltpu.make_async_copy(a.at[token], b.at[token], row_sems.at[i, c])
-            rows[i, c].start()
-            for j in range(2):
-                at = (token, pl.ds(j * split, split))
-                wide[i, c, j] = pltpu.make_async_copy(
-                    wide_a.at[at], wide_b.at[at], wide_sems.at[i, c, j]
-                )
-                wide[i, c, j].start()
+    rows, wide = [], {}
+    for i, (a, b) in enumerate(((v_hbm, v), (dy_hbm, dy))):
+        rows.append(pltpu.make_async_copy(a, b, row_sems.at[i]))
+    rows[0].start()
+    for i, (a, b) in enumerate(((k_hbm, k), (q_hbm, q))):
+        wide[i] = pltpu.make_async_copy(a, b, wide_sems.at[i, 0])
+        wide[i].start()
+        if i == 0:
+            rows[1].start()
     small[0].wait()
     mat_copies = []
     for c in range(blocks):
@@ -94,28 +90,32 @@
         )
         copy.start()
         mat_copies.append(copy)
-    for i, (out, narrow_in, wide_in) in enumerate(((update, v, k), (source, dy, q))):
-        for c in range(blocks):
-            token = slice(c * BLOCK, (c + 1) * BLOCK)
-            rows[i, c].wait()
-            for h in range(heads):
-                if h % (heads // 2) == 0:
-                    wide[i, c, h // (heads // 2)].wait()
-                columns = slice(h * STATE, (h + 1) * STATE)
-                narrow = slice(h * HEAD_DIM, (h + 1) * HEAD_DIM)
-                out[c, narrow, :] = dot(narrow_in[token, narrow], wide_in[token, columns], TN)
+    def products(i, c, out, narrow_in, wide_in):
+        token = slice(c * BLOCK, (c + 1) * BLOCK)
+        if c == (0, blocks - 1)[i]:
+            rows[i].wait()
+        flipped = narrow_in[token, :].T
+        if c == (0, blocks - 1)[i]:
+            wide[i].wait()
+        for h in range(heads):
+            columns = slice(h * STATE, (h + 1) * STATE)
+            narrow = slice(h * HEAD_DIM, (h + 1) * HEAD_DIM)
+            out[c, narrow, :] = dot(flipped[narrow], wide_in[token, columns], NN)
+
+    for c in range(blocks):
+        products(0, c, update, v, k)
     for copy in small[1:] + mat_copies:
         copy.wait()
     decay = decay_column(gammas, 0, heads, 1)
+    factors = [kept_at(documents, seq * blocks + c) * decay for c in range(blocks)]
     state = update[0]
     for c in range(1, blocks):
-        factor = kept_at(documents, seq * blocks + c) * decay
-        state = update[c] + factor * dot_exact(state, mats[c], NT)
+        state = update[c] + factors[c] * dot_exact(state, mats[c], NT)
     carried = None
     for c in reversed(range(blocks)):
+        products(1, c, source, dy, q)
         total = source[c] if carried is None else source[c] + carried
-        factor = kept_at(documents, seq * blocks + c) * decay
-        carried = factor * dot_exact(total, mats[c], NN)
+        carried = factors[c] * dot_exact(total, mats[c], NN)
     upper = lax.rem(seq, 2) == 1
     for i, value in enumerate((state, carried)):
         first, second = value[:half], value[half:]
@@ -123,15 +123,46 @@
         sent[i] = jnp.where(upper, first, second)
 
 
-def maps_kernel(blocks, reach, last_block, regimes, documents, pos, transitions, device_maps, *far):
-    seq = pos[0]
+def maps_kernel(
+    blocks, heads, reach, masks, regimes, documents, gammas, transitions,
+    device_maps, powers, factors, weights, *rest,
+):
+    seq = lax.axis_index("seq")
     level = lax.div(seq, 2)
+    last_block = documents.shape[0] - 1
+    far, (mats, mat_sems) = rest[:-2], rest[-2:]
+    first = (level - reach + 1) * 2 * blocks
+    copies = []
+    for i in range(mats.shape[0]):
+        block = jnp.clip(first + i, 0, last_block)
+        copies.append(
+            pltpu.make_async_copy(transitions.at[regimes[block]], mats.at[i], mat_sems.at[i])
+        )
+        copies[-1].start()
+    for i in range(reach):
+        powers[i] = decay_column(gammas, 0, heads, blocks * max(1, 2 * i))
+    decay = decay_column(gammas, 0, heads, 1)
+    for c in range(blocks):
+        factors[c] = kept_at(documents, seq * blocks + c) * decay
+    owned, count = weights.shape[1:3]
+    for i, mask in enumerate(masks):
+        for c in range(blocks):
+            regime = regimes[(seq ^ mask) * blocks + c]
+            for j in range(2):
+                for r in range(owned):
+                    match = regime == (seq ^ (1 - j)) * owned + r
+                    weights[j, r, i * blocks + c : i * blocks + c + 1, :] = jnp.full(
+                        (1, STATE), jnp.where(match, 1.0, 0.0).astype(F32)
+                    )
+
+    for copy in copies:
+        copy.wait()
 
     def device_map(device):
         result = None
         for c in range(blocks):
             block = jnp.clip(device * blocks + c, 0, last_block)
-            mat = transitions[regimes[block]]
+            mat = mats[device * blocks + c - first]
             kept = kept_at(documents, block)
             if result is None:
                 result = mat.astype(F32)
@@ -165,11 +196,16 @@
             far[distance - 2, 1, 0], far[distance - 2, 1, 1] = halves(backward)
 
 
-def pair_kernel(blocks, heads, routes, pos, gammas, held, arrived, device_maps, *outs):
-    seq = pos[0]
+def half_rows(columns, i, upper):
+    half = columns.shape[1] // 2
+    return columns[i, pl.ds(pl.multiple_of(upper * half, half), half), :]
+
+
+def pair_kernel(routes, powers, held, arrived, device_maps, *outs):
+    seq = lax.axis_index("seq")
     level, upper = lax.div(seq, 2), lax.rem(seq, 2)
     is_upper = upper == 1
-    decay = decay_column(gammas, upper * (heads // 2), heads // 2, blocks)
+    decay = half_rows(powers, 0, upper)
     ends = [jnp.where(is_upper, arrived[0], held[0]), jnp.where(is_upper, held[0], arrived[0])]
     starts = [jnp.where(is_upper, arrived[1], held[1]), jnp.where(is_upper, held[1], arrived[1])]
     low_map = (device_maps[0, 0], device_maps[0, 1])
@@ -181,14 +217,14 @@
         out[...] = jnp.where(ahead, forward, backward)
 
 
-def entry_kernel(blocks, heads, reach, routes, pos, gammas, held, arrived, device_maps, *rest):
+def entry_kernel(reach, routes, powers, held, arrived, device_maps, *rest):
     count = len(routes)
     received, (own, sent) = rest[:count], rest[-2:]
     far = rest[count] if reach > 1 else None
-    seq = pos[0]
+    seq = lax.axis_index("seq")
     level, upper = lax.div(seq, 2), lax.rem(seq, 2)
     is_upper = upper == 1
-    decay = decay_column(gammas, upper * (heads // 2), heads // 2, blocks)
+    decay = half_rows(powers, 0, upper)
     found = dict(zip(routes, received))
     forward = backward = None
     for distance in range(1, reach + 1):
@@ -200,9 +236,7 @@
         if distance == 1:
             forward, backward = behind, ahead
         else:
-            power = decay_column(
-                gammas, upper * (heads // 2), heads // 2, 2 * blocks * (distance - 1)
-            )
+            power = half_rows(powers, distance - 1, upper)
             i = distance - 2
             forward += power * dot_pair(halves(behind), (far[i, 0, 0], far[i, 0, 1]), NT)
             backward += power * dot_pair(halves(ahead), (far[i, 1, 0], far[i, 1, 1]), NN)
@@ -218,7 +252,9 @@
     sent[1] = jnp.where(is_upper, inner_backward, backward)
 
 
-def states_of(blocks, upper, kept, decay, own, arrived, update, source, mats):
+def states_of(blocks, factors, own, arrived, update, source, mats):
+    upper = lax.rem(lax.axis_index("seq"), 2) == 1
+
     def whole(i):
         first = jnp.where(upper, arrived[i], own[i])
         second = jnp.where(upper, own[i], arrived[i])
@@ -229,57 +265,45 @@
     for c in range(blocks):
         befores.append(halves(before))
         high, low = befores[-1]
-        entry = (kept[c] * decay) * (dot(high, mats[c], NT) + dot(low, mats[c], NT))
+        entry = factors[c] * (dot(high, mats[c], NT) + dot(low, mats[c], NT))
         entries.append(entry)
         before = entry + update[c]
     for c in reversed(range(blocks)):
         leaves[c] = carried
         totals[c] = source[c] + carried
         if c > 0:
-            carried = (kept[c] * decay) * dot_exact(totals[c], mats[c], NN)
+            carried = factors[c] * dot_exact(totals[c], mats[c], NN)
     return befores, entries, leaves, totals
 
 
-def terms_kernel(
-    blocks, heads, ways, documents, pos, gammas, own, arrived, update, source, mats, held, sent, term
-):
-    seq, head = pos[0], pos[1]
-    decay = decay_column(gammas, 0, heads, 1)
-    kept = [kept_at(documents, seq * blocks + c) for c in range(blocks)]
-    befores, _, _, totals = states_of(
-        blocks, lax.rem(seq, 2) == 1, kept, decay, own, arrived, update, source, mats
-    )
+def terms_kernel(blocks, ways, factors, own, arrived, update, source, mats, held, sent, term):
+    head = lax.axis_index("head")
+    befores, _, _, totals = states_of(blocks, factors, own, arrived, update, source, mats)
     part = STATE // ways
     core = lax.rem(head, 2)
     for c in range(blocks):
-        term[...] = dot_pair(halves((kept[c] * decay) * totals[c]), befores[c], TN)
+        term[...] = dot_pair(halves(factors[c] * totals[c]), befores[c], TN)
         for i in range(ways // 2):
             held[i, c] = term[pl.ds(pl.multiple_of((2 * i + core) * part, part), part), :]
             sent[i, c] = term[pl.ds(pl.multiple_of((2 * i + 1 - core) * part, part), part), :]
 
 
-def rounded_kernel(
-    blocks, heads, documents, pos, gammas, own, arrived, update, source, mats, entries, leaves
-):
-    seq = pos[0]
-    decay = decay_column(gammas, 0, heads, 1)
-    kept = [kept_at(documents, seq * blocks + c) for c in range(blocks)]
-    _, entry, leave, _ = states_of(
-        blocks, lax.rem(seq, 2) == 1, kept, decay, own, arrived, update, source, mats
-    )
+def rounded_kernel(blocks, factors, own, arrived, update, source, mats, entries, leaves):
+    _, entry, leave, _ = states_of(blocks, factors, own, arrived, update, source, mats)
     for c in range(blocks):
         entries[c] = entry[c].astype(BF16)
         leaves[c] = leave[c].astype(BF16)
 
 
-def regime_kernel(blocks, owned, count, regimes, base, sources, *rest):
-    pieces, out = rest[:count], rest[count]
-    for r in range(owned):
+def regime_kernel(owner, weights, *rest):
+    pieces, out = rest[:-1], rest[-1]
+    blocks = pieces[0].shape[0]
+    for r in range(out.shape[0]):
         total = None
-        for i in range(count):
+        for i, piece in enumerate(pieces):
             for c in range(blocks):
-                match = regimes[sources[i] * blocks + c] == base[0] + r
-                value = jnp.where(match, pieces[i][c], 0.0)
+                at = i * blocks + c
+                value = weights[owner, r, at : at + 1, :] * piece[c]
                 total = value if total is None else total + value
         out[r] = total
 
@@ -342,8 +366,12 @@
     half = rows // 2
     reach = min(levels - 1, -(-(all_blocks // 2 - 1) // (2 * blocks)))
     routes = routes_up_to(reach, levels)[::-1]
-    seq, head = lax.axis_index("seq"), lax.axis_index("head")
-    pos = jnp.stack([seq, head]).astype(jnp.int32)
+    head = lax.axis_index("head")
+    owned, part = REGIMES // devices, STATE // ways
+    masks, by = [0], devices // 2
+    while by > 1:
+        masks += [x ^ by for x in masks]
+        by //= 2
 
     def shape(*dims, dtype=F32):
         return jax.ShapeDtypeStruct(dims, dtype)
@@ -371,8 +399,8 @@
             pltpu.SMEM(gammas.shape, F32),
             pltpu.SemaphoreType.DMA((3,)),
             pltpu.SemaphoreType.DMA((blocks,)),
+            pltpu.SemaphoreType.DMA((2,)),
             pltpu.SemaphoreType.DMA((2, blocks)),
-            pltpu.SemaphoreType.DMA((2, blocks, 2)),
         ],
         compiler_params=PARAMS,
     )(
@@ -380,74 +408,65 @@
     )
 
     arrived = swap(sent, "seq", 1)
-    map_shapes = (shape(2, 2, STATE, STATE, dtype=BF16),)
+    map_shapes = (
+        shape(2, 2, STATE, STATE, dtype=BF16),
+        shape(reach, rows, 1),
+        shape(blocks, rows, 1),
+        shape(2, owned, len(masks) * blocks, STATE),
+    )
     if reach > 1:
         map_shapes += (shape(reach - 1, 2, 2, STATE, STATE, dtype=BF16),)
-    maps = pl.pallas_call(
-        functools.partial(maps_kernel, blocks, reach, all_blocks - 1),
-        in_specs=[SMEM, SMEM, SMEM, VMEM],
+    needed = (2 * reach - 1) * 2 * blocks
+    device_maps, powers, factors, weights, *far = pl.pallas_call(
+        functools.partial(maps_kernel, blocks, heads, reach, masks),
+        in_specs=[SMEM, SMEM, SMEM, HBM],
         out_specs=(VMEM,) * len(map_shapes),
         out_shape=map_shapes,
+        scratch_shapes=[
+            pltpu.VMEM((needed, STATE, STATE), BF16),
+            pltpu.SemaphoreType.DMA((needed,)),
+        ],
         compiler_params=PARAMS,
-    )(regimes, documents, pos, transitions)
+    )(regimes, documents, gammas, in_hbm(transitions))
 
     trades = pl.pallas_call(
-        functools.partial(pair_kernel, blocks, heads, routes),
-        in_specs=[SMEM, SMEM, VMEM, VMEM, VMEM],
+        functools.partial(pair_kernel, routes),
+        in_specs=[VMEM] * 4,
         out_specs=(VMEM,) * len(routes),
         out_shape=(shape(half, STATE),) * len(routes),
         compiler_params=PARAMS,
-    )(pos, gammas, held, arrived, maps[0])
+    )(powers, held, arrived, device_maps)
     received = [level_route(x, *route) for x, route in zip(trades, routes)]
 
     own, sent_entry = pl.pallas_call(
-        functools.partial(entry_kernel, blocks, heads, reach, routes),
-        in_specs=[SMEM, SMEM] + [VMEM] * (3 + len(received) + len(maps) - 1),
+        functools.partial(entry_kernel, reach, routes),
+        in_specs=[VMEM] * (4 + len(received) + len(far)),
         out_specs=(VMEM, VMEM),
         out_shape=(half_shape, half_shape),
         compiler_params=PARAMS,
-    )(pos, gammas, held, arrived, maps[0], *received, *maps[1:])
+    )(powers, held, arrived, device_maps, *received, *far)
     arrived_entry = swap(sent_entry, "seq", 1)
 
-    part = STATE // ways
     part_shape = shape(ways // 2, blocks, part, STATE)
     bf16_states = shape(blocks, rows, STATE, dtype=BF16)
-    states = (own, arrived_entry, update, source, mats)
+    states = (factors, own, arrived_entry, update, source, mats)
 
     def states_call(kernel, states, outs, scratch):
         return pl.pallas_call(
             kernel,
-            in_specs=[SMEM] * 3 + [VMEM] * len(states),
+            in_specs=[VMEM] * len(states),
             out_specs=(VMEM,) * len(outs),
             out_shape=outs,
             scratch_shapes=scratch,
             compiler_params=PARAMS,
-        )(documents, pos, gammas, *states)
+        )(*states)
 
     held_term, sent_term = states_call(
-        functools.partial(terms_kernel, blocks, heads, ways),
+        functools.partial(terms_kernel, blocks, ways),
         states,
         (part_shape, part_shape),
         [pltpu.VMEM((STATE, STATE), F32)],
     )
-
-    summed = held_term + swap(sent_term, "head", 1)
-    states, summed = lax.optimization_barrier((states, summed))
-    entries, leaves = states_call(
-        functools.partial(rounded_kernel, blocks, heads), states, (bf16_states, bf16_states), []
-    )
-    by = 2
-    while by < ways:
-        split = summed.reshape(-1, 2, blocks, part, STATE)
-        bit = lax.rem(lax.div(head, by), 2)
-        going = lax.dynamic_index_in_dim(split, 1 - bit, 1, keepdims=False)
-        staying = lax.dynamic_index_in_dim(split, bit, 1, keepdims=False)
-        arrived_part = swap(going, "head", by)
-        arrived_part, entries, leaves = lax.optimization_barrier((arrived_part, entries, leaves))
-        summed = staying + arrived_part
-        by *= 2
-    summed = summed.reshape(blocks, part, STATE)
-    summed, entries, leaves = lax.optimization_barrier((summed, entries, leaves))
 
     def output_call(c, entries, leaves, before):
         wide = pl.BlockSpec((BLOCK, 2 * STATE), lambda h: (c, h))
@@ -468,32 +487,50 @@
             ),
         )(*[in_hbm(x) for x in inputs], entries, leaves, *before)
 
-    pieces, sources, by = [summed], [seq], devices // 2
+    sent_term, states = lax.optimization_barrier((sent_term, states))
+    arrived_term = swap(sent_term, "head", 1)
+    entries, leaves = states_call(
+        functools.partial(rounded_kernel, blocks), states, (bf16_states, bf16_states), []
+    )
+    arrived_term, entries, leaves = lax.optimization_barrier((arrived_term, entries, leaves))
+    summed = held_term + arrived_term
+    by, grads = 2, ()
+    while by < ways:
+        split = summed.reshape(-1, 2, blocks, part, STATE)
+        bit = lax.rem(lax.div(head, by), 2)
+        going = lax.dynamic_index_in_dim(split, 1 - bit, 1, keepdims=False)
+        staying = lax.dynamic_index_in_dim(split, bit, 1, keepdims=False)
+        going, entries, leaves = lax.optimization_barrier((going, entries, leaves))
+        arrived_part = swap(going, "head", by)
+        if not grads:
+            grads = output_call(0, entries, leaves, ())
+            arrived_part, grads = lax.optimization_barrier((arrived_part, grads))
+        summed = staying + arrived_part
+        by *= 2
+    summed = summed.reshape(blocks, part, STATE)
+
+    pieces, by = [summed], devices // 2
     direct = [swap(summed, "seq", 1 << i) for i in range(1, by.bit_length())][::-1]
-    grads = output_call(0, entries, leaves, ())
-    direct, grads = lax.optimization_barrier((direct, grads))
+    direct = lax.optimization_barrier(direct)
     while by > 1:
         pieces += [direct[0]] + [swap(x, "seq", by) for x in pieces[1:]]
-        sources += [x ^ by for x in sources]
         direct, by = direct[1:], by // 2
-    sources = jnp.stack(sources).astype(jnp.int32)
-    owned = REGIMES // devices
-
-    def regime_sum(device):
+
+    def regime_sum(owner):
         return pl.pallas_call(
-            functools.partial(regime_kernel, blocks, owned, len(pieces)),
-            in_specs=[SMEM] * 3 + [VMEM] * len(pieces),
+            functools.partial(regime_kernel, owner),
+            in_specs=[VMEM] * (1 + len(pieces)),
             out_specs=VMEM,
             out_shape=shape(owned, part, STATE),
             compiler_params=PARAMS,
-        )(regimes, jnp.reshape(device * owned, (1,)).astype(jnp.int32), sources, *pieces)
-
-    sent_sum = regime_sum(seq ^ 1)
+        )(weights, *pieces)
+
+    sent_sum = regime_sum(0)
     sent_sum, grads = lax.optimization_barrier((sent_sum, grads))
     arrived_sum = swap(sent_sum, "seq", 1)
     for c in range(1, blocks):
         grads = output_call(c, entries, leaves, grads)
-    own_sum = regime_sum(seq)
+    own_sum = regime_sum(1)
     arrived_sum, own_sum, grads = lax.optimization_barrier((arrived_sum, own_sum, grads))
     regime_grad = pl.pallas_call(
         add_kernel,

time: 64.8 us -> 62 us (0.957)
  Pallas kernels: 19.3 us -> 16.7 us
  local copies, waits for them, and re-layouts: 2.22 us -> 0.03 us
  waiting for transfers between devices: 20.9 us -> 22.5 us
    unnamed x8 -> x6, local copies, waits for them, and re-layouts: 2.2 us -> 0.01 us
    pallas_call x7, Pallas kernels: 7.13 us -> 5.41 us  [the longest x1 2.84 us: local(): pl.pallas_call(functools.partial(maps_kernel, blocks, heads, reach, masks...]
    ppermute x8, waiting for transfers between devices: 17.2 us -> 18.8 us  [swap(): return lax.ppermute(x, axis, [(i, i ^ by) for i in range(count)])]
    pallas_call x1, Pallas kernels: 4.01 us -> 3.16 us  [local(): pl.pallas_call(functools.partial(local_kernel, blocks, heads), in_specs=[...]
  transfers between devices with their start and end apart: 11 -> 11, of which waited for: 9 -> 10; matrix products, arithmetic and copies ran while one was open for 0% -> 0% of each run, Pallas kernels for 16% -> 18%
where the time goes in v4:
time: 62 us; the launch traced here: 61.8 us
  waiting for transfers between devices  22.5 us (36%)
  starting transfers between devices  21.8 us (35%)
  Pallas kernels  16.7 us (27%)
  between operations  0.75 us (1%)
    ppermute x8, waiting for transfers between devices, swap(): return lax.ppermute(x, axis, [(i, i ^ by) for i in range(count)])  18.8 us
    ppermute x8, starting transfers between devices, swap(): return lax.ppermute(x, axis, [(i, i ^ by) for i in range(count)])  15.3 us
    pallas_call x2, Pallas kernels, output_call(): pl.pallas_call(within_kernel, grid=(heads // 2,), in_specs=[wide, wide, n...  7.39 us
    ppermute x3, starting transfers between devices, level_route(): return lax.ppermute(x, 'seq', pairs)  6.46 us
    ppermute x3, waiting for transfers between devices, level_route(): return lax.ppermute(x, 'seq', pairs)  3.73 us
    pallas_call x1, Pallas kernels, local(): pl.pallas_call(functools.partial(local_kernel, blocks, heads), in_specs=[...  3.16 us
    pallas_call x1, Pallas kernels, local(): pl.pallas_call(functools.partial(maps_kernel, blocks, heads, reach, masks...  2.84 us
    pallas_call x2, Pallas kernels, states_call(): pl.pallas_call(kernel, in_specs=[VMEM] * len(states), out_specs=(VMEM,) *...  1.28 us
  transfers between devices with their start and end apart: 11, of which 10 were waited for; matrix products, arithmetic and copies ran while one was open for 0% of the time, Pallas kernels for 18%

profile of v4, /device:TPU:0, one launch (start us, length us, event | category | flops | bytes accessed | tf_op | source)
XLA Modules:
  0.0 61.8 jit_solution(12994462128135807379)
XLA Ops:
  0.7 3.2 %shard_map.112 = (f32[2,256,256]{2,1,0:T(8,128)S(1)}, f32[2,256,256]{2,1,0:T(8,128)S(1)}, f32[2,128,256]{2,1,0:T(8,128)S(1)}, f32[2,128,256]{2,1,0:T(8,128)S(1)}, bf16[2,256,256]{2,1,0:T(8,128)(2,1)S(1)}) custom-call(s32[16]{0:T(128)} %regimes_hbm.1, s32[16]{0:T(128)} %documents_hbm.1, f32[4]{0:T(128)} %gammas_hbm.1, bf16[32,256,256]{2,1,0:T(8,128)(2,1)} %transitions.3, ...), custom_call_target="tpu_custom_call" | custom-call | tf_op jit(solution)/shard_map/pallas_call | solution.py:390
  3.8 3.0 %collective-permute-start = (f32[2,128,256]{2,1,0:T(8,128)S(1)}, f32[2,128,256]{2,1,0:T(8,128)S(1)}, u32[]{:S(2)}, u32[]{:S(2)}) collective-permute-start(f32[2,128,256]{2,1,0:T(8,128)S(1)} %get-tuple-element.61), channel_id=1, source_target_pairs={{0,4},{4,0},{8,12},{12,8},{16,20},{20,16},{24,28},{28,24},{1,5},{5... | collective-permute-start | bytes 786440 | tf_op jit(solution)/shard_map/ppermute | solution.py:335
  6.8 2.8 %shard_map.111 = (bf16[2,2,256,256]{3,2,1,0:T(8,128)(2,1)S(1)}, f32[2,256,1]{2,1,0:T(8,128)S(1)}, f32[2,256,1]{2,1,0:T(8,128)S(1)}, f32[2,4,8,256]{3,2,1,0:T(8,128)S(1)}, bf16[1,2,2,256,256]{4,3,2,1,0:T(8,128)(2,1)S(1)}) custom-call(s32[16]{0:T(128)S(1)} %copy-done, s32[16]{0:T(128)S(1)} %copy-done.1, f32[4]{0:T(128)S(1)} %copy-done.2, ...), custom_call_target="tpu_custom_call" | custom-call | tf_op jit(solution)/shard_map/pallas_call | solution.py:420
  9.7 3.4 %collective-permute-done.arrived = f32[2,128,256]{2,1,0:T(8,128)S(1)} collective-permute-done((f32[2,128,256]{2,1,0:T(8,128)S(1)}, f32[2,128,256]{2,1,0:T(8,128)S(1)}, u32[]{:S(2)}, u32[]{:S(2)}) %collective-permute-start) | collective-permute-done | bytes 262176 | tf_op jit(solution)/shard_map/ppermute | solution.py:335
  13.1 0.4 shard_map.113
  13.5 2.9 %collective-permute-start.1 = (f32[128,256]{1,0:T(8,128)S(1)}, f32[128,256]{1,0:T(8,128)S(1)}, u32[]{:S(2)}, u32[]{:S(2)}) collective-permute-start(f32[128,256]{1,0:T(8,128)S(1)} %get-tuple-element.63), channel_id=1, source_target_pairs={{0,16},{16,0},{4,20},{20,4},{8,24},{24,8},{12,28},{28,12},{1,17},{... | collective-permute-start | bytes 393224 | tf_op jit(solution)/shard_map/ppermute | solution.py:346
  16.4 0.7 %collective-permute-start.2 = (f32[128,256]{1,0:T(8,128)S(1)}, f32[128,256]{1,0:T(8,128)S(1)}, u32[]{:S(2)}, u32[]{:S(2)}) collective-permute-start(f32[128,256]{1,0:T(8,128)S(1)} %get-tuple-element.64), channel_id=1, source_target_pairs={{8,16},{16,8},{12,20},{20,12},{9,17},{17,9},{13,21},{21,13},{10,18... | collective-permute-start | bytes 393224 | tf_op jit(solution)/shard_map/ppermute | solution.py:346
  17.1 2.9 %collective-permute-start.3 = (f32[128,256]{1,0:T(8,128)S(1)}, f32[128,256]{1,0:T(8,128)S(1)}, u32[]{:S(2)}, u32[]{:S(2)}) collective-permute-start(f32[128,256]{1,0:T(8,128)S(1)} %get-tuple-element.65), channel_id=1, source_target_pairs={{0,8},{8,0},{4,12},{12,4},{16,24},{24,16},{20,28},{28,20},{1,9},{9... | collective-permute-start | bytes 393224 | tf_op jit(solution)/shard_map/ppermute | solution.py:346
  20.0 3.1 %collective-permute-done.1.rest_0_ = f32[128,256]{1,0:T(8,128)S(1)} collective-permute-done((f32[128,256]{1,0:T(8,128)S(1)}, f32[128,256]{1,0:T(8,128)S(1)}, u32[]{:S(2)}, u32[]{:S(2)}) %collective-permute-start.1) | collective-permute-done | bytes 131104 | tf_op jit(solution)/shard_map/ppermute | solution.py:346
  23.1 0.6 %collective-permute-done.3.rest_2_ = f32[128,256]{1,0:T(8,128)S(1)} collective-permute-done((f32[128,256]{1,0:T(8,128)S(1)}, f32[128,256]{1,0:T(8,128)S(1)}, u32[]{:S(2)}, u32[]{:S(2)}) %collective-permute-start.3) | collective-permute-done | bytes 131104 | tf_op jit(solution)/shard_map/ppermute | solution.py:346
  23.7 0.6 %shard_map.114 = (f32[2,128,256]{2,1,0:T(8,128)S(1)}, f32[2,128,256]{2,1,0:T(8,128)S(1)}) custom-call(f32[2,256,1]{2,1,0:T(8,128)S(1)} %get-tuple-element.59.powers, f32[2,128,256]{2,1,0:T(8,128)S(1)} %get-tuple-element.60.held, f32[2,128,256]{2,1,0:T(8,128)S(1)} %collective-permute-done.arrived, bf16[2,2,256,256]{3,2,1,0:T(8,128)(2,1)S(1)} %get-tuple-element.62.device_maps, ...), custom_call_target="tpu_custom_call" | custom-call | tf_op jit(solution)/shard_map/pallas_call | solution.py:441
  24.3 1.5 %collective-permute-start.4 = (f32[2,128,256]{2,1,0:T(8,128)S(1)}, f32[2,128,256]{2,1,0:T(8,128)S(1)}, u32[]{:S(2)}, u32[]{:S(2)}) collective-permute-start(f32[2,128,256]{2,1,0:T(8,128)S(1)} %get-tuple-element.68), channel_id=1, source_target_pairs={{0,4},{4,0},{8,12},{12,8},{16,20},{20,16},{24,28},{28,24},{1,5},{5... | collective-permute-start | bytes 786440 | tf_op jit(solution)/shard_map/ppermute | solution.py:335
  25.8 4.9 %collective-permute-done.4.arrived = f32[2,128,256]{2,1,0:T(8,128)S(1)} collective-permute-done((f32[2,128,256]{2,1,0:T(8,128)S(1)}, f32[2,128,256]{2,1,0:T(8,128)S(1)}, u32[]{:S(2)}, u32[]{:S(2)}) %collective-permute-start.4) | collective-permute-done | bytes 262176 | tf_op jit(solution)/shard_map/ppermute | solution.py:335
  30.8 0.8 %shard_map.115 = (f32[2,2,64,256]{3,2,1,0:T(8,128)S(1)}, f32[2,2,64,256]{3,2,1,0:T(8,128)S(1)}) custom-call(f32[2,256,1]{2,1,0:T(8,128)S(1)} %get-tuple-element.75.factors, f32[2,128,256]{2,1,0:T(8,128)S(1)} %get-tuple-element.76.own, f32[2,128,256]{2,1,0:T(8,128)S(1)} %collective-permute-done.4.arrived, f32[2,256,256]{2,1,0:T(8,128)S(1)} %get-tuple-element.78.update, ...), custom_call_target="tpu_custom_call" | custom-call | tf_op jit(solution)/shard_map/pallas_call | solution.py:455
  31.6 0.1 collective-permute-start.5
  31.7 0.5 shard_map.116
  32.2 1.0 %collective-permute-done.5 = f32[2,2,64,256]{3,2,1,0:T(8,128)S(1)} collective-permute-done((f32[2,2,64,256]{3,2,1,0:T(8,128)S(1)}, f32[2,2,64,256]{3,2,1,0:T(8,128)S(1)}, u32[]{:S(2)}, u32[]{:S(2)}) %collective-permute-start.5) | collective-permute-done | bytes 262176 | tf_op jit(solution)/shard_map/ppermute | solution.py:335
  33.3 1.5 %collective-permute-start.6 = (f32[1,2,64,256]{3,2,1,0:T(8,128)S(1)}, f32[1,2,64,256]{3,2,1,0:T(8,128)S(1)}, u32[]{:S(2)}, u32[]{:S(2)}) collective-permute-start(f32[1,2,64,256]{3,2,1,0:T(8,128)S(1)} %constant_dynamic-slice_fusion), channel_id=1, source_target_pairs={{0,2},{1,3},{2,0},{3,1},{4,6},{5,7},{6,4},{7,5},{8,10},{9,11},{10,... | collective-permute-start | bytes 393224 | tf_op jit(solution)/shard_map/ppermute | solution.py:335
  34.8 3.7 %shard_map.117 = (bf16[512,1024]{1,0:T(8,128)(2,1)}, bf16[512,1024]{1,0:T(8,128)(2,1)}, bf16[512,256]{1,0:T(8,128)(2,1)}) custom-call(bf16[512,1024]{1,0:T(8,128)(2,1)} %q.3, bf16[512,1024]{1,0:T(8,128)(2,1)} %k.3, bf16[512,256]{1,0:T(8,128)(2,1)} %v.3, bf16[512,256]{1,0:T(8,128)(2,1)} %dy.3, bf16[2,256,256]{2,1,0:T(8,128)(2,1)S(1)} %get-tuple-element.87.entries, ...), custom_call_target="tpu_custom_call" | custom-call | flops 1342177280 | bytes 3145728 | tf_op jit(solution)/shard_map/pallas_call | solution.py:475
  38.5 0.4 collective-permute-done.6
  38.9 3.0 %collective-permute-start.8 = (f32[2,64,256]{2,1,0:T(8,128)S(1)}, f32[2,64,256]{2,1,0:T(8,128)S(1)}, u32[]{:S(2)}, u32[]{:S(2)}) collective-permute-start(f32[2,64,256]{2,1,0:T(8,128)S(1)} %add_bitcast_fusion.rest_0_), channel_id=1, source_target_pairs={{0,8},{4,12},{8,0},{12,4},{16,24},{20,28},{24,16},{28,20},{1,9},{5... | collective-permute-start | bytes 393224 | tf_op jit(solution)/shard_map/ppermute | solution.py:335
  41.9 2.0 %collective-permute-start.7 = (f32[2,64,256]{2,1,0:T(8,128)S(1)}, f32[2,64,256]{2,1,0:T(8,128)S(1)}, u32[]{:S(2)}, u32[]{:S(2)}) collective-permute-start(f32[2,64,256]{2,1,0:T(8,128)S(1)} %add_bitcast_fusion.rest_0_), channel_id=1, source_target_pairs={{0,16},{4,20},{8,24},{12,28},{16,0},{20,4},{24,8},{28,12},{1,17},{... | collective-permute-start | bytes 393224 | tf_op jit(solution)/shard_map/ppermute | solution.py:335
  43.9 3.1 %collective-permute-done.8.rest_2_ = f32[2,64,256]{2,1,0:T(8,128)S(1)} collective-permute-done((f32[2,64,256]{2,1,0:T(8,128)S(1)}, f32[2,64,256]{2,1,0:T(8,128)S(1)}, u32[]{:S(2)}, u32[]{:S(2)}) %collective-permute-start.8) | collective-permute-done | bytes 131104 | tf_op jit(solution)/shard_map/ppermute | solution.py:335
  47.0 1.8 %collective-permute-done.7.rest_1_ = f32[2,64,256]{2,1,0:T(8,128)S(1)} collective-permute-done((f32[2,64,256]{2,1,0:T(8,128)S(1)}, f32[2,64,256]{2,1,0:T(8,128)S(1)}, u32[]{:S(2)}, u32[]{:S(2)}) %collective-permute-start.7) | collective-permute-done | bytes 131104 | tf_op jit(solution)/shard_map/ppermute | solution.py:335
  48.8 2.7 %collective-permute-start.9 = (f32[2,64,256]{2,1,0:T(8,128)S(1)}, f32[2,64,256]{2,1,0:T(8,128)S(1)}, u32[]{:S(2)}, u32[]{:S(2)}) collective-permute-start(f32[2,64,256]{2,1,0:T(8,128)S(1)} %collective-permute-done.7.rest_1_), channel_id=1, source_target_pairs={{0,8},{4,12},{8,0},{12,4},{16,24},{20,28},{24,16},{28,20},{1,9},{5... | collective-permute-start | bytes 393224 | tf_op jit(solution)/shard_map/ppermute | solution.py:335
  51.6 2.9 %collective-permute-done.9.rest_3_ = f32[2,64,256]{2,1,0:T(8,128)S(1)} collective-permute-done((f32[2,64,256]{2,1,0:T(8,128)S(1)}, f32[2,64,256]{2,1,0:T(8,128)S(1)}, u32[]{:S(2)}, u32[]{:S(2)}) %collective-permute-start.9) | collective-permute-done | bytes 131104 | tf_op jit(solution)/shard_map/ppermute | solution.py:335
  54.5 0.1 shard_map.118
  54.7 1.5 %collective-permute-start.10 = (f32[4,64,256]{2,1,0:T(8,128)S(1)}, f32[4,64,256]{2,1,0:T(8,128)S(1)}, u32[]{:S(2)}, u32[]{:S(2)}) collective-permute-start(f32[4,64,256]{2,1,0:T(8,128)S(1)} %shard_map.118), channel_id=1, source_target_pairs={{0,4},{4,0},{8,12},{12,8},{16,20},{20,16},{24,28},{28,24},{1,5},{5... | collective-permute-start | bytes 786440 | tf_op jit(solution)/shard_map/ppermute | solution.py:335
  56.1 0.1 shard_map.119.a
  56.3 3.7 %shard_map.120 = (bf16[512,1024]{1,0:T(8,128)(2,1)}, bf16[512,1024]{1,0:T(8,128)(2,1)}, bf16[512,256]{1,0:T(8,128)(2,1)}) custom-call(bf16[512,1024]{1,0:T(8,128)(2,1)} %q.3, bf16[512,1024]{1,0:T(8,128)(2,1)} %k.3, bf16[512,256]{1,0:T(8,128)(2,1)} %v.3, bf16[512,256]{1,0:T(8,128)(2,1)} %dy.3, ...), custom_call_target="tpu_custom_call", output_to_operand_aliasing={{0}: (6, {}), {1}: (7, {}), {2}: (8, {})} | custom-call | flops 1342177280 | bytes 3145728 | tf_op jit(solution)/shard_map/pallas_call | solution.py:475
  60.0 1.1 %collective-permute-done.10.b = f32[4,64,256]{2,1,0:T(8,128)S(1)} collective-permute-done((f32[4,64,256]{2,1,0:T(8,128)S(1)}, f32[4,64,256]{2,1,0:T(8,128)S(1)}, u32[]{:S(2)}, u32[]{:S(2)}) %collective-permute-start.10) | collective-permute-done | bytes 262176 | tf_op jit(solution)/shard_map/ppermute | solution.py:335
  61.1 0.7 %shard_map.121 = f32[4,64,256]{2,1,0:T(8,128)} custom-call(f32[4,64,256]{2,1,0:T(8,128)S(1)} %shard_map.119.a, f32[4,64,256]{2,1,0:T(8,128)S(1)} %collective-permute-done.10.b), custom_call_target="tpu_custom_call" | custom-call | tf_op jit(solution)/shard_map/pallas_call | solution.py:535
  (10 shorter events, 0.1 us)
Async XLA Ops:
  0.6 6.2 %copy-start.1 = (s32[16]{0:T(128)S(1)}, s32[16]{0:T(128)}, u32[]{:S(2)}) copy-start(s32[16]{0:T(128)} %documents_hbm.1) | copy-start | bytes 196
  0.6 6.2 %copy-start = (s32[16]{0:T(128)S(1)}, s32[16]{0:T(128)}, u32[]{:S(2)}) copy-start(s32[16]{0:T(128)} %regimes_hbm.1) | copy-start | bytes 196
  0.7 6.2 %copy-start.2 = (f32[4]{0:T(128)S(1)}, f32[4]{0:T(128)}, u32[]{:S(2)}) copy-start(f32[4]{0:T(128)} %gammas_hbm.1) | copy-start | bytes 52
  3.8 9.3 %collective-permute-start = (f32[2,128,256]{2,1,0:T(8,128)S(1)}, f32[2,128,256]{2,1,0:T(8,128)S(1)}, u32[]{:S(2)}, u32[]{:S(2)}) collective-permute-start(f32[2,128,256]{2,1,0:T(8,128)S(1)} %get-tuple-element.61), channel_id=1, source_target_pairs={{0,4},{4,0},{8,12},{12,8},{16,20},{20,16},{24,28},{28,24},{1,5},{5... | collective-permute-start | bytes 786440 | tf_op jit(solution)/shard_map/ppermute | solution.py:335
  13.5 9.6 %collective-permute-start.1 = (f32[128,256]{1,0:T(8,128)S(1)}, f32[128,256]{1,0:T(8,128)S(1)}, u32[]{:S(2)}, u32[]{:S(2)}) collective-permute-start(f32[128,256]{1,0:T(8,128)S(1)} %get-tuple-element.63), channel_id=1, source_target_pairs={{0,16},{16,0},{4,20},{20,4},{8,24},{24,8},{12,28},{28,12},{1,17},{... | collective-permute-start | bytes 393224 | tf_op jit(solution)/shard_map/ppermute | solution.py:346
  16.4 6.6 %collective-permute-start.2 = (f32[128,256]{1,0:T(8,128)S(1)}, f32[128,256]{1,0:T(8,128)S(1)}, u32[]{:S(2)}, u32[]{:S(2)}) collective-permute-start(f32[128,256]{1,0:T(8,128)S(1)} %get-tuple-element.64), channel_id=1, source_target_pairs={{8,16},{16,8},{12,20},{20,12},{9,17},{17,9},{13,21},{21,13},{10,18... | collective-permute-start | bytes 393224 | tf_op jit(solution)/shard_map/ppermute | solution.py:346
  17.1 6.6 %collective-permute-start.3 = (f32[128,256]{1,0:T(8,128)S(1)}, f32[128,256]{1,0:T(8,128)S(1)}, u32[]{:S(2)}, u32[]{:S(2)}) collective-permute-start(f32[128,256]{1,0:T(8,128)S(1)} %get-tuple-element.65), channel_id=1, source_target_pairs={{0,8},{8,0},{4,12},{12,4},{16,24},{24,16},{20,28},{28,20},{1,9},{9... | collective-permute-start | bytes 393224 | tf_op jit(solution)/shard_map/ppermute | solution.py:346
  24.3 6.4 %collective-permute-start.4 = (f32[2,128,256]{2,1,0:T(8,128)S(1)}, f32[2,128,256]{2,1,0:T(8,128)S(1)}, u32[]{:S(2)}, u32[]{:S(2)}) collective-permute-start(f32[2,128,256]{2,1,0:T(8,128)S(1)} %get-tuple-element.68), channel_id=1, source_target_pairs={{0,4},{4,0},{8,12},{12,8},{16,20},{20,16},{24,28},{28,24},{1,5},{5... | collective-permute-start | bytes 786440 | tf_op jit(solution)/shard_map/ppermute | solution.py:335
  31.6 1.6 %collective-permute-start.5 = (f32[2,2,64,256]{3,2,1,0:T(8,128)S(1)}, f32[2,2,64,256]{3,2,1,0:T(8,128)S(1)}, u32[]{:S(2)}, u32[]{:S(2)}) collective-permute-start(f32[2,2,64,256]{3,2,1,0:T(8,128)S(1)} %get-tuple-element.74), channel_id=1, source_target_pairs={{0,1},{1,0},{2,3},{3,2},{4,5},{5,4},{6,7},{7,6},{8,9},{9,8},{10,11... | collective-permute-start | bytes 786440 | tf_op jit(solution)/shard_map/ppermute | solution.py:335
  33.3 5.6 %collective-permute-start.6 = (f32[1,2,64,256]{3,2,1,0:T(8,128)S(1)}, f32[1,2,64,256]{3,2,1,0:T(8,128)S(1)}, u32[]{:S(2)}, u32[]{:S(2)}) collective-permute-start(f32[1,2,64,256]{3,2,1,0:T(8,128)S(1)} %constant_dynamic-slice_fusion), channel_id=1, source_target_pairs={{0,2},{1,3},{2,0},{3,1},{4,6},{5,7},{6,4},{7,5},{8,10},{9,11},{10,... | collective-permute-start | bytes 393224 | tf_op jit(solution)/shard_map/ppermute | solution.py:335
  38.9 8.2 %collective-permute-start.8 = (f32[2,64,256]{2,1,0:T(8,128)S(1)}, f32[2,64,256]{2,1,0:T(8,128)S(1)}, u32[]{:S(2)}, u32[]{:S(2)}) collective-permute-start(f32[2,64,256]{2,1,0:T(8,128)S(1)} %add_bitcast_fusion.rest_0_), channel_id=1, source_target_pairs={{0,8},{4,12},{8,0},{12,4},{16,24},{20,28},{24,16},{28,20},{1,9},{5... | collective-permute-start | bytes 393224 | tf_op jit(solution)/shard_map/ppermute | solution.py:335
  41.9 6.9 %collective-permute-start.7 = (f32[2,64,256]{2,1,0:T(8,128)S(1)}, f32[2,64,256]{2,1,0:T(8,128)S(1)}, u32[]{:S(2)}, u32[]{:S(2)}) collective-permute-start(f32[2,64,256]{2,1,0:T(8,128)S(1)} %add_bitcast_fusion.rest_0_), channel_id=1, source_target_pairs={{0,16},{4,20},{8,24},{12,28},{16,0},{20,4},{24,8},{28,12},{1,17},{... | collective-permute-start | bytes 393224 | tf_op jit(solution)/shard_map/ppermute | solution.py:335
  48.8 5.7 %collective-permute-start.9 = (f32[2,64,256]{2,1,0:T(8,128)S(1)}, f32[2,64,256]{2,1,0:T(8,128)S(1)}, u32[]{:S(2)}, u32[]{:S(2)}) collective-permute-start(f32[2,64,256]{2,1,0:T(8,128)S(1)} %collective-permute-done.7.rest_1_), channel_id=1, source_target_pairs={{0,8},{4,12},{8,0},{12,4},{16,24},{20,28},{24,16},{28,20},{1,9},{5... | collective-permute-start | bytes 393224 | tf_op jit(solution)/shard_map/ppermute | solution.py:335
  54.7 6.4 %collective-permute-start.10 = (f32[4,64,256]{2,1,0:T(8,128)S(1)}, f32[4,64,256]{2,1,0:T(8,128)S(1)}, u32[]{:S(2)}, u32[]{:S(2)}) collective-permute-start(f32[4,64,256]{2,1,0:T(8,128)S(1)} %shard_map.118), channel_id=1, source_target_pairs={{0,4},{4,0},{8,12},{12,8},{16,20},{20,16},{24,28},{28,24},{1,5},{5... | collective-permute-start | bytes 786440 | tf_op jit(solution)/shard_map/ppermute | solution.py:335

commit v5 on v4

--- a/solution.py
+++ b/solution.py
@@ -123,6 +123,20 @@
         sent[i] = jnp.where(upper, first, second)
 
 
+def near_step():
+    return 1 + lax.rem(lax.axis_index("head"), 2)
+
+
+def swap_near(x, first):
+    devices, ways = lax.axis_size("seq"), lax.axis_size("head")
+    pairs = []
+    for seq in range(devices):
+        for head in range(ways):
+            by = 1 + head % 2 if first else 2 - head % 2
+            pairs.append((seq * ways + head, (seq ^ by) * ways + head))
+    return lax.ppermute(x, ("seq", "head"), pairs)
+
+
 def maps_kernel(
     blocks, heads, reach, masks, regimes, documents, gammas, transitions,
     device_maps, powers, factors, weights, *rest,
@@ -144,16 +158,18 @@
     decay = decay_column(gammas, 0, heads, 1)
     for c in range(blocks):
         factors[c] = kept_at(documents, seq * blocks + c) * decay
-    owned, count = weights.shape[1:3]
-    for i, mask in enumerate(masks):
+    near = near_step()
+    owned = weights.shape[1]
+    sources = [seq ^ mask for mask in masks]
+    sources += [x ^ near for x in sources]
+    for i, source in enumerate(sources):
         for c in range(blocks):
-            regime = regimes[(seq ^ mask) * blocks + c]
-            for j in range(2):
+            regime = regimes[source * blocks + c]
+            at = slice(i * blocks + c, i * blocks + c + 1)
+            for j, owner in enumerate((seq ^ (3 - near), seq)):
                 for r in range(owned):
-                    match = regime == (seq ^ (1 - j)) * owned + r
-                    weights[j, r, i * blocks + c : i * blocks + c + 1, :] = jnp.full(
-                        (1, STATE), jnp.where(match, 1.0, 0.0).astype(F32)
-                    )
+                    match = jnp.where(regime == owner * owned + r, 1.0, 0.0).astype(F32)
+                    weights[j, r, at, :] = jnp.full((1, STATE), match)
 
     for copy in copies:
         copy.wait()
@@ -368,10 +384,10 @@
     routes = routes_up_to(reach, levels)[::-1]
     head = lax.axis_index("head")
     owned, part = REGIMES // devices, STATE // ways
-    masks, by = [0], devices // 2
-    while by > 1:
+    steps = [devices - 2] + [1 << i for i in range(2, levels.bit_length() - 1)][::-1]
+    masks = [0]
+    for by in steps:
         masks += [x ^ by for x in masks]
-        by //= 2
 
     def shape(*dims, dtype=F32):
         return jax.ShapeDtypeStruct(dims, dtype)
@@ -412,7 +428,7 @@
         shape(2, 2, STATE, STATE, dtype=BF16),
         shape(reach, rows, 1),
         shape(blocks, rows, 1),
-        shape(2, owned, len(masks) * blocks, STATE),
+        shape(2, owned, 2 * len(masks) * blocks, STATE),
     )
     if reach > 1:
         map_shapes += (shape(reach - 1, 2, 2, STATE, STATE, dtype=BF16),)
@@ -509,12 +525,11 @@
         by *= 2
     summed = summed.reshape(blocks, part, STATE)
 
-    pieces, by = [summed], devices // 2
-    direct = [swap(summed, "seq", 1 << i) for i in range(1, by.bit_length())][::-1]
-    direct = lax.optimization_barrier(direct)
-    while by > 1:
-        pieces += [direct[0]] + [swap(x, "seq", by) for x in pieces[1:]]
-        direct, by = direct[1:], by // 2
+    pieces = [summed]
+    for by in steps:
+        pieces += [swap(x, "seq", by) for x in pieces]
+    near = swap_near(summed, True)
+    pieces += [near] + [swap_near(x, True) for x in pieces[1:]]
 
     def regime_sum(owner):
         return pl.pallas_call(
@@ -527,7 +542,7 @@
 
     sent_sum = regime_sum(0)
     sent_sum, grads = lax.optimization_barrier((sent_sum, grads))
-    arrived_sum = swap(sent_sum, "seq", 1)
+    arrived_sum = swap_near(sent_sum, False)
     for c in range(1, blocks):
         grads = output_call(c, entries, leaves, grads)
     own_sum = regime_sum(1)

time: 62 us -> 59.7 us (0.963)
  waiting for transfers between devices: 22.5 us -> 19.6 us
    ppermute x8 -> x5, waiting for transfers between devices: 18.8 us -> 11.9 us  [swap(): return lax.ppermute(x, axis, [(i, i ^ by) for i in range(count)])]
    ppermute x0 -> x3, starting transfers between devices: none -> 6.02 us  [swap_near(): return lax.ppermute(x, ('seq', 'head'), pairs)]
    ppermute x8 -> x5, starting transfers between devices: 15.3 us -> 9.71 us  [swap(): return lax.ppermute(x, axis, [(i, i ^ by) for i in range(count)])]
    ppermute x0 -> x3, waiting for transfers between devices: none -> 3.97 us  [swap_near(): return lax.ppermute(x, ('seq', 'head'), pairs)]
  transfers between devices with their start and end apart: 11 -> 11, of which waited for: 10 -> 9; matrix products, arithmetic and copies ran while one was open for 0% -> 0% of each run, Pallas kernels for 18% -> 19%
where the time goes in v5:
time: 59.7 us; the launch traced here: 59.4 us
  starting transfers between devices  22.2 us (37%)
  waiting for transfers between devices  19.6 us (33%)
  Pallas kernels  16.8 us (28%)
  between operations  0.75 us (1%)
    ppermute x5, waiting for transfers between devices, swap(): return lax.ppermute(x, axis, [(i, i ^ by) for i in range(count)])  11.9 us
    ppermute x5, starting transfers between devices, swap(): return lax.ppermute(x, axis, [(i, i ^ by) for i in range(count)])  9.71 us
    pallas_call x2, Pallas kernels, output_call(): pl.pallas_call(within_kernel, grid=(heads // 2,), in_specs=[wide, wide, n...  7.38 us
    ppermute x3, starting transfers between devices, level_route(): return lax.ppermute(x, 'seq', pairs)  6.46 us
    ppermute x3, starting transfers between devices, swap_near(): return lax.ppermute(x, ('seq', 'head'), pairs)  6.02 us
    ppermute x3, waiting for transfers between devices, swap_near(): return lax.ppermute(x, ('seq', 'head'), pairs)  3.97 us
    ppermute x3, waiting for transfers between devices, level_route(): return lax.ppermute(x, 'seq', pairs)  3.73 us
    pallas_call x1, Pallas kernels, local(): pl.pallas_call(functools.partial(local_kernel, blocks, heads), in_specs=[...  3.16 us
  transfers between devices with their start and end apart: 11, of which 9 were waited for; matrix products, arithmetic and copies ran while one was open for 0% of the time, Pallas kernels for 19%

profile of v5, /device:TPU:0, one launch (start us, length us, event | category | flops | bytes accessed | tf_op | source)
XLA Modules:
  0.0 59.4 jit_solution(2269700472555396655)
XLA Ops:
  0.7 3.2 %shard_map.112 = (f32[2,256,256]{2,1,0:T(8,128)S(1)}, f32[2,256,256]{2,1,0:T(8,128)S(1)}, f32[2,128,256]{2,1,0:T(8,128)S(1)}, f32[2,128,256]{2,1,0:T(8,128)S(1)}, bf16[2,256,256]{2,1,0:T(8,128)(2,1)S(1)}) custom-call(s32[16]{0:T(128)} %regimes_hbm.1, s32[16]{0:T(128)} %documents_hbm.1, f32[4]{0:T(128)} %gammas_hbm.1, bf16[32,256,256]{2,1,0:T(8,128)(2,1)} %transitions.3, ...), custom_call_target="tpu_custom_call" | custom-call | tf_op jit(solution)/shard_map/pallas_call | solution.py:406
  3.8 3.0 %collective-permute-start = (f32[2,128,256]{2,1,0:T(8,128)S(1)}, f32[2,128,256]{2,1,0:T(8,128)S(1)}, u32[]{:S(2)}, u32[]{:S(2)}) collective-permute-start(f32[2,128,256]{2,1,0:T(8,128)S(1)} %get-tuple-element.59), channel_id=1, source_target_pairs={{0,4},{4,0},{8,12},{12,8},{16,20},{20,16},{24,28},{28,24},{1,5},{5... | collective-permute-start | bytes 786440 | tf_op jit(solution)/shard_map/ppermute | solution.py:351
  6.8 3.0 %shard_map.111 = (bf16[2,2,256,256]{3,2,1,0:T(8,128)(2,1)S(1)}, f32[2,256,1]{2,1,0:T(8,128)S(1)}, f32[2,256,1]{2,1,0:T(8,128)S(1)}, f32[2,4,8,256]{3,2,1,0:T(8,128)S(1)}, bf16[1,2,2,256,256]{4,3,2,1,0:T(8,128)(2,1)S(1)}) custom-call(s32[16]{0:T(128)S(1)} %copy-done, s32[16]{0:T(128)S(1)} %copy-done.1, f32[4]{0:T(128)S(1)} %copy-done.2, ...), custom_call_target="tpu_custom_call" | custom-call | tf_op jit(solution)/shard_map/pallas_call | solution.py:436
  9.8 3.3 %collective-permute-done.arrived = f32[2,128,256]{2,1,0:T(8,128)S(1)} collective-permute-done((f32[2,128,256]{2,1,0:T(8,128)S(1)}, f32[2,128,256]{2,1,0:T(8,128)S(1)}, u32[]{:S(2)}, u32[]{:S(2)}) %collective-permute-start) | collective-permute-done | bytes 262176 | tf_op jit(solution)/shard_map/ppermute | solution.py:351
  13.1 0.4 shard_map.113
  13.5 2.9 %collective-permute-start.1 = (f32[128,256]{1,0:T(8,128)S(1)}, f32[128,256]{1,0:T(8,128)S(1)}, u32[]{:S(2)}, u32[]{:S(2)}) collective-permute-start(f32[128,256]{1,0:T(8,128)S(1)} %get-tuple-element.61), channel_id=1, source_target_pairs={{0,16},{16,0},{4,20},{20,4},{8,24},{24,8},{12,28},{28,12},{1,17},{... | collective-permute-start | bytes 393224 | tf_op jit(solution)/shard_map/ppermute | solution.py:362
  16.4 0.7 %collective-permute-start.2 = (f32[128,256]{1,0:T(8,128)S(1)}, f32[128,256]{1,0:T(8,128)S(1)}, u32[]{:S(2)}, u32[]{:S(2)}) collective-permute-start(f32[128,256]{1,0:T(8,128)S(1)} %get-tuple-element.62), channel_id=1, source_target_pairs={{8,16},{16,8},{12,20},{20,12},{9,17},{17,9},{13,21},{21,13},{10,18... | collective-permute-start | bytes 393224 | tf_op jit(solution)/shard_map/ppermute | solution.py:362
  17.1 2.9 %collective-permute-start.3 = (f32[128,256]{1,0:T(8,128)S(1)}, f32[128,256]{1,0:T(8,128)S(1)}, u32[]{:S(2)}, u32[]{:S(2)}) collective-permute-start(f32[128,256]{1,0:T(8,128)S(1)} %get-tuple-element.63), channel_id=1, source_target_pairs={{0,8},{8,0},{4,12},{12,4},{16,24},{24,16},{20,28},{28,20},{1,9},{9... | collective-permute-start | bytes 393224 | tf_op jit(solution)/shard_map/ppermute | solution.py:362
  20.0 3.1 %collective-permute-done.1.rest_0_ = f32[128,256]{1,0:T(8,128)S(1)} collective-permute-done((f32[128,256]{1,0:T(8,128)S(1)}, f32[128,256]{1,0:T(8,128)S(1)}, u32[]{:S(2)}, u32[]{:S(2)}) %collective-permute-start.1) | collective-permute-done | bytes 131104 | tf_op jit(solution)/shard_map/ppermute | solution.py:362
  23.1 0.0 collective-permute-done.2.rest_1_
  23.1 0.6 %collective-permute-done.3.rest_2_ = f32[128,256]{1,0:T(8,128)S(1)} collective-permute-done((f32[128,256]{1,0:T(8,128)S(1)}, f32[128,256]{1,0:T(8,128)S(1)}, u32[]{:S(2)}, u32[]{:S(2)}) %collective-permute-start.3) | collective-permute-done | bytes 131104 | tf_op jit(solution)/shard_map/ppermute | solution.py:362
  23.7 0.6 %shard_map.114 = (f32[2,128,256]{2,1,0:T(8,128)S(1)}, f32[2,128,256]{2,1,0:T(8,128)S(1)}) custom-call(f32[2,256,1]{2,1,0:T(8,128)S(1)} %get-tuple-element.57.powers, f32[2,128,256]{2,1,0:T(8,128)S(1)} %get-tuple-element.58.held, f32[2,128,256]{2,1,0:T(8,128)S(1)} %collective-permute-done.arrived, bf16[2,2,256,256]{3,2,1,0:T(8,128)(2,1)S(1)} %get-tuple-element.60.device_maps, ...), custom_call_target="tpu_custom_call" | custom-call | tf_op jit(solution)/shard_map/pallas_call | solution.py:457
  24.3 1.5 %collective-permute-start.4 = (f32[2,128,256]{2,1,0:T(8,128)S(1)}, f32[2,128,256]{2,1,0:T(8,128)S(1)}, u32[]{:S(2)}, u32[]{:S(2)}) collective-permute-start(f32[2,128,256]{2,1,0:T(8,128)S(1)} %get-tuple-element.66), channel_id=1, source_target_pairs={{0,4},{4,0},{8,12},{12,8},{16,20},{20,16},{24,28},{28,24},{1,5},{5... | collective-permute-start | bytes 786440 | tf_op jit(solution)/shard_map/ppermute | solution.py:351
  25.8 4.9 %collective-permute-done.4.arrived = f32[2,128,256]{2,1,0:T(8,128)S(1)} collective-permute-done((f32[2,128,256]{2,1,0:T(8,128)S(1)}, f32[2,128,256]{2,1,0:T(8,128)S(1)}, u32[]{:S(2)}, u32[]{:S(2)}) %collective-permute-start.4) | collective-permute-done | bytes 262176 | tf_op jit(solution)/shard_map/ppermute | solution.py:351
  30.8 0.8 %shard_map.115 = (f32[2,2,64,256]{3,2,1,0:T(8,128)S(1)}, f32[2,2,64,256]{3,2,1,0:T(8,128)S(1)}) custom-call(f32[2,256,1]{2,1,0:T(8,128)S(1)} %get-tuple-element.73.factors, f32[2,128,256]{2,1,0:T(8,128)S(1)} %get-tuple-element.74.own, f32[2,128,256]{2,1,0:T(8,128)S(1)} %collective-permute-done.4.arrived, f32[2,256,256]{2,1,0:T(8,128)S(1)} %get-tuple-element.76.update, ...), custom_call_target="tpu_custom_call" | custom-call | tf_op jit(solution)/shard_map/pallas_call | solution.py:471
  31.6 0.1 collective-permute-start.5
  31.7 0.5 shard_map.116
  32.2 1.0 %collective-permute-done.5 = f32[2,2,64,256]{3,2,1,0:T(8,128)S(1)} collective-permute-done((f32[2,2,64,256]{3,2,1,0:T(8,128)S(1)}, f32[2,2,64,256]{3,2,1,0:T(8,128)S(1)}, u32[]{:S(2)}, u32[]{:S(2)}) %collective-permute-start.5) | collective-permute-done | bytes 262176 | tf_op jit(solution)/shard_map/ppermute | solution.py:351
  33.3 1.5 %collective-permute-start.6 = (f32[1,2,64,256]{3,2,1,0:T(8,128)S(1)}, f32[1,2,64,256]{3,2,1,0:T(8,128)S(1)}, u32[]{:S(2)}, u32[]{:S(2)}) collective-permute-start(f32[1,2,64,256]{3,2,1,0:T(8,128)S(1)} %constant_dynamic-slice_fusion), channel_id=1, source_target_pairs={{0,2},{1,3},{2,0},{3,1},{4,6},{5,7},{6,4},{7,5},{8,10},{9,11},{10,... | collective-permute-start | bytes 393224 | tf_op jit(solution)/shard_map/ppermute | solution.py:351
  34.8 3.7 %shard_map.117 = (bf16[512,1024]{1,0:T(8,128)(2,1)}, bf16[512,1024]{1,0:T(8,128)(2,1)}, bf16[512,256]{1,0:T(8,128)(2,1)}) custom-call(bf16[512,1024]{1,0:T(8,128)(2,1)} %q.3, bf16[512,1024]{1,0:T(8,128)(2,1)} %k.3, bf16[512,256]{1,0:T(8,128)(2,1)} %v.3, bf16[512,256]{1,0:T(8,128)(2,1)} %dy.3, bf16[2,256,256]{2,1,0:T(8,128)(2,1)S(1)} %get-tuple-element.85.entries, ...), custom_call_target="tpu_custom_call" | custom-call | flops 1342177280 | bytes 3145728 | tf_op jit(solution)/shard_map/pallas_call | solution.py:491
  38.5 0.4 collective-permute-done.6
  38.9 3.6 %collective-permute-start.7 = (f32[2,64,256]{2,1,0:T(8,128)S(1)}, f32[2,64,256]{2,1,0:T(8,128)S(1)}, u32[]{:S(2)}, u32[]{:S(2)}) collective-permute-start(f32[2,64,256]{2,1,0:T(8,128)S(1)} %add_bitcast_fusion.rest_0_), channel_id=1, source_target_pairs={{0,24},{4,28},{8,16},{12,20},{16,8},{20,12},{24,0},{28,4},{1,25},{... | collective-permute-start | bytes 393224 | tf_op jit(solution)/shard_map/ppermute | solution.py:351
  42.5 1.5 %collective-permute-start.8 = (f32[2,64,256]{2,1,0:T(8,128)S(1)}, f32[2,64,256]{2,1,0:T(8,128)S(1)}, u32[]{:S(2)}, u32[]{:S(2)}) collective-permute-start(f32[2,64,256]{2,1,0:T(8,128)S(1)} %add_bitcast_fusion.rest_0_), channel_id=1, source_target_pairs={{0,4},{1,9},{2,6},{3,11},{4,0},{5,13},{6,2},{7,15},{8,12},{9,1},{1... | collective-permute-start | bytes 393224 | tf_op jit(solution)/shard_map/ppermute | solution.py:137
  44.0 2.3 %collective-permute-done.7.rest_1_ = f32[2,64,256]{2,1,0:T(8,128)S(1)} collective-permute-done((f32[2,64,256]{2,1,0:T(8,128)S(1)}, f32[2,64,256]{2,1,0:T(8,128)S(1)}, u32[]{:S(2)}, u32[]{:S(2)}) %collective-permute-start.7) | collective-permute-done | bytes 131104 | tf_op jit(solution)/shard_map/ppermute | solution.py:351
  46.2 1.5 %collective-permute-start.9 = (f32[2,64,256]{2,1,0:T(8,128)S(1)}, f32[2,64,256]{2,1,0:T(8,128)S(1)}, u32[]{:S(2)}, u32[]{:S(2)}) collective-permute-start(f32[2,64,256]{2,1,0:T(8,128)S(1)} %collective-permute-done.7.rest_1_), channel_id=1, source_target_pairs={{0,4},{1,9},{2,6},{3,11},{4,0},{5,13},{6,2},{7,15},{8,12},{9,1},{1... | collective-permute-start | bytes 393224 | tf_op jit(solution)/shard_map/ppermute | solution.py:137
  47.7 3.5 %collective-permute-done.9.rest_3_ = f32[2,64,256]{2,1,0:T(8,128)S(1)} collective-permute-done((f32[2,64,256]{2,1,0:T(8,128)S(1)}, f32[2,64,256]{2,1,0:T(8,128)S(1)}, u32[]{:S(2)}, u32[]{:S(2)}) %collective-permute-start.9) | collective-permute-done | bytes 131104 | tf_op jit(solution)/shard_map/ppermute | solution.py:137
  51.2 0.1 shard_map.118
  51.3 3.0 %collective-permute-start.10 = (f32[4,64,256]{2,1,0:T(8,128)S(1)}, f32[4,64,256]{2,1,0:T(8,128)S(1)}, u32[]{:S(2)}, u32[]{:S(2)}) collective-permute-start(f32[4,64,256]{2,1,0:T(8,128)S(1)} %shard_map.118), channel_id=1, source_target_pairs={{0,8},{1,5},{2,10},{3,7},{4,12},{5,1},{6,14},{7,3},{8,0},{9,13},{1... | collective-permute-start | bytes 786440 | tf_op jit(solution)/shard_map/ppermute | solution.py:137
  54.4 0.1 shard_map.119.a
  54.5 3.7 %shard_map.120 = (bf16[512,1024]{1,0:T(8,128)(2,1)}, bf16[512,1024]{1,0:T(8,128)(2,1)}, bf16[512,256]{1,0:T(8,128)(2,1)}) custom-call(bf16[512,1024]{1,0:T(8,128)(2,1)} %q.3, bf16[512,1024]{1,0:T(8,128)(2,1)} %k.3, bf16[512,256]{1,0:T(8,128)(2,1)} %v.3, bf16[512,256]{1,0:T(8,128)(2,1)} %dy.3, ...), custom_call_target="tpu_custom_call", output_to_operand_aliasing={{0}: (6, {}), {1}: (7, {}), {2}: (8, {})} | custom-call | flops 1342177280 | bytes 3145728 | tf_op jit(solution)/shard_map/pallas_call | solution.py:491
  58.2 0.5 collective-permute-done.10.b
  58.7 0.7 %shard_map.121 = f32[4,64,256]{2,1,0:T(8,128)} custom-call(f32[4,64,256]{2,1,0:T(8,128)S(1)} %shard_map.119.a, f32[4,64,256]{2,1,0:T(8,128)S(1)} %collective-permute-done.10.b), custom_call_target="tpu_custom_call" | custom-call | tf_op jit(solution)/shard_map/pallas_call | solution.py:550
  (10 shorter events, 0.1 us)
Async XLA Ops:
  0.6 6.2 %copy-start.1 = (s32[16]{0:T(128)S(1)}, s32[16]{0:T(128)}, u32[]{:S(2)}) copy-start(s32[16]{0:T(128)} %documents_hbm.1) | copy-start | bytes 196
  0.6 6.2 %copy-start = (s32[16]{0:T(128)S(1)}, s32[16]{0:T(128)}, u32[]{:S(2)}) copy-start(s32[16]{0:T(128)} %regimes_hbm.1) | copy-start | bytes 196
  0.7 6.2 %copy-start.2 = (f32[4]{0:T(128)S(1)}, f32[4]{0:T(128)}, u32[]{:S(2)}) copy-start(f32[4]{0:T(128)} %gammas_hbm.1) | copy-start | bytes 52
  3.8 9.3 %collective-permute-start = (f32[2,128,256]{2,1,0:T(8,128)S(1)}, f32[2,128,256]{2,1,0:T(8,128)S(1)}, u32[]{:S(2)}, u32[]{:S(2)}) collective-permute-start(f32[2,128,256]{2,1,0:T(8,128)S(1)} %get-tuple-element.59), channel_id=1, source_target_pairs={{0,4},{4,0},{8,12},{12,8},{16,20},{20,16},{24,28},{28,24},{1,5},{5... | collective-permute-start | bytes 786440 | tf_op jit(solution)/shard_map/ppermute | solution.py:351
  13.5 9.6 %collective-permute-start.1 = (f32[128,256]{1,0:T(8,128)S(1)}, f32[128,256]{1,0:T(8,128)S(1)}, u32[]{:S(2)}, u32[]{:S(2)}) collective-permute-start(f32[128,256]{1,0:T(8,128)S(1)} %get-tuple-element.61), channel_id=1, source_target_pairs={{0,16},{16,0},{4,20},{20,4},{8,24},{24,8},{12,28},{28,12},{1,17},{... | collective-permute-start | bytes 393224 | tf_op jit(solution)/shard_map/ppermute | solution.py:362
  16.4 6.7 %collective-permute-start.2 = (f32[128,256]{1,0:T(8,128)S(1)}, f32[128,256]{1,0:T(8,128)S(1)}, u32[]{:S(2)}, u32[]{:S(2)}) collective-permute-start(f32[128,256]{1,0:T(8,128)S(1)} %get-tuple-element.62), channel_id=1, source_target_pairs={{8,16},{16,8},{12,20},{20,12},{9,17},{17,9},{13,21},{21,13},{10,18... | collective-permute-start | bytes 393224 | tf_op jit(solution)/shard_map/ppermute | solution.py:362
  17.1 6.6 %collective-permute-start.3 = (f32[128,256]{1,0:T(8,128)S(1)}, f32[128,256]{1,0:T(8,128)S(1)}, u32[]{:S(2)}, u32[]{:S(2)}) collective-permute-start(f32[128,256]{1,0:T(8,128)S(1)} %get-tuple-element.63), channel_id=1, source_target_pairs={{0,8},{8,0},{4,12},{12,4},{16,24},{24,16},{20,28},{28,20},{1,9},{9... | collective-permute-start | bytes 393224 | tf_op jit(solution)/shard_map/ppermute | solution.py:362
  24.3 6.4 %collective-permute-start.4 = (f32[2,128,256]{2,1,0:T(8,128)S(1)}, f32[2,128,256]{2,1,0:T(8,128)S(1)}, u32[]{:S(2)}, u32[]{:S(2)}) collective-permute-start(f32[2,128,256]{2,1,0:T(8,128)S(1)} %get-tuple-element.66), channel_id=1, source_target_pairs={{0,4},{4,0},{8,12},{12,8},{16,20},{20,16},{24,28},{28,24},{1,5},{5... | collective-permute-start | bytes 786440 | tf_op jit(solution)/shard_map/ppermute | solution.py:351
  31.6 1.6 %collective-permute-start.5 = (f32[2,2,64,256]{3,2,1,0:T(8,128)S(1)}, f32[2,2,64,256]{3,2,1,0:T(8,128)S(1)}, u32[]{:S(2)}, u32[]{:S(2)}) collective-permute-start(f32[2,2,64,256]{3,2,1,0:T(8,128)S(1)} %get-tuple-element.72), channel_id=1, source_target_pairs={{0,1},{1,0},{2,3},{3,2},{4,5},{5,4},{6,7},{7,6},{8,9},{9,8},{10,11... | collective-permute-start | bytes 786440 | tf_op jit(solution)/shard_map/ppermute | solution.py:351
  33.3 5.6 %collective-permute-start.6 = (f32[1,2,64,256]{3,2,1,0:T(8,128)S(1)}, f32[1,2,64,256]{3,2,1,0:T(8,128)S(1)}, u32[]{:S(2)}, u32[]{:S(2)}) collective-permute-start(f32[1,2,64,256]{3,2,1,0:T(8,128)S(1)} %constant_dynamic-slice_fusion), channel_id=1, source_target_pairs={{0,2},{1,3},{2,0},{3,1},{4,6},{5,7},{6,4},{7,5},{8,10},{9,11},{10,... | collective-permute-start | bytes 393224 | tf_op jit(solution)/shard_map/ppermute | solution.py:351
  38.9 7.3 %collective-permute-start.7 = (f32[2,64,256]{2,1,0:T(8,128)S(1)}, f32[2,64,256]{2,1,0:T(8,128)S(1)}, u32[]{:S(2)}, u32[]{:S(2)}) collective-permute-start(f32[2,64,256]{2,1,0:T(8,128)S(1)} %add_bitcast_fusion.rest_0_), channel_id=1, source_target_pairs={{0,24},{4,28},{8,16},{12,20},{16,8},{20,12},{24,0},{28,4},{1,25},{... | collective-permute-start | bytes 393224 | tf_op jit(solution)/shard_map/ppermute | solution.py:351
  42.5 5.3 %collective-permute-start.8 = (f32[2,64,256]{2,1,0:T(8,128)S(1)}, f32[2,64,256]{2,1,0:T(8,128)S(1)}, u32[]{:S(2)}, u32[]{:S(2)}) collective-permute-start(f32[2,64,256]{2,1,0:T(8,128)S(1)} %add_bitcast_fusion.rest_0_), channel_id=1, source_target_pairs={{0,4},{1,9},{2,6},{3,11},{4,0},{5,13},{6,2},{7,15},{8,12},{9,1},{1... | collective-permute-start | bytes 393224 | tf_op jit(solution)/shard_map/ppermute | solution.py:137
  46.2 5.0 %collective-permute-start.9 = (f32[2,64,256]{2,1,0:T(8,128)S(1)}, f32[2,64,256]{2,1,0:T(8,128)S(1)}, u32[]{:S(2)}, u32[]{:S(2)}) collective-permute-start(f32[2,64,256]{2,1,0:T(8,128)S(1)} %collective-permute-done.7.rest_1_), channel_id=1, source_target_pairs={{0,4},{1,9},{2,6},{3,11},{4,0},{5,13},{6,2},{7,15},{8,12},{9,1},{1... | collective-permute-start | bytes 393224 | tf_op jit(solution)/shard_map/ppermute | solution.py:137
  51.3 7.4 %collective-permute-start.10 = (f32[4,64,256]{2,1,0:T(8,128)S(1)}, f32[4,64,256]{2,1,0:T(8,128)S(1)}, u32[]{:S(2)}, u32[]{:S(2)}) collective-permute-start(f32[4,64,256]{2,1,0:T(8,128)S(1)} %shard_map.118), channel_id=1, source_target_pairs={{0,8},{1,5},{2,10},{3,7},{4,12},{5,1},{6,14},{7,3},{8,0},{9,13},{1... | collective-permute-start | bytes 786440 | tf_op jit(solution)/shard_map/ppermute | solution.py:137

commit v6 on v5

--- a/solution.py
+++ b/solution.py
@@ -292,13 +292,42 @@
     return befores, entries, leaves, totals
 
 
-def terms_kernel(blocks, ways, factors, own, arrived, update, source, mats, held, sent, term):
+def half_terms(blocks, side, factors, entering, update, source, mats):
+    half = entering.shape[1]
+    rows = pl.ds(pl.multiple_of(side * half, half), half)
+    before, carried = entering[0], entering[1]
+    befores, totals = [], [None] * blocks
+    for c in range(blocks):
+        befores.append(halves(before))
+        if c + 1 < blocks:
+            high, low = befores[c]
+            entry = dot(high, mats[c], NT) + dot(low, mats[c], NT)
+            before = factors[c, rows, :] * entry + update[c, rows, :]
+    for c in reversed(range(blocks)):
+        totals[c] = source[c, rows, :] + carried
+        if c > 0:
+            carried = factors[c, rows, :] * dot_exact(totals[c], mats[c], NN)
+    return [
+        dot_pair(halves(factors[c, rows, :] * totals[c]), befores[c], TN) for c in range(blocks)
+    ]
+
+
+def own_terms_kernel(blocks, factors, own, update, source, mats, out):
+    side = lax.rem(lax.axis_index("seq"), 2)
+    for c, term in enumerate(half_terms(blocks, side, factors, own, update, source, mats)):
+        out[c] = term
+
+
+def terms_kernel(
+    blocks, ways, factors, own_terms, arrived, update, source, mats, held, sent, term
+):
     head = lax.axis_index("head")
-    befores, _, _, totals = states_of(blocks, factors, own, arrived, update, source, mats)
+    side = 1 - lax.rem(lax.axis_index("seq"), 2)
     part = STATE // ways
     core = lax.rem(head, 2)
+    terms = half_terms(blocks, side, factors, arrived, update, source, mats)
     for c in range(blocks):
-        term[...] = dot_pair(halves(factors[c] * totals[c]), befores[c], TN)
+        term[...] = own_terms[c] + terms[c]
         for i in range(ways // 2):
             held[i, c] = term[pl.ds(pl.multiple_of((2 * i + core) * part, part), part), :]
             sent[i, c] = term[pl.ds(pl.multiple_of((2 * i + 1 - core) * part, part), part), :]
@@ -477,9 +506,15 @@
             compiler_params=PARAMS,
         )(*states)
 
+    (own_terms,) = states_call(
+        functools.partial(own_terms_kernel, blocks),
+        (factors, own, update, source, mats),
+        (shape(blocks, STATE, STATE),),
+        [],
+    )
     held_term, sent_term = states_call(
         functools.partial(terms_kernel, blocks, ways),
-        states,
+        (factors, own_terms, arrived_entry, update, source, mats),
         (part_shape, part_shape),
         [pltpu.VMEM((STATE, STATE), F32)],
     )

time: 59.7 us -> 59.6 us (level)
  waiting for transfers between devices: 19.6 us -> 19 us
  Pallas kernels: 16.8 us -> 17.4 us
    ppermute x5, waiting for transfers between devices: 11.9 us -> 11.3 us  [swap(): return lax.ppermute(x, axis, [(i, i ^ by) for i in range(count)])]
    pallas_call x2 -> x3, Pallas kernels: 1.28 us -> 1.84 us  [states_call(): pl.pallas_call(kernel, in_specs=[VMEM] * len(states), out_specs=(VMEM,) *...]
  transfers between devices with their start and end apart: 11 -> 11, of which waited for: 9 -> 9; matrix products, arithmetic and copies ran while one was open for 0% -> 0% of each run, Pallas kernels for 19% -> 20%
where the time goes in v6:
time: 59.6 us; the launch traced here: 59.4 us
  starting transfers between devices  22.2 us (37%)
  waiting for transfers between devices  19 us (32%)
  Pallas kernels  17.4 us (29%)
  between operations  0.76 us (1%)
    ppermute x5, waiting for transfers between devices, swap(): return lax.ppermute(x, axis, [(i, i ^ by) for i in range(count)])  11.3 us
    ppermute x5, starting transfers between devices, swap(): return lax.ppermute(x, axis, [(i, i ^ by) for i in range(count)])  9.71 us
    pallas_call x2, Pallas kernels, output_call(): pl.pallas_call(within_kernel, grid=(heads // 2,), in_specs=[wide, wide, n...  7.38 us
    ppermute x3, starting transfers between devices, level_route(): return lax.ppermute(x, 'seq', pairs)  6.46 us
    ppermute x3, starting transfers between devices, swap_near(): return lax.ppermute(x, ('seq', 'head'), pairs)  6 us
    ppermute x3, waiting for transfers between devices, swap_near(): return lax.ppermute(x, ('seq', 'head'), pairs)  3.98 us
    ppermute x3, waiting for transfers between devices, level_route(): return lax.ppermute(x, 'seq', pairs)  3.73 us
    pallas_call x1, Pallas kernels, local(): pl.pallas_call(functools.partial(local_kernel, blocks, heads), in_specs=[...  3.16 us
  transfers between devices with their start and end apart: 11, of which 9 were waited for; matrix products, arithmetic and copies ran while one was open for 0% of the time, Pallas kernels for 20%

profile of v6, /device:TPU:0, one launch (start us, length us, event | category | flops | bytes accessed | tf_op | source)
XLA Modules:
  0.0 59.4 jit_solution(14536471528445527527)
XLA Ops:
  0.7 3.2 %shard_map.112 = (f32[2,256,256]{2,1,0:T(8,128)S(1)}, f32[2,256,256]{2,1,0:T(8,128)S(1)}, f32[2,128,256]{2,1,0:T(8,128)S(1)}, f32[2,128,256]{2,1,0:T(8,128)S(1)}, bf16[2,256,256]{2,1,0:T(8,128)(2,1)S(1)}) custom-call(s32[16]{0:T(128)} %regimes_hbm.1, s32[16]{0:T(128)} %documents_hbm.1, f32[4]{0:T(128)} %gammas_hbm.1, bf16[32,256,256]{2,1,0:T(8,128)(2,1)} %transitions.3, ...), custom_call_target="tpu_custom_call" | custom-call | tf_op jit(solution)/shard_map/pallas_call | solution.py:435
  3.8 3.0 %collective-permute-start = (f32[2,128,256]{2,1,0:T(8,128)S(1)}, f32[2,128,256]{2,1,0:T(8,128)S(1)}, u32[]{:S(2)}, u32[]{:S(2)}) collective-permute-start(f32[2,128,256]{2,1,0:T(8,128)S(1)} %get-tuple-element.59), channel_id=1, source_target_pairs={{0,4},{4,0},{8,12},{12,8},{16,20},{20,16},{24,28},{28,24},{1,5},{5... | collective-permute-start | bytes 786440 | tf_op jit(solution)/shard_map/ppermute | solution.py:380
  6.8 3.0 %shard_map.111 = (bf16[2,2,256,256]{3,2,1,0:T(8,128)(2,1)S(1)}, f32[2,256,1]{2,1,0:T(8,128)S(1)}, f32[2,256,1]{2,1,0:T(8,128)S(1)}, f32[2,4,8,256]{3,2,1,0:T(8,128)S(1)}, bf16[1,2,2,256,256]{4,3,2,1,0:T(8,128)(2,1)S(1)}) custom-call(s32[16]{0:T(128)S(1)} %copy-done, s32[16]{0:T(128)S(1)} %copy-done.1, f32[4]{0:T(128)S(1)} %copy-done.2, ...), custom_call_target="tpu_custom_call" | custom-call | tf_op jit(solution)/shard_map/pallas_call | solution.py:465
  9.8 3.3 %collective-permute-done.arrived = f32[2,128,256]{2,1,0:T(8,128)S(1)} collective-permute-done((f32[2,128,256]{2,1,0:T(8,128)S(1)}, f32[2,128,256]{2,1,0:T(8,128)S(1)}, u32[]{:S(2)}, u32[]{:S(2)}) %collective-permute-start) | collective-permute-done | bytes 262176 | tf_op jit(solution)/shard_map/ppermute | solution.py:380
  13.1 0.4 shard_map.113
  13.5 2.9 %collective-permute-start.1 = (f32[128,256]{1,0:T(8,128)S(1)}, f32[128,256]{1,0:T(8,128)S(1)}, u32[]{:S(2)}, u32[]{:S(2)}) collective-permute-start(f32[128,256]{1,0:T(8,128)S(1)} %get-tuple-element.61), channel_id=1, source_target_pairs={{0,16},{16,0},{4,20},{20,4},{8,24},{24,8},{12,28},{28,12},{1,17},{... | collective-permute-start | bytes 393224 | tf_op jit(solution)/shard_map/ppermute | solution.py:391
  16.4 0.7 %collective-permute-start.2 = (f32[128,256]{1,0:T(8,128)S(1)}, f32[128,256]{1,0:T(8,128)S(1)}, u32[]{:S(2)}, u32[]{:S(2)}) collective-permute-start(f32[128,256]{1,0:T(8,128)S(1)} %get-tuple-element.62), channel_id=1, source_target_pairs={{8,16},{16,8},{12,20},{20,12},{9,17},{17,9},{13,21},{21,13},{10,18... | collective-permute-start | bytes 393224 | tf_op jit(solution)/shard_map/ppermute | solution.py:391
  17.1 2.9 %collective-permute-start.3 = (f32[128,256]{1,0:T(8,128)S(1)}, f32[128,256]{1,0:T(8,128)S(1)}, u32[]{:S(2)}, u32[]{:S(2)}) collective-permute-start(f32[128,256]{1,0:T(8,128)S(1)} %get-tuple-element.63), channel_id=1, source_target_pairs={{0,8},{8,0},{4,12},{12,4},{16,24},{24,16},{20,28},{28,20},{1,9},{9... | collective-permute-start | bytes 393224 | tf_op jit(solution)/shard_map/ppermute | solution.py:391
  20.0 3.1 %collective-permute-done.1.rest_0_ = f32[128,256]{1,0:T(8,128)S(1)} collective-permute-done((f32[128,256]{1,0:T(8,128)S(1)}, f32[128,256]{1,0:T(8,128)S(1)}, u32[]{:S(2)}, u32[]{:S(2)}) %collective-permute-start.1) | collective-permute-done | bytes 131104 | tf_op jit(solution)/shard_map/ppermute | solution.py:391
  23.1 0.6 %collective-permute-done.3.rest_2_ = f32[128,256]{1,0:T(8,128)S(1)} collective-permute-done((f32[128,256]{1,0:T(8,128)S(1)}, f32[128,256]{1,0:T(8,128)S(1)}, u32[]{:S(2)}, u32[]{:S(2)}) %collective-permute-start.3) | collective-permute-done | bytes 131104 | tf_op jit(solution)/shard_map/ppermute | solution.py:391
  23.7 0.6 %shard_map.114 = (f32[2,128,256]{2,1,0:T(8,128)S(1)}, f32[2,128,256]{2,1,0:T(8,128)S(1)}) custom-call(f32[2,256,1]{2,1,0:T(8,128)S(1)} %get-tuple-element.57.powers, f32[2,128,256]{2,1,0:T(8,128)S(1)} %get-tuple-element.58.held, f32[2,128,256]{2,1,0:T(8,128)S(1)} %collective-permute-done.arrived, bf16[2,2,256,256]{3,2,1,0:T(8,128)(2,1)S(1)} %get-tuple-element.60.device_maps, ...), custom_call_target="tpu_custom_call" | custom-call | tf_op jit(solution)/shard_map/pallas_call | solution.py:486
  24.3 1.5 %collective-permute-start.4 = (f32[2,128,256]{2,1,0:T(8,128)S(1)}, f32[2,128,256]{2,1,0:T(8,128)S(1)}, u32[]{:S(2)}, u32[]{:S(2)}) collective-permute-start(f32[2,128,256]{2,1,0:T(8,128)S(1)} %get-tuple-element.69), channel_id=1, source_target_pairs={{0,4},{4,0},{8,12},{12,8},{16,20},{20,16},{24,28},{28,24},{1,5},{5... | collective-permute-start | bytes 786440 | tf_op jit(solution)/shard_map/ppermute | solution.py:380
  25.8 0.6 %shard_map.115.own_terms = f32[2,256,256]{2,1,0:T(8,128)S(1)} custom-call(f32[2,256,1]{2,1,0:T(8,128)S(1)} %get-tuple-element.73.factors, f32[2,128,256]{2,1,0:T(8,128)S(1)} %get-tuple-element.74.own, f32[2,256,256]{2,1,0:T(8,128)S(1)} %get-tuple-element.76.update, f32[2,256,256]{2,1,0:T(8,128)S(1)} %get-tuple-element.77.source, ...), custom_call_target="tpu_custom_call" | custom-call | tf_op jit(solution)/shard_map/pallas_call | solution.py:500
  26.5 4.3 %collective-permute-done.4.arrived = f32[2,128,256]{2,1,0:T(8,128)S(1)} collective-permute-done((f32[2,128,256]{2,1,0:T(8,128)S(1)}, f32[2,128,256]{2,1,0:T(8,128)S(1)}, u32[]{:S(2)}, u32[]{:S(2)}) %collective-permute-start.4) | collective-permute-done | bytes 262176 | tf_op jit(solution)/shard_map/ppermute | solution.py:380
  30.8 0.7 %shard_map.116 = (f32[2,2,64,256]{3,2,1,0:T(8,128)S(1)}, f32[2,2,64,256]{3,2,1,0:T(8,128)S(1)}) custom-call(f32[2,256,1]{2,1,0:T(8,128)S(1)} %get-tuple-element.73.factors, f32[2,256,256]{2,1,0:T(8,128)S(1)} %shard_map.115.own_terms, f32[2,128,256]{2,1,0:T(8,128)S(1)} %collective-permute-done.4.arrived, f32[2,256,256]{2,1,0:T(8,128)S(1)} %get-tuple-element.76.update, ...), custom_call_target="tpu_custom_call" | custom-call | tf_op jit(solution)/shard_map/pallas_call | solution.py:500
  31.5 0.1 collective-permute-start.5
  31.6 0.5 shard_map.117
  32.1 1.0 %collective-permute-done.5 = f32[2,2,64,256]{3,2,1,0:T(8,128)S(1)} collective-permute-done((f32[2,2,64,256]{3,2,1,0:T(8,128)S(1)}, f32[2,2,64,256]{3,2,1,0:T(8,128)S(1)}, u32[]{:S(2)}, u32[]{:S(2)}) %collective-permute-start.5) | collective-permute-done | bytes 262176 | tf_op jit(solution)/shard_map/ppermute | solution.py:380
  33.2 1.5 %collective-permute-start.6 = (f32[1,2,64,256]{3,2,1,0:T(8,128)S(1)}, f32[1,2,64,256]{3,2,1,0:T(8,128)S(1)}, u32[]{:S(2)}, u32[]{:S(2)}) collective-permute-start(f32[1,2,64,256]{3,2,1,0:T(8,128)S(1)} %constant_dynamic-slice_fusion), channel_id=1, source_target_pairs={{0,2},{1,3},{2,0},{3,1},{4,6},{5,7},{6,4},{7,5},{8,10},{9,11},{10,... | collective-permute-start | bytes 393224 | tf_op jit(solution)/shard_map/ppermute | solution.py:380
  34.7 3.7 %shard_map.118 = (bf16[512,1024]{1,0:T(8,128)(2,1)}, bf16[512,1024]{1,0:T(8,128)(2,1)}, bf16[512,256]{1,0:T(8,128)(2,1)}) custom-call(bf16[512,1024]{1,0:T(8,128)(2,1)} %q.3, bf16[512,1024]{1,0:T(8,128)(2,1)} %k.3, bf16[512,256]{1,0:T(8,128)(2,1)} %v.3, bf16[512,256]{1,0:T(8,128)(2,1)} %dy.3, bf16[2,256,256]{2,1,0:T(8,128)(2,1)S(1)} %get-tuple-element.85.entries, ...), custom_call_target="tpu_custom_call" | custom-call | flops 1342177280 | bytes 3145728 | tf_op jit(solution)/shard_map/pallas_call | solution.py:526
  38.4 0.4 collective-permute-done.6
  38.8 3.6 %collective-permute-start.7 = (f32[2,64,256]{2,1,0:T(8,128)S(1)}, f32[2,64,256]{2,1,0:T(8,128)S(1)}, u32[]{:S(2)}, u32[]{:S(2)}) collective-permute-start(f32[2,64,256]{2,1,0:T(8,128)S(1)} %add_bitcast_fusion.rest_0_), channel_id=1, source_target_pairs={{0,24},{4,28},{8,16},{12,20},{16,8},{20,12},{24,0},{28,4},{1,25},{... | collective-permute-start | bytes 393224 | tf_op jit(solution)/shard_map/ppermute | solution.py:380
  42.4 1.5 %collective-permute-start.8 = (f32[2,64,256]{2,1,0:T(8,128)S(1)}, f32[2,64,256]{2,1,0:T(8,128)S(1)}, u32[]{:S(2)}, u32[]{:S(2)}) collective-permute-start(f32[2,64,256]{2,1,0:T(8,128)S(1)} %add_bitcast_fusion.rest_0_), channel_id=1, source_target_pairs={{0,4},{1,9},{2,6},{3,11},{4,0},{5,13},{6,2},{7,15},{8,12},{9,1},{1... | collective-permute-start | bytes 393224 | tf_op jit(solution)/shard_map/ppermute | solution.py:137
  43.9 2.3 %collective-permute-done.7.rest_1_ = f32[2,64,256]{2,1,0:T(8,128)S(1)} collective-permute-done((f32[2,64,256]{2,1,0:T(8,128)S(1)}, f32[2,64,256]{2,1,0:T(8,128)S(1)}, u32[]{:S(2)}, u32[]{:S(2)}) %collective-permute-start.7) | collective-permute-done | bytes 131104 | tf_op jit(solution)/shard_map/ppermute | solution.py:380
  46.2 1.5 %collective-permute-start.9 = (f32[2,64,256]{2,1,0:T(8,128)S(1)}, f32[2,64,256]{2,1,0:T(8,128)S(1)}, u32[]{:S(2)}, u32[]{:S(2)}) collective-permute-start(f32[2,64,256]{2,1,0:T(8,128)S(1)} %collective-permute-done.7.rest_1_), channel_id=1, source_target_pairs={{0,4},{1,9},{2,6},{3,11},{4,0},{5,13},{6,2},{7,15},{8,12},{9,1},{1... | collective-permute-start | bytes 393224 | tf_op jit(solution)/shard_map/ppermute | solution.py:137
  47.7 3.5 %collective-permute-done.9.rest_3_ = f32[2,64,256]{2,1,0:T(8,128)S(1)} collective-permute-done((f32[2,64,256]{2,1,0:T(8,128)S(1)}, f32[2,64,256]{2,1,0:T(8,128)S(1)}, u32[]{:S(2)}, u32[]{:S(2)}) %collective-permute-start.9) | collective-permute-done | bytes 131104 | tf_op jit(solution)/shard_map/ppermute | solution.py:137
  51.1 0.1 shard_map.119
  51.3 3.0 %collective-permute-start.10 = (f32[4,64,256]{2,1,0:T(8,128)S(1)}, f32[4,64,256]{2,1,0:T(8,128)S(1)}, u32[]{:S(2)}, u32[]{:S(2)}) collective-permute-start(f32[4,64,256]{2,1,0:T(8,128)S(1)} %shard_map.119), channel_id=1, source_target_pairs={{0,8},{1,5},{2,10},{3,7},{4,12},{5,1},{6,14},{7,3},{8,0},{9,13},{1... | collective-permute-start | bytes 786440 | tf_op jit(solution)/shard_map/ppermute | solution.py:137
  54.3 0.1 shard_map.120.a
  54.4 3.7 %shard_map.121 = (bf16[512,1024]{1,0:T(8,128)(2,1)}, bf16[512,1024]{1,0:T(8,128)(2,1)}, bf16[512,256]{1,0:T(8,128)(2,1)}) custom-call(bf16[512,1024]{1,0:T(8,128)(2,1)} %q.3, bf16[512,1024]{1,0:T(8,128)(2,1)} %k.3, bf16[512,256]{1,0:T(8,128)(2,1)} %v.3, bf16[512,256]{1,0:T(8,128)(2,1)} %dy.3, ...), custom_call_target="tpu_custom_call", output_to_operand_aliasing={{0}: (6, {}), {1}: (7, {}), {2}: (8, {})} | custom-call | flops 1342177280 | bytes 3145728 | tf_op jit(solution)/shard_map/pallas_call | solution.py:526
  58.1 0.5 collective-permute-done.10.b
  58.6 0.7 %shard_map.122 = f32[4,64,256]{2,1,0:T(8,128)} custom-call(f32[4,64,256]{2,1,0:T(8,128)S(1)} %shard_map.120.a, f32[4,64,256]{2,1,0:T(8,128)S(1)} %collective-permute-done.10.b), custom_call_target="tpu_custom_call" | custom-call | tf_op jit(solution)/shard_map/pallas_call | solution.py:585
  (11 shorter events, 0.1 us)
Async XLA Ops:
  0.6 6.2 %copy-start.1 = (s32[16]{0:T(128)S(1)}, s32[16]{0:T(128)}, u32[]{:S(2)}) copy-start(s32[16]{0:T(128)} %documents_hbm.1) | copy-start | bytes 196
  0.6 6.2 %copy-start = (s32[16]{0:T(128)S(1)}, s32[16]{0:T(128)}, u32[]{:S(2)}) copy-start(s32[16]{0:T(128)} %regimes_hbm.1) | copy-start | bytes 196
  0.7 6.2 %copy-start.2 = (f32[4]{0:T(128)S(1)}, f32[4]{0:T(128)}, u32[]{:S(2)}) copy-start(f32[4]{0:T(128)} %gammas_hbm.1) | copy-start | bytes 52
  3.8 9.3 %collective-permute-start = (f32[2,128,256]{2,1,0:T(8,128)S(1)}, f32[2,128,256]{2,1,0:T(8,128)S(1)}, u32[]{:S(2)}, u32[]{:S(2)}) collective-permute-start(f32[2,128,256]{2,1,0:T(8,128)S(1)} %get-tuple-element.59), channel_id=1, source_target_pairs={{0,4},{4,0},{8,12},{12,8},{16,20},{20,16},{24,28},{28,24},{1,5},{5... | collective-permute-start | bytes 786440 | tf_op jit(solution)/shard_map/ppermute | solution.py:380
  13.5 9.6 %collective-permute-start.1 = (f32[128,256]{1,0:T(8,128)S(1)}, f32[128,256]{1,0:T(8,128)S(1)}, u32[]{:S(2)}, u32[]{:S(2)}) collective-permute-start(f32[128,256]{1,0:T(8,128)S(1)} %get-tuple-element.61), channel_id=1, source_target_pairs={{0,16},{16,0},{4,20},{20,4},{8,24},{24,8},{12,28},{28,12},{1,17},{... | collective-permute-start | bytes 393224 | tf_op jit(solution)/shard_map/ppermute | solution.py:391
  16.4 6.7 %collective-permute-start.2 = (f32[128,256]{1,0:T(8,128)S(1)}, f32[128,256]{1,0:T(8,128)S(1)}, u32[]{:S(2)}, u32[]{:S(2)}) collective-permute-start(f32[128,256]{1,0:T(8,128)S(1)} %get-tuple-element.62), channel_id=1, source_target_pairs={{8,16},{16,8},{12,20},{20,12},{9,17},{17,9},{13,21},{21,13},{10,18... | collective-permute-start | bytes 393224 | tf_op jit(solution)/shard_map/ppermute | solution.py:391
  17.1 6.6 %collective-permute-start.3 = (f32[128,256]{1,0:T(8,128)S(1)}, f32[128,256]{1,0:T(8,128)S(1)}, u32[]{:S(2)}, u32[]{:S(2)}) collective-permute-start(f32[128,256]{1,0:T(8,128)S(1)} %get-tuple-element.63), channel_id=1, source_target_pairs={{0,8},{8,0},{4,12},{12,4},{16,24},{24,16},{20,28},{28,20},{1,9},{9... | collective-permute-start | bytes 393224 | tf_op jit(solution)/shard_map/ppermute | solution.py:391
  24.3 6.4 %collective-permute-start.4 = (f32[2,128,256]{2,1,0:T(8,128)S(1)}, f32[2,128,256]{2,1,0:T(8,128)S(1)}, u32[]{:S(2)}, u32[]{:S(2)}) collective-permute-start(f32[2,128,256]{2,1,0:T(8,128)S(1)} %get-tuple-element.69), channel_id=1, source_target_pairs={{0,4},{4,0},{8,12},{12,8},{16,20},{20,16},{24,28},{28,24},{1,5},{5... | collective-permute-start | bytes 786440 | tf_op jit(solution)/shard_map/ppermute | solution.py:380
  31.5 1.6 %collective-permute-start.5 = (f32[2,2,64,256]{3,2,1,0:T(8,128)S(1)}, f32[2,2,64,256]{3,2,1,0:T(8,128)S(1)}, u32[]{:S(2)}, u32[]{:S(2)}) collective-permute-start(f32[2,2,64,256]{3,2,1,0:T(8,128)S(1)} %get-tuple-element.72), channel_id=1, source_target_pairs={{0,1},{1,0},{2,3},{3,2},{4,5},{5,4},{6,7},{7,6},{8,9},{9,8},{10,11... | collective-permute-start | bytes 786440 | tf_op jit(solution)/shard_map/ppermute | solution.py:380
  33.2 5.6 %collective-permute-start.6 = (f32[1,2,64,256]{3,2,1,0:T(8,128)S(1)}, f32[1,2,64,256]{3,2,1,0:T(8,128)S(1)}, u32[]{:S(2)}, u32[]{:S(2)}) collective-permute-start(f32[1,2,64,256]{3,2,1,0:T(8,128)S(1)} %constant_dynamic-slice_fusion), channel_id=1, source_target_pairs={{0,2},{1,3},{2,0},{3,1},{4,6},{5,7},{6,4},{7,5},{8,10},{9,11},{10,... | collective-permute-start | bytes 393224 | tf_op jit(solution)/shard_map/ppermute | solution.py:380
  38.8 7.4 %collective-permute-start.7 = (f32[2,64,256]{2,1,0:T(8,128)S(1)}, f32[2,64,256]{2,1,0:T(8,128)S(1)}, u32[]{:S(2)}, u32[]{:S(2)}) collective-permute-start(f32[2,64,256]{2,1,0:T(8,128)S(1)} %add_bitcast_fusion.rest_0_), channel_id=1, source_target_pairs={{0,24},{4,28},{8,16},{12,20},{16,8},{20,12},{24,0},{28,4},{1,25},{... | collective-permute-start | bytes 393224 | tf_op jit(solution)/shard_map/ppermute | solution.py:380
  42.4 5.3 %collective-permute-start.8 = (f32[2,64,256]{2,1,0:T(8,128)S(1)}, f32[2,64,256]{2,1,0:T(8,128)S(1)}, u32[]{:S(2)}, u32[]{:S(2)}) collective-permute-start(f32[2,64,256]{2,1,0:T(8,128)S(1)} %add_bitcast_fusion.rest_0_), channel_id=1, source_target_pairs={{0,4},{1,9},{2,6},{3,11},{4,0},{5,13},{6,2},{7,15},{8,12},{9,1},{1... | collective-permute-start | bytes 393224 | tf_op jit(solution)/shard_map/ppermute | solution.py:137
  46.2 5.0 %collective-permute-start.9 = (f32[2,64,256]{2,1,0:T(8,128)S(1)}, f32[2,64,256]{2,1,0:T(8,128)S(1)}, u32[]{:S(2)}, u32[]{:S(2)}) collective-permute-start(f32[2,64,256]{2,1,0:T(8,128)S(1)} %collective-permute-done.7.rest_1_), channel_id=1, source_target_pairs={{0,4},{1,9},{2,6},{3,11},{4,0},{5,13},{6,2},{7,15},{8,12},{9,1},{1... | collective-permute-start | bytes 393224 | tf_op jit(solution)/shard_map/ppermute | solution.py:137
  51.3 7.4 %collective-permute-start.10 = (f32[4,64,256]{2,1,0:T(8,128)S(1)}, f32[4,64,256]{2,1,0:T(8,128)S(1)}, u32[]{:S(2)}, u32[]{:S(2)}) collective-permute-start(f32[4,64,256]{2,1,0:T(8,128)S(1)} %shard_map.119), channel_id=1, source_target_pairs={{0,8},{1,5},{2,10},{3,7},{4,12},{5,1},{6,14},{7,3},{8,0},{9,13},{1... | collective-permute-start | bytes 786440 | tf_op jit(solution)/shard_map/ppermute | solution.py:137

commit v7 on v6

--- a/solution.py
+++ b/solution.py
@@ -319,7 +319,7 @@
 
 
 def terms_kernel(
-    blocks, ways, factors, own_terms, arrived, update, source, mats, held, sent, term
+    blocks, ways, factors, own_terms, arrived, update, source, mats, held, sent
 ):
     head = lax.axis_index("head")
     side = 1 - lax.rem(lax.axis_index("seq"), 2)
@@ -327,10 +327,12 @@
     core = lax.rem(head, 2)
     terms = half_terms(blocks, side, factors, arrived, update, source, mats)
     for c in range(blocks):
-        term[...] = own_terms[c] + terms[c]
+        term = own_terms[c] + terms[c]
         for i in range(ways // 2):
-            held[i, c] = term[pl.ds(pl.multiple_of((2 * i + core) * part, part), part), :]
-            sent[i, c] = term[pl.ds(pl.multiple_of((2 * i + 1 - core) * part, part), part), :]
+            even = term[2 * i * part : (2 * i + 1) * part]
+            odd = term[(2 * i + 1) * part : (2 * i + 2) * part]
+            held[i, c] = jnp.where(core == 0, even, odd)
+            sent[i, c] = jnp.where(core == 0, odd, even)
 
 
 def rounded_kernel(blocks, factors, own, arrived, update, source, mats, entries, leaves):
@@ -516,7 +518,7 @@
         functools.partial(terms_kernel, blocks, ways),
         (factors, own_terms, arrived_entry, update, source, mats),
         (part_shape, part_shape),
-        [pltpu.VMEM((STATE, STATE), F32)],
+        [],
     )
 
     def output_call(c, entries, leaves, before):

time: 59.6 us -> 59.5 us (level)
  no operation moved by 1% of the time
where the time goes in v7:
time: 59.5 us; the launch traced here: 59.3 us
  starting transfers between devices  22.2 us (37%)
  waiting for transfers between devices  19 us (32%)
  Pallas kernels  17.2 us (29%)
  between operations  0.76 us (1%)
    ppermute x5, waiting for transfers between devices, swap(): return lax.ppermute(x, axis, [(i, i ^ by) for i in range(count)])  11.3 us
    ppermute x5, starting transfers between devices, swap(): return lax.ppermute(x, axis, [(i, i ^ by) for i in range(count)])  9.71 us
    pallas_call x2, Pallas kernels, output_call(): pl.pallas_call(within_kernel, grid=(heads // 2,), in_specs=[wide, wide, n...  7.38 us
    ppermute x3, starting transfers between devices, level_route(): return lax.ppermute(x, 'seq', pairs)  6.46 us
    ppermute x3, starting transfers between devices, swap_near(): return lax.ppermute(x, ('seq', 'head'), pairs)  6.01 us
    ppermute x3, waiting for transfers between devices, swap_near(): return lax.ppermute(x, ('seq', 'head'), pairs)  3.97 us
    ppermute x3, waiting for transfers between devices, level_route(): return lax.ppermute(x, 'seq', pairs)  3.73 us
    pallas_call x1, Pallas kernels, local(): pl.pallas_call(functools.partial(local_kernel, blocks, heads), in_specs=[...  3.16 us
  transfers between devices with their start and end apart: 11, of which 9 were waited for; matrix products, arithmetic and copies ran while one was open for 0% of the time, Pallas kernels for 20%

profile of v7, /device:TPU:0, one launch (start us, length us, event | category | flops | bytes accessed | tf_op | source)
XLA Modules:
  0.0 59.3 jit_solution(9200818517042933915)
XLA Ops:
  0.7 3.2 %shard_map.112 = (f32[2,256,256]{2,1,0:T(8,128)S(1)}, f32[2,256,256]{2,1,0:T(8,128)S(1)}, f32[2,128,256]{2,1,0:T(8,128)S(1)}, f32[2,128,256]{2,1,0:T(8,128)S(1)}, bf16[2,256,256]{2,1,0:T(8,128)(2,1)S(1)}) custom-call(s32[16]{0:T(128)} %regimes_hbm.1, s32[16]{0:T(128)} %documents_hbm.1, f32[4]{0:T(128)} %gammas_hbm.1, bf16[32,256,256]{2,1,0:T(8,128)(2,1)} %transitions.3, ...), custom_call_target="tpu_custom_call" | custom-call | tf_op jit(solution)/shard_map/pallas_call | solution.py:437
  3.8 3.0 %collective-permute-start = (f32[2,128,256]{2,1,0:T(8,128)S(1)}, f32[2,128,256]{2,1,0:T(8,128)S(1)}, u32[]{:S(2)}, u32[]{:S(2)}) collective-permute-start(f32[2,128,256]{2,1,0:T(8,128)S(1)} %get-tuple-element.59), channel_id=1, source_target_pairs={{0,4},{4,0},{8,12},{12,8},{16,20},{20,16},{24,28},{28,24},{1,5},{5... | collective-permute-start | bytes 786440 | tf_op jit(solution)/shard_map/ppermute | solution.py:382
  6.8 2.9 %shard_map.111 = (bf16[2,2,256,256]{3,2,1,0:T(8,128)(2,1)S(1)}, f32[2,256,1]{2,1,0:T(8,128)S(1)}, f32[2,256,1]{2,1,0:T(8,128)S(1)}, f32[2,4,8,256]{3,2,1,0:T(8,128)S(1)}, bf16[1,2,2,256,256]{4,3,2,1,0:T(8,128)(2,1)S(1)}) custom-call(s32[16]{0:T(128)S(1)} %copy-done, s32[16]{0:T(128)S(1)} %copy-done.1, f32[4]{0:T(128)S(1)} %copy-done.2, ...), custom_call_target="tpu_custom_call" | custom-call | tf_op jit(solution)/shard_map/pallas_call | solution.py:467
  9.8 3.3 %collective-permute-done.arrived = f32[2,128,256]{2,1,0:T(8,128)S(1)} collective-permute-done((f32[2,128,256]{2,1,0:T(8,128)S(1)}, f32[2,128,256]{2,1,0:T(8,128)S(1)}, u32[]{:S(2)}, u32[]{:S(2)}) %collective-permute-start) | collective-permute-done | bytes 262176 | tf_op jit(solution)/shard_map/ppermute | solution.py:382
  13.1 0.4 shard_map.113
  13.5 2.9 %collective-permute-start.1 = (f32[128,256]{1,0:T(8,128)S(1)}, f32[128,256]{1,0:T(8,128)S(1)}, u32[]{:S(2)}, u32[]{:S(2)}) collective-permute-start(f32[128,256]{1,0:T(8,128)S(1)} %get-tuple-element.61), channel_id=1, source_target_pairs={{0,16},{16,0},{4,20},{20,4},{8,24},{24,8},{12,28},{28,12},{1,17},{... | collective-permute-start | bytes 393224 | tf_op jit(solution)/shard_map/ppermute | solution.py:393
  16.4 0.7 %collective-permute-start.2 = (f32[128,256]{1,0:T(8,128)S(1)}, f32[128,256]{1,0:T(8,128)S(1)}, u32[]{:S(2)}, u32[]{:S(2)}) collective-permute-start(f32[128,256]{1,0:T(8,128)S(1)} %get-tuple-element.62), channel_id=1, source_target_pairs={{8,16},{16,8},{12,20},{20,12},{9,17},{17,9},{13,21},{21,13},{10,18... | collective-permute-start | bytes 393224 | tf_op jit(solution)/shard_map/ppermute | solution.py:393
  17.1 2.9 %collective-permute-start.3 = (f32[128,256]{1,0:T(8,128)S(1)}, f32[128,256]{1,0:T(8,128)S(1)}, u32[]{:S(2)}, u32[]{:S(2)}) collective-permute-start(f32[128,256]{1,0:T(8,128)S(1)} %get-tuple-element.63), channel_id=1, source_target_pairs={{0,8},{8,0},{4,12},{12,4},{16,24},{24,16},{20,28},{28,20},{1,9},{9... | collective-permute-start | bytes 393224 | tf_op jit(solution)/shard_map/ppermute | solution.py:393
  20.0 3.1 %collective-permute-done.1.rest_0_ = f32[128,256]{1,0:T(8,128)S(1)} collective-permute-done((f32[128,256]{1,0:T(8,128)S(1)}, f32[128,256]{1,0:T(8,128)S(1)}, u32[]{:S(2)}, u32[]{:S(2)}) %collective-permute-start.1) | collective-permute-done | bytes 131104 | tf_op jit(solution)/shard_map/ppermute | solution.py:393
  23.1 0.6 %collective-permute-done.3.rest_2_ = f32[128,256]{1,0:T(8,128)S(1)} collective-permute-done((f32[128,256]{1,0:T(8,128)S(1)}, f32[128,256]{1,0:T(8,128)S(1)}, u32[]{:S(2)}, u32[]{:S(2)}) %collective-permute-start.3) | collective-permute-done | bytes 131104 | tf_op jit(solution)/shard_map/ppermute | solution.py:393
  23.7 0.6 %shard_map.114 = (f32[2,128,256]{2,1,0:T(8,128)S(1)}, f32[2,128,256]{2,1,0:T(8,128)S(1)}) custom-call(f32[2,256,1]{2,1,0:T(8,128)S(1)} %get-tuple-element.57.powers, f32[2,128,256]{2,1,0:T(8,128)S(1)} %get-tuple-element.58.held, f32[2,128,256]{2,1,0:T(8,128)S(1)} %collective-permute-done.arrived, bf16[2,2,256,256]{3,2,1,0:T(8,128)(2,1)S(1)} %get-tuple-element.60.device_maps, ...), custom_call_target="tpu_custom_call" | custom-call | tf_op jit(solution)/shard_map/pallas_call | solution.py:488
  24.3 1.5 %collective-permute-start.4 = (f32[2,128,256]{2,1,0:T(8,128)S(1)}, f32[2,128,256]{2,1,0:T(8,128)S(1)}, u32[]{:S(2)}, u32[]{:S(2)}) collective-permute-start(f32[2,128,256]{2,1,0:T(8,128)S(1)} %get-tuple-element.69), channel_id=1, source_target_pairs={{0,4},{4,0},{8,12},{12,8},{16,20},{20,16},{24,28},{28,24},{1,5},{5... | collective-permute-start | bytes 786440 | tf_op jit(solution)/shard_map/ppermute | solution.py:382
  25.8 0.6 %shard_map.115.own_terms = f32[2,256,256]{2,1,0:T(8,128)S(1)} custom-call(f32[2,256,1]{2,1,0:T(8,128)S(1)} %get-tuple-element.73.factors, f32[2,128,256]{2,1,0:T(8,128)S(1)} %get-tuple-element.74.own, f32[2,256,256]{2,1,0:T(8,128)S(1)} %get-tuple-element.76.update, f32[2,256,256]{2,1,0:T(8,128)S(1)} %get-tuple-element.77.source, ...), custom_call_target="tpu_custom_call" | custom-call | tf_op jit(solution)/shard_map/pallas_call | solution.py:502
  26.5 4.3 %collective-permute-done.4.arrived = f32[2,128,256]{2,1,0:T(8,128)S(1)} collective-permute-done((f32[2,128,256]{2,1,0:T(8,128)S(1)}, f32[2,128,256]{2,1,0:T(8,128)S(1)}, u32[]{:S(2)}, u32[]{:S(2)}) %collective-permute-start.4) | collective-permute-done | bytes 262176 | tf_op jit(solution)/shard_map/ppermute | solution.py:382
  30.8 0.6 %shard_map.116 = (f32[2,2,64,256]{3,2,1,0:T(8,128)S(1)}, f32[2,2,64,256]{3,2,1,0:T(8,128)S(1)}) custom-call(f32[2,256,1]{2,1,0:T(8,128)S(1)} %get-tuple-element.73.factors, f32[2,256,256]{2,1,0:T(8,128)S(1)} %shard_map.115.own_terms, f32[2,128,256]{2,1,0:T(8,128)S(1)} %collective-permute-done.4.arrived, f32[2,256,256]{2,1,0:T(8,128)S(1)} %get-tuple-element.76.update, ...), custom_call_target="tpu_custom_call" | custom-call | tf_op jit(solution)/shard_map/pallas_call | solution.py:502
  31.4 0.1 collective-permute-start.5
  31.5 0.5 shard_map.117
  32.0 1.0 %collective-permute-done.5 = f32[2,2,64,256]{3,2,1,0:T(8,128)S(1)} collective-permute-done((f32[2,2,64,256]{3,2,1,0:T(8,128)S(1)}, f32[2,2,64,256]{3,2,1,0:T(8,128)S(1)}, u32[]{:S(2)}, u32[]{:S(2)}) %collective-permute-start.5) | collective-permute-done | bytes 262176 | tf_op jit(solution)/shard_map/ppermute | solution.py:382
  33.1 1.5 %collective-permute-start.6 = (f32[1,2,64,256]{3,2,1,0:T(8,128)S(1)}, f32[1,2,64,256]{3,2,1,0:T(8,128)S(1)}, u32[]{:S(2)}, u32[]{:S(2)}) collective-permute-start(f32[1,2,64,256]{3,2,1,0:T(8,128)S(1)} %constant_dynamic-slice_fusion), channel_id=1, source_target_pairs={{0,2},{1,3},{2,0},{3,1},{4,6},{5,7},{6,4},{7,5},{8,10},{9,11},{10,... | collective-permute-start | bytes 393224 | tf_op jit(solution)/shard_map/ppermute | solution.py:382
  34.6 3.7 %shard_map.118 = (bf16[512,1024]{1,0:T(8,128)(2,1)}, bf16[512,1024]{1,0:T(8,128)(2,1)}, bf16[512,256]{1,0:T(8,128)(2,1)}) custom-call(bf16[512,1024]{1,0:T(8,128)(2,1)} %q.3, bf16[512,1024]{1,0:T(8,128)(2,1)} %k.3, bf16[512,256]{1,0:T(8,128)(2,1)} %v.3, bf16[512,256]{1,0:T(8,128)(2,1)} %dy.3, bf16[2,256,256]{2,1,0:T(8,128)(2,1)S(1)} %get-tuple-element.85.entries, ...), custom_call_target="tpu_custom_call" | custom-call | flops 1342177280 | bytes 3145728 | tf_op jit(solution)/shard_map/pallas_call | solution.py:528
  38.3 0.4 collective-permute-done.6
  38.7 3.6 %collective-permute-start.7 = (f32[2,64,256]{2,1,0:T(8,128)S(1)}, f32[2,64,256]{2,1,0:T(8,128)S(1)}, u32[]{:S(2)}, u32[]{:S(2)}) collective-permute-start(f32[2,64,256]{2,1,0:T(8,128)S(1)} %add_bitcast_fusion.rest_0_), channel_id=1, source_target_pairs={{0,24},{4,28},{8,16},{12,20},{16,8},{20,12},{24,0},{28,4},{1,25},{... | collective-permute-start | bytes 393224 | tf_op jit(solution)/shard_map/ppermute | solution.py:382
  42.3 1.5 %collective-permute-start.8 = (f32[2,64,256]{2,1,0:T(8,128)S(1)}, f32[2,64,256]{2,1,0:T(8,128)S(1)}, u32[]{:S(2)}, u32[]{:S(2)}) collective-permute-start(f32[2,64,256]{2,1,0:T(8,128)S(1)} %add_bitcast_fusion.rest_0_), channel_id=1, source_target_pairs={{0,4},{1,9},{2,6},{3,11},{4,0},{5,13},{6,2},{7,15},{8,12},{9,1},{1... | collective-permute-start | bytes 393224 | tf_op jit(solution)/shard_map/ppermute | solution.py:137
  43.8 2.3 %collective-permute-done.7.rest_1_ = f32[2,64,256]{2,1,0:T(8,128)S(1)} collective-permute-done((f32[2,64,256]{2,1,0:T(8,128)S(1)}, f32[2,64,256]{2,1,0:T(8,128)S(1)}, u32[]{:S(2)}, u32[]{:S(2)}) %collective-permute-start.7) | collective-permute-done | bytes 131104 | tf_op jit(solution)/shard_map/ppermute | solution.py:382
  46.1 1.5 %collective-permute-start.9 = (f32[2,64,256]{2,1,0:T(8,128)S(1)}, f32[2,64,256]{2,1,0:T(8,128)S(1)}, u32[]{:S(2)}, u32[]{:S(2)}) collective-permute-start(f32[2,64,256]{2,1,0:T(8,128)S(1)} %collective-permute-done.7.rest_1_), channel_id=1, source_target_pairs={{0,4},{1,9},{2,6},{3,11},{4,0},{5,13},{6,2},{7,15},{8,12},{9,1},{1... | collective-permute-start | bytes 393224 | tf_op jit(solution)/shard_map/ppermute | solution.py:137
  47.6 3.5 %collective-permute-done.9.rest_3_ = f32[2,64,256]{2,1,0:T(8,128)S(1)} collective-permute-done((f32[2,64,256]{2,1,0:T(8,128)S(1)}, f32[2,64,256]{2,1,0:T(8,128)S(1)}, u32[]{:S(2)}, u32[]{:S(2)}) %collective-permute-start.9) | collective-permute-done | bytes 131104 | tf_op jit(solution)/shard_map/ppermute | solution.py:137
  51.0 0.1 shard_map.119
  51.2 3.0 %collective-permute-start.10 = (f32[4,64,256]{2,1,0:T(8,128)S(1)}, f32[4,64,256]{2,1,0:T(8,128)S(1)}, u32[]{:S(2)}, u32[]{:S(2)}) collective-permute-start(f32[4,64,256]{2,1,0:T(8,128)S(1)} %shard_map.119), channel_id=1, source_target_pairs={{0,8},{1,5},{2,10},{3,7},{4,12},{5,1},{6,14},{7,3},{8,0},{9,13},{1... | collective-permute-start | bytes 786440 | tf_op jit(solution)/shard_map/ppermute | solution.py:137
  54.2 0.1 shard_map.120.a
  54.3 3.7 %shard_map.121 = (bf16[512,1024]{1,0:T(8,128)(2,1)}, bf16[512,1024]{1,0:T(8,128)(2,1)}, bf16[512,256]{1,0:T(8,128)(2,1)}) custom-call(bf16[512,1024]{1,0:T(8,128)(2,1)} %q.3, bf16[512,1024]{1,0:T(8,128)(2,1)} %k.3, bf16[512,256]{1,0:T(8,128)(2,1)} %v.3, bf16[512,256]{1,0:T(8,128)(2,1)} %dy.3, ...), custom_call_target="tpu_custom_call", output_to_operand_aliasing={{0}: (6, {}), {1}: (7, {}), {2}: (8, {})} | custom-call | flops 1342177280 | bytes 3145728 | tf_op jit(solution)/shard_map/pallas_call | solution.py:528
  58.0 0.5 collective-permute-done.10.b
  58.5 0.7 %shard_map.122 = f32[4,64,256]{2,1,0:T(8,128)} custom-call(f32[4,64,256]{2,1,0:T(8,128)S(1)} %shard_map.120.a, f32[4,64,256]{2,1,0:T(8,128)S(1)} %collective-permute-done.10.b), custom_call_target="tpu_custom_call" | custom-call | tf_op jit(solution)/shard_map/pallas_call | solution.py:587
  (11 shorter events, 0.1 us)
Async XLA Ops:
  0.6 6.2 %copy-start.1 = (s32[16]{0:T(128)S(1)}, s32[16]{0:T(128)}, u32[]{:S(2)}) copy-start(s32[16]{0:T(128)} %documents_hbm.1) | copy-start | bytes 196
  0.6 6.2 %copy-start = (s32[16]{0:T(128)S(1)}, s32[16]{0:T(128)}, u32[]{:S(2)}) copy-start(s32[16]{0:T(128)} %regimes_hbm.1) | copy-start | bytes 196
  0.7 6.2 %copy-start.2 = (f32[4]{0:T(128)S(1)}, f32[4]{0:T(128)}, u32[]{:S(2)}) copy-start(f32[4]{0:T(128)} %gammas_hbm.1) | copy-start | bytes 52
  3.8 9.3 %collective-permute-start = (f32[2,128,256]{2,1,0:T(8,128)S(1)}, f32[2,128,256]{2,1,0:T(8,128)S(1)}, u32[]{:S(2)}, u32[]{:S(2)}) collective-permute-start(f32[2,128,256]{2,1,0:T(8,128)S(1)} %get-tuple-element.59), channel_id=1, source_target_pairs={{0,4},{4,0},{8,12},{12,8},{16,20},{20,16},{24,28},{28,24},{1,5},{5... | collective-permute-start | bytes 786440 | tf_op jit(solution)/shard_map/ppermute | solution.py:382
  13.5 9.6 %collective-permute-start.1 = (f32[128,256]{1,0:T(8,128)S(1)}, f32[128,256]{1,0:T(8,128)S(1)}, u32[]{:S(2)}, u32[]{:S(2)}) collective-permute-start(f32[128,256]{1,0:T(8,128)S(1)} %get-tuple-element.61), channel_id=1, source_target_pairs={{0,16},{16,0},{4,20},{20,4},{8,24},{24,8},{12,28},{28,12},{1,17},{... | collective-permute-start | bytes 393224 | tf_op jit(solution)/shard_map/ppermute | solution.py:393
  16.4 6.7 %collective-permute-start.2 = (f32[128,256]{1,0:T(8,128)S(1)}, f32[128,256]{1,0:T(8,128)S(1)}, u32[]{:S(2)}, u32[]{:S(2)}) collective-permute-start(f32[128,256]{1,0:T(8,128)S(1)} %get-tuple-element.62), channel_id=1, source_target_pairs={{8,16},{16,8},{12,20},{20,12},{9,17},{17,9},{13,21},{21,13},{10,18... | collective-permute-start | bytes 393224 | tf_op jit(solution)/shard_map/ppermute | solution.py:393
  17.1 6.6 %collective-permute-start.3 = (f32[128,256]{1,0:T(8,128)S(1)}, f32[128,256]{1,0:T(8,128)S(1)}, u32[]{:S(2)}, u32[]{:S(2)}) collective-permute-start(f32[128,256]{1,0:T(8,128)S(1)} %get-tuple-element.63), channel_id=1, source_target_pairs={{0,8},{8,0},{4,12},{12,4},{16,24},{24,16},{20,28},{28,20},{1,9},{9... | collective-permute-start | bytes 393224 | tf_op jit(solution)/shard_map/ppermute | solution.py:393
  24.3 6.4 %collective-permute-start.4 = (f32[2,128,256]{2,1,0:T(8,128)S(1)}, f32[2,128,256]{2,1,0:T(8,128)S(1)}, u32[]{:S(2)}, u32[]{:S(2)}) collective-permute-start(f32[2,128,256]{2,1,0:T(8,128)S(1)} %get-tuple-element.69), channel_id=1, source_target_pairs={{0,4},{4,0},{8,12},{12,8},{16,20},{20,16},{24,28},{28,24},{1,5},{5... | collective-permute-start | bytes 786440 | tf_op jit(solution)/shard_map/ppermute | solution.py:382
  31.4 1.6 %collective-permute-start.5 = (f32[2,2,64,256]{3,2,1,0:T(8,128)S(1)}, f32[2,2,64,256]{3,2,1,0:T(8,128)S(1)}, u32[]{:S(2)}, u32[]{:S(2)}) collective-permute-start(f32[2,2,64,256]{3,2,1,0:T(8,128)S(1)} %get-tuple-element.72), channel_id=1, source_target_pairs={{0,1},{1,0},{2,3},{3,2},{4,5},{5,4},{6,7},{7,6},{8,9},{9,8},{10,11... | collective-permute-start | bytes 786440 | tf_op jit(solution)/shard_map/ppermute | solution.py:382
  33.1 5.6 %collective-permute-start.6 = (f32[1,2,64,256]{3,2,1,0:T(8,128)S(1)}, f32[1,2,64,256]{3,2,1,0:T(8,128)S(1)}, u32[]{:S(2)}, u32[]{:S(2)}) collective-permute-start(f32[1,2,64,256]{3,2,1,0:T(8,128)S(1)} %constant_dynamic-slice_fusion), channel_id=1, source_target_pairs={{0,2},{1,3},{2,0},{3,1},{4,6},{5,7},{6,4},{7,5},{8,10},{9,11},{10,... | collective-permute-start | bytes 393224 | tf_op jit(solution)/shard_map/ppermute | solution.py:382
  38.7 7.3 %collective-permute-start.7 = (f32[2,64,256]{2,1,0:T(8,128)S(1)}, f32[2,64,256]{2,1,0:T(8,128)S(1)}, u32[]{:S(2)}, u32[]{:S(2)}) collective-permute-start(f32[2,64,256]{2,1,0:T(8,128)S(1)} %add_bitcast_fusion.rest_0_), channel_id=1, source_target_pairs={{0,24},{4,28},{8,16},{12,20},{16,8},{20,12},{24,0},{28,4},{1,25},{... | collective-permute-start | bytes 393224 | tf_op jit(solution)/shard_map/ppermute | solution.py:382
  42.3 5.3 %collective-permute-start.8 = (f32[2,64,256]{2,1,0:T(8,128)S(1)}, f32[2,64,256]{2,1,0:T(8,128)S(1)}, u32[]{:S(2)}, u32[]{:S(2)}) collective-permute-start(f32[2,64,256]{2,1,0:T(8,128)S(1)} %add_bitcast_fusion.rest_0_), channel_id=1, source_target_pairs={{0,4},{1,9},{2,6},{3,11},{4,0},{5,13},{6,2},{7,15},{8,12},{9,1},{1... | collective-permute-start | bytes 393224 | tf_op jit(solution)/shard_map/ppermute | solution.py:137
  46.1 5.0 %collective-permute-start.9 = (f32[2,64,256]{2,1,0:T(8,128)S(1)}, f32[2,64,256]{2,1,0:T(8,128)S(1)}, u32[]{:S(2)}, u32[]{:S(2)}) collective-permute-start(f32[2,64,256]{2,1,0:T(8,128)S(1)} %collective-permute-done.7.rest_1_), channel_id=1, source_target_pairs={{0,4},{1,9},{2,6},{3,11},{4,0},{5,13},{6,2},{7,15},{8,12},{9,1},{1... | collective-permute-start | bytes 393224 | tf_op jit(solution)/shard_map/ppermute | solution.py:137
  51.2 7.4 %collective-permute-start.10 = (f32[4,64,256]{2,1,0:T(8,128)S(1)}, f32[4,64,256]{2,1,0:T(8,128)S(1)}, u32[]{:S(2)}, u32[]{:S(2)}) collective-permute-start(f32[4,64,256]{2,1,0:T(8,128)S(1)} %shard_map.119), channel_id=1, source_target_pairs={{0,8},{1,5},{2,10},{3,7},{4,12},{5,1},{6,14},{7,3},{8,0},{9,13},{1... | collective-permute-start | bytes 786440 | tf_op jit(solution)/shard_map/ppermute | solution.py:137
